TPU v7x, 32 devices: a whole 2x2x4 slice. The times are simulated.
32 devices in a mesh: seq: 4 (over y, x), ctx: 4 (over z), fsdp: 2 (over core).
Axes of the slice: x: 2, y: 2, z: 4, core: 2. Of those that a mesh axis runs over, the one named last changes fastest.
Arguments:
- tokens: bfloat16 [8, 2048, 1024], P(('seq', 'fsdp'), 'ctx'), may hold values from -6 to 6
- cotangent: bfloat16 [8, 2048, 1024], P(('seq', 'fsdp'), 'ctx'), may hold values from -6 to 6
- global_pos: int32 [8, 64], P(('seq', 'fsdp')), may hold values from 0 to 2047, as said below
- attn_gain: bfloat16 [1024], P('fsdp'), may hold values from 0.5 to 1.5
- attn_shift: bfloat16 [1024], P('fsdp'), may hold values from -1 to 1
- mlp_gain: bfloat16 [1024], P('fsdp'), may hold values from 0.5 to 1.5
- mlp_shift: bfloat16 [1024], P('fsdp'), may hold values from -1 to 1
- qkv_weight: bfloat16 [1024, 3072], P('fsdp'), may hold values from -0.1875 to 0.1875
- qkv_bias: bfloat16 [3072], P('fsdp'), may hold values from -1 to 1
- proj_weight: bfloat16 [1024, 1024], P('fsdp'), may hold values from -0.5 to 0.5
- proj_bias: bfloat16 [1024], P('fsdp'), may hold values from -1 to 1
- up_weight: bfloat16 [1024, 4096], P('fsdp'), may hold values from -0.1875 to 0.1875
- up_bias: bfloat16 [4096], P('fsdp'), may hold values from -1 to 1
- down_weight: bfloat16 [4096, 1024], P('fsdp'), may hold values from -0.09375 to 0.09375
- down_bias: bfloat16 [1024], P('fsdp'), may hold values from -1 to 1
Outputs:
- layer_out: bfloat16 [8, 2048, 1024], P(('seq', 'fsdp'), 'ctx')
- tokens_grad: float32 [8, 2048, 1024], P(('seq', 'fsdp'), 'ctx')
- attn_gain_grad: float32 [1024], P('fsdp')
- attn_shift_grad: float32 [1024], P('fsdp')
- mlp_gain_grad: float32 [1024], P('fsdp')
- mlp_shift_grad: float32 [1024], P('fsdp')
- qkv_weight_grad: float32 [1024, 3072], P('fsdp')
- qkv_bias_grad: float32 [3072], P('fsdp')
- proj_weight_grad: float32 [1024, 1024], P('fsdp')
- proj_bias_grad: float32 [1024], P('fsdp')
- up_weight_grad: float32 [1024, 4096], P('fsdp')
- up_bias_grad: float32 [4096], P('fsdp')
- down_weight_grad: float32 [4096, 1024], P('fsdp')
- down_bias_grad: float32 [1024], P('fsdp')
Inputs may be any that keep to these rules, and one draw needn't show every extreme that they name: `global_pos`: each row rises strictly; its g-th entry lies in [g * 32, (g + 1) * 32); in some row the first entry is 0 and the last is 2047.
All inputs are finite; a program needn't handle non-finite values.
Results may differ from a plain program's by a relative error of at most 0.011.
Values may be sent and summed in bfloat16 or wider, within the bound.
No kernel may reach another device: no remote copies, remote signals or barrier semaphores. Data moves between devices by JAX's collectives and lax.ppermute only.
A program may use at most 320 MiB of HBM per device.

v0:
```python
import math

import jax
import jax.numpy as jnp
from jax import lax
from jax.sharding import PartitionSpec as P

D = 1024
H = 16
HD = 64
ROT = 16
WIN = 512


epsilon = 1e-05
negative = -1e30
rotary_base = 10000.0


def shifted(block, axis, distance):
    devices = range(lax.axis_size(axis))
    route = [(i - distance, i) for i in devices if i - distance in devices]
    return lax.ppermute(block, axis, route)


def merged(part, axis, combine):
    gathered = jax.tree.map(lambda a: lax.all_gather(a, axis), part)

    def take(source):
        return jax.tree.map(lambda a: lax.dynamic_index_in_dim(a, source, 0, False), gathered)

    return lax.fori_loop(
        1, lax.axis_size(axis), lambda source, state: combine(state, take(source)), take(0)
    )


def layer_norm_forward(values, gain, shift):
    center = values - jnp.mean(values, axis=-1, keepdims=True)
    invstd = lax.rsqrt(jnp.mean(center * center, axis=-1, keepdims=True) + epsilon)
    normal = center * invstd
    return (normal * gain + shift, normal, invstd)


def layer_norm_backward(upper, normal, invstd, gain):
    scaled = upper * gain
    lower = invstd * (
        scaled
        - jnp.mean(scaled, axis=-1, keepdims=True)
        - normal * jnp.mean(scaled * normal, axis=-1, keepdims=True)
    )
    return (lower, jnp.sum(upper * normal, axis=0), jnp.sum(upper, axis=0))


def rotary_tables(positions, rotary):
    half = rotary // 2
    freqs = rotary_base ** (-2.0 * jnp.arange(half, dtype=jnp.float32) / rotary)
    angles = positions.astype(jnp.float32)[:, None] * freqs[None, :]
    return (jnp.cos(angles), jnp.sin(angles))


def rotate(field, cosine, sine, direction):
    half = cosine.shape[1]
    first = field[..., :half]
    second = field[..., half : 2 * half]
    remain = field[..., 2 * half :]
    cos_wide = cosine[:, None, :]
    sin_wide = sine[:, None, :] * direction
    return jnp.concatenate(
        [first * cos_wide - second * sin_wide, second * cos_wide + first * sin_wide, remain],
        axis=-1,
    )


def gelu_slope(value):
    normal_cdf = 0.5 * (1.0 + jax.scipy.special.erf(value * 0.5**0.5))
    density = jnp.exp(-0.5 * value * value) / math.sqrt(2.0 * math.pi)
    return normal_cdf + value * density


def combine_stats(first, second):
    top = jnp.maximum(first[0], second[0])
    return (top, first[1] * jnp.exp(first[0] - top) + second[1] * jnp.exp(second[0] - top))


def outer_sum(left, right):
    return lax.dot_general(
        left, right, (((0,), (0,)), ((), ())), preferred_element_type=jnp.float32
    )


def back_dot(left, right):
    return lax.dot_general(
        left, right, (((1,), (1,)), ((), ())), preferred_element_type=jnp.float32
    )


def near_scores(query, key_all, query_pos, key_pos, glob_keys, glob_at, scale):
    near = jnp.einsum("qhd,khd->hqk", query, key_all, preferred_element_type=jnp.float32) * scale
    far = jnp.einsum("qhd,khd->hqk", query, glob_keys, preferred_element_type=jnp.float32) * scale
    offset = query_pos[:, None] - key_pos[None, :]
    near_mask = (offset >= 0) & (offset < WIN) & (key_pos[None, :] >= 0)
    far_mask = query_pos[:, None] - glob_at[None, :] >= WIN
    scores = jnp.concatenate([near, far], axis=-1)
    mask = jnp.concatenate([near_mask, far_mask], axis=-1)[None]
    return (jnp.where(mask, scores, negative), mask)


def per_device(
    tokens,
    cotangent,
    global_pos,
    attn_gain,
    attn_shift,
    mlp_gain,
    mlp_shift,
    qkv_weight,
    qkv_bias,
    proj_weight,
    proj_bias,
    up_weight,
    up_bias,
    down_weight,
    down_bias,
):
    single_float = jnp.float32
    bf16 = jnp.bfloat16
    scale = HD ** (-0.5)
    highest = lax.Precision.HIGHEST
    layer_state = tokens[0].astype(single_float)
    grad_out = cotangent[0]
    rows = layer_state.shape[0]
    ctx_size = lax.axis_size("ctx")
    ctx_rank = lax.axis_index("ctx")
    glob_all = global_pos[0]
    glob_count = glob_all.shape[0]
    per_block = glob_count // ctx_size
    gathered = (
        lax.all_gather(attn_gain, "fsdp", axis=0, tiled=True),
        lax.all_gather(attn_shift, "fsdp", axis=0, tiled=True),
        lax.all_gather(mlp_gain, "fsdp", axis=0, tiled=True),
        lax.all_gather(mlp_shift, "fsdp", axis=0, tiled=True),
        lax.all_gather(qkv_weight, "fsdp", axis=0, tiled=True),
        lax.all_gather(qkv_bias, "fsdp", axis=0, tiled=True),
        lax.all_gather(proj_weight, "fsdp", axis=0, tiled=True),
        lax.all_gather(proj_bias, "fsdp", axis=0, tiled=True),
        lax.all_gather(up_weight, "fsdp", axis=0, tiled=True),
        lax.all_gather(up_bias, "fsdp", axis=0, tiled=True),
        lax.all_gather(down_weight, "fsdp", axis=0, tiled=True),
        lax.all_gather(down_bias, "fsdp", axis=0, tiled=True),
    )
    (
        attention_norm_gain,
        attention_norm_shift,
        perceptron_norm_gain,
        perceptron_norm_shift,
        w_qkv,
        b_qkv,
        w_proj,
        b_proj,
        w_up,
        b_up,
        w_down,
        b_down,
    ) = gathered
    attention_norm_gain = attention_norm_gain.astype(single_float)
    perceptron_norm_gain = perceptron_norm_gain.astype(single_float)
    base = ctx_rank * rows
    positions = base + jnp.arange(rows, dtype=jnp.int32)
    attention_normed_input, attention_centered_input, attention_inverse_deviation = (
        layer_norm_forward(
            layer_state, attention_norm_gain, attention_norm_shift.astype(single_float)
        )
    )
    perceptron_normed_input, perceptron_centered_input, perceptron_inverse_deviation = (
        layer_norm_forward(
            layer_state, perceptron_norm_gain, perceptron_norm_shift.astype(single_float)
        )
    )
    in_attn = attention_normed_input.astype(bf16)
    in_mlp = perceptron_normed_input.astype(bf16)
    linear = jnp.dot(in_attn, w_qkv, preferred_element_type=single_float) + b_qkv.astype(
        single_float
    )
    parts = linear.reshape(rows, 3, H, HD)
    cosine, sine = rotary_tables(positions, ROT)
    query = rotate(parts[:, 0], cosine, sine, 1.0).astype(bf16)
    keys = rotate(parts[:, 1], cosine, sine, 1.0).astype(bf16)
    values = parts[:, 2].astype(bf16)
    prev_keys, prev_values = shifted((keys, values), "ctx", 1)
    own_start = ctx_rank * per_block
    own_glob = lax.dynamic_slice_in_dim(glob_all, own_start, per_block, 0)
    own_index = own_glob - base
    glob_query, glob_keys, glob_values = (
        lax.all_gather(jnp.take(query, own_index, axis=0), "ctx", axis=0, tiled=True),
        lax.all_gather(jnp.take(keys, own_index, axis=0), "ctx", axis=0, tiled=True),
        lax.all_gather(jnp.take(values, own_index, axis=0), "ctx", axis=0, tiled=True),
    )
    key_all = jnp.concatenate([prev_keys, keys, glob_keys], axis=0)
    value_all = jnp.concatenate([prev_values, values, glob_values], axis=0)
    key_pos = base - rows + jnp.arange(2 * rows, dtype=jnp.int32)
    masked, mask = near_scores(
        query,
        jnp.concatenate([prev_keys, keys], axis=0),
        positions,
        key_pos,
        glob_keys,
        glob_all,
        scale,
    )
    top = jnp.max(masked, axis=-1, keepdims=True)
    total = jnp.sum(jnp.where(mask, jnp.exp(masked - top), 0.0), axis=-1, keepdims=True)
    log_total = top + jnp.log(total)
    prob = jnp.where(mask, jnp.exp(masked - log_total), 0.0)
    near_out = jnp.einsum(
        "hqk,khd->qhd", prob.astype(bf16), value_all, preferred_element_type=single_float
    )
    glob_mask = (positions[None, :] <= glob_all[:, None])[None]
    glob_scores = (
        jnp.einsum("ghd,khd->hgk", glob_query, keys, preferred_element_type=single_float) * scale
    )
    glob_masked = jnp.where(glob_mask, glob_scores, negative)
    part_top = jnp.max(glob_masked, axis=-1)
    part_total = jnp.sum(
        jnp.where(glob_mask, jnp.exp(glob_masked - part_top[..., None]), 0.0), axis=-1
    )
    glob_top, glob_total = merged((part_top, part_total), "ctx", combine_stats)
    glob_lse = glob_top + jnp.log(glob_total)
    glob_prob = jnp.where(glob_mask, jnp.exp(glob_masked - glob_lse[..., None]), 0.0)
    acc_low = jnp.einsum(
        "hgk,khd->ghd", glob_prob.astype(bf16), values, preferred_element_type=single_float
    )
    acc_exact = jnp.einsum(
        "hgk,khd->ghd", glob_prob, values.astype(single_float), precision=highest
    )
    glob_low, glob_exact = (
        lax.psum(acc_low.reshape(glob_count, D).astype(jnp.bfloat16), "ctx").astype(jnp.float32),
        lax.psum(acc_exact.reshape(glob_count, D).astype(jnp.bfloat16), "ctx").astype(jnp.float32),
    )
    row_ids = jnp.arange(rows, dtype=jnp.int32)
    is_glob = jnp.any(row_ids[:, None] == own_index[None, :], axis=1)
    own_rows = lax.dynamic_slice_in_dim(glob_low, own_start, per_block, 0)
    mixed = near_out.reshape(rows, D).at[own_index].set(own_rows)
    mixed_low = mixed.astype(bf16)
    upper = jnp.dot(in_mlp, w_up, preferred_element_type=single_float) + b_up.astype(single_float)
    active = jax.nn.gelu(upper, approximate=False).astype(bf16)
    result = (
        layer_state
        + jnp.dot(mixed_low, w_proj, preferred_element_type=single_float)
        + b_proj.astype(single_float)
    )
    result = (
        result
        + jnp.dot(active, w_down, preferred_element_type=single_float)
        + b_down.astype(single_float)
    )
    layer_out = result.astype(bf16)[None]
    grad_f32 = grad_out.astype(single_float)
    proj_w_term = outer_sum(mixed_low, grad_out)
    bias_term = jnp.sum(grad_f32, axis=0)
    down_w_term = outer_sum(active, grad_out)
    d_upper = (back_dot(grad_out, w_down) * gelu_slope(upper)).astype(bf16)
    up_w_term = outer_sum(in_mlp, d_upper)
    up_b_term = jnp.sum(d_upper.astype(single_float), axis=0)
    perceptron_input_grad = back_dot(d_upper, w_up)
    grad_attn = back_dot(grad_out, w_proj).astype(bf16).reshape(rows, H, HD)
    grad_local = jnp.where(is_glob[:, None, None], jnp.zeros_like(grad_attn), grad_attn)
    d_prob = jnp.einsum("qhd,khd->hqk", grad_local, value_all, preferred_element_type=single_float)
    delta = jnp.sum(prob * d_prob, axis=-1, keepdims=True)
    d_score = (prob * (d_prob - delta)).astype(bf16)
    d_query = (
        jnp.einsum("hqk,khd->qhd", d_score, key_all, preferred_element_type=single_float) * scale
    )
    d_keys = jnp.einsum("hqk,qhd->khd", d_score, query, preferred_element_type=single_float) * scale
    d_values = jnp.einsum(
        "hqk,qhd->khd", prob.astype(bf16), grad_local, preferred_element_type=single_float
    )
    own_grad = jnp.take(grad_attn, own_index, axis=0)
    glob_grad = lax.all_gather(own_grad, "ctx", axis=0, tiled=True)
    glob_delta = jnp.sum(
        glob_grad.astype(single_float) * glob_exact.reshape(glob_count, H, HD), axis=-1
    )
    glob_dprob = jnp.einsum("ghd,khd->hgk", glob_grad, values, preferred_element_type=single_float)
    glob_dscore = (glob_prob * (glob_dprob - jnp.transpose(glob_delta)[..., None])).astype(bf16)
    glob_dquery = (
        jnp.einsum("hgk,khd->ghd", glob_dscore, keys, preferred_element_type=single_float) * scale
    )
    keys_from_glob = (
        jnp.einsum("hgk,ghd->khd", glob_dscore, glob_query, preferred_element_type=single_float)
        * scale
    )
    values_from_glob = jnp.einsum(
        "hgk,ghd->khd", glob_prob.astype(bf16), glob_grad, preferred_element_type=single_float
    )
    back_query, back_keys, back_values = (
        lax.psum_scatter(
            glob_dquery.reshape(glob_count, D).astype(jnp.bfloat16),
            "ctx",
            scatter_dimension=0,
            tiled=True,
        ).astype(jnp.float32),
        lax.psum_scatter(
            d_keys[2 * rows :].reshape(glob_count, D).astype(jnp.bfloat16),
            "ctx",
            scatter_dimension=0,
            tiled=True,
        ).astype(jnp.float32),
        lax.psum_scatter(
            d_values[2 * rows :].reshape(glob_count, D).astype(jnp.bfloat16),
            "ctx",
            scatter_dimension=0,
            tiled=True,
        ).astype(jnp.float32),
    )
    next_keys, next_values = (
        shifted(d_keys[:rows].astype(jnp.bfloat16), "ctx", -1).astype(jnp.float32),
        shifted(d_values[:rows].astype(jnp.bfloat16), "ctx", -1).astype(jnp.float32),
    )
    empty = jnp.zeros((rows, H, HD), single_float)
    total_query = d_query + empty.at[own_index].add(back_query.reshape(per_block, H, HD))
    total_keys = (
        d_keys[rows : 2 * rows]
        + next_keys
        + keys_from_glob
        + empty.at[own_index].add(back_keys.reshape(per_block, H, HD))
    )
    total_values = (
        d_values[rows : 2 * rows]
        + next_values
        + values_from_glob
        + empty.at[own_index].add(back_values.reshape(per_block, H, HD))
    )
    total_query = rotate(total_query, cosine, sine, -1.0)
    total_keys = rotate(total_keys, cosine, sine, -1.0)
    d_linear = (
        jnp.stack([total_query, total_keys, total_values], axis=1).reshape(rows, 3 * D).astype(bf16)
    )
    qkv_w_term = outer_sum(in_attn, d_linear)
    qkv_b_term = jnp.sum(d_linear.astype(single_float), axis=0)
    attention_input_grad = back_dot(d_linear, w_qkv)
    dx_attn, gain_attn_term, shift_attn_term = layer_norm_backward(
        attention_input_grad,
        attention_centered_input,
        attention_inverse_deviation,
        attention_norm_gain,
    )
    perceptron_residual_grad, perceptron_gain_term, perceptron_shift_term = layer_norm_backward(
        perceptron_input_grad,
        perceptron_centered_input,
        perceptron_inverse_deviation,
        perceptron_norm_gain,
    )
    tokens_grad = (grad_f32 + dx_attn + perceptron_residual_grad)[None]
    halves = (
        lax.psum_scatter(gain_attn_term, "fsdp", scatter_dimension=0, tiled=True),
        lax.psum_scatter(shift_attn_term, "fsdp", scatter_dimension=0, tiled=True),
        lax.psum_scatter(perceptron_gain_term, "fsdp", scatter_dimension=0, tiled=True),
        lax.psum_scatter(perceptron_shift_term, "fsdp", scatter_dimension=0, tiled=True),
        lax.psum_scatter(qkv_w_term, "fsdp", scatter_dimension=0, tiled=True),
        lax.psum_scatter(qkv_b_term, "fsdp", scatter_dimension=0, tiled=True),
        lax.psum_scatter(proj_w_term, "fsdp", scatter_dimension=0, tiled=True),
        lax.psum_scatter(bias_term, "fsdp", scatter_dimension=0, tiled=True),
        lax.psum_scatter(up_w_term, "fsdp", scatter_dimension=0, tiled=True),
        lax.psum_scatter(up_b_term, "fsdp", scatter_dimension=0, tiled=True),
        lax.psum_scatter(down_w_term, "fsdp", scatter_dimension=0, tiled=True),
        lax.psum_scatter(bias_term, "fsdp", scatter_dimension=0, tiled=True),
    )
    (
        half_a,
        half_b,
        half_c,
        half_d,
        half_e,
        half_f,
        half_g,
        half_h,
        half_i,
        half_j,
        half_k,
        half_l,
    ) = halves
    pieces = (
        lax.psum_scatter(half_a, "ctx", scatter_dimension=0, tiled=True),
        lax.psum_scatter(half_b, "ctx", scatter_dimension=0, tiled=True),
        lax.psum_scatter(half_c, "ctx", scatter_dimension=0, tiled=True),
        lax.psum_scatter(half_d, "ctx", scatter_dimension=0, tiled=True),
        lax.psum_scatter(half_e, "ctx", scatter_dimension=0, tiled=True),
        lax.psum_scatter(half_f, "ctx", scatter_dimension=0, tiled=True),
        lax.psum_scatter(half_g, "ctx", scatter_dimension=0, tiled=True),
        lax.psum_scatter(half_h, "ctx", scatter_dimension=0, tiled=True),
        lax.psum_scatter(half_i, "ctx", scatter_dimension=0, tiled=True),
        lax.psum_scatter(half_j, "ctx", scatter_dimension=0, tiled=True),
        lax.psum_scatter(half_k, "ctx", scatter_dimension=0, tiled=True),
        lax.psum_scatter(half_l, "ctx", scatter_dimension=0, tiled=True),
    )
    (
        piece_a,
        piece_b,
        piece_c,
        piece_d,
        piece_e,
        piece_f,
        piece_g,
        piece_h,
        piece_i,
        piece_j,
        piece_k,
        piece_l,
    ) = pieces
    summed = lax.psum(
        (
            piece_a,
            piece_b,
            piece_c,
            piece_d,
            piece_e,
            piece_f,
            piece_g,
            piece_h,
            piece_i,
            piece_j,
            piece_k,
            piece_l,
        ),
        "seq",
    )
    sum_a, sum_b, sum_c, sum_d, sum_e, sum_f, sum_g, sum_h, sum_i, sum_j, sum_k, sum_l = summed
    shards = (
        lax.all_gather(sum_a, "ctx", axis=0, tiled=True),
        lax.all_gather(sum_b, "ctx", axis=0, tiled=True),
        lax.all_gather(sum_c, "ctx", axis=0, tiled=True),
        lax.all_gather(sum_d, "ctx", axis=0, tiled=True),
        lax.all_gather(sum_e, "ctx", axis=0, tiled=True),
        lax.all_gather(sum_f, "ctx", axis=0, tiled=True),
        lax.all_gather(sum_g, "ctx", axis=0, tiled=True),
        lax.all_gather(sum_h, "ctx", axis=0, tiled=True),
        lax.all_gather(sum_i, "ctx", axis=0, tiled=True),
        lax.all_gather(sum_j, "ctx", axis=0, tiled=True),
        lax.all_gather(sum_k, "ctx", axis=0, tiled=True),
        lax.all_gather(sum_l, "ctx", axis=0, tiled=True),
    )
    return (layer_out, tokens_grad) + tuple(shards)


def solution(mesh):
    placed = (
        P(("seq", "fsdp"), "ctx", None),
        P(("seq", "fsdp"), "ctx", None),
        P(("seq", "fsdp"), None),
        P("fsdp"),
        P("fsdp"),
        P("fsdp"),
        P("fsdp"),
        P("fsdp", None),
        P("fsdp"),
        P("fsdp", None),
        P("fsdp"),
        P("fsdp", None),
        P("fsdp"),
        P("fsdp", None),
        P("fsdp"),
    )
    return jax.shard_map(
        per_device,
        mesh=mesh,
        in_specs=placed,
        out_specs=(
            P(("seq", "fsdp"), "ctx", None),
            P(("seq", "fsdp"), "ctx", None),
            P("fsdp"),
            P("fsdp"),
            P("fsdp"),
            P("fsdp"),
            P("fsdp", None),
            P("fsdp"),
            P("fsdp", None),
            P("fsdp"),
            P("fsdp", None),
            P("fsdp"),
            P("fsdp", None),
            P("fsdp"),
        ),
        check_vma=False,
    )
```

profile of v0, /device:TPU:0, one launch (start us, length us, event | category | flops | bytes accessed | tf_op | source)
XLA Modules:
  0.0 1744.7 jit_solution(2869736051119565915)
XLA Ops:
  85.9 35.2 %all_gather.100 = bf16[64,16,64]{2,0,1:T(8,128)(2,1)S(1)} all-gather(bf16[16,16,64]{2,0,1:T(8,128)(2,1)S(1)} %get-tuple-element.229), channel_id=1, replica_groups=mesh['seq'=4,'ctx'=4,'fsdp'=2] {'ctx'}, dimensions={0}, use_global_device_ids=true | all-gather | bytes 163840 | tf_op jit(solution)/shard_map/all_gather | solution.py:194
  123.4 13.4 all-gather
  137.6 13.4 all-gather.1
  167.2 15.2 all_gather.99
  182.3 15.1 all_gather.98
  197.5 14.6 all_gather.113
  220.5 35.8 %all-reduce.24.cloned.1.call-done = (bf16[64,1024]{1,0:T(8,128)(2,1)}, bf16[64,16,64]{2,0,1:T(8,128)(2,1)}) async-done(((bf16[64,1024]{1,0:T(8,128)(2,1)}, bf16[64,16,64]{2,0,1:T(8,128)(2,1)}), (bf16[64,1024]{1,0:T(8,128)(2,1)}, bf16[64,16,64]{2,0,1:T(8,128)(2,1)})) %all-reduce.24.cloned.1.call-update) | async-done | bytes 262160 | tf_op jit(solution)/shard_map/psum | solution.py:236
  262.0 17.5 %broadcast_multiply_fusion = f32[16,512,1024]{1,2,0:T(8,128)} fusion(bf16[512,16,48]{0,2,1:T(8,128)(2,1)} %copy-done.12, bf16[512,16,8]{0,2,1:T(8,128)(2,1)} %copy-done.31, bf16[512,16,8]{0,2,1:T(8,128)(2,1)} %copy-done.34, bf16[512,16,64]{0,2,1:T(8,128)(2,1)} %collective-permute-done.1, bf16[512,16,48]{0,2,1:T(8,128)(2,1)S(1)} %slice.148, ...), kind=kOutput, calls=%fused_computation.19 | convolution fusion | flops 1093664768 | bytes 36700160 | tf_op jit(solution)/shard_map/qhd,khd->hqk/dot_general | solution.py:98
  279.4 12.8 fusion.137
  292.3 14.7 select_reduce_fusion
  307.1 25.5 %multiply_reduce_fusion = (f32[16,512]{1,0:T(8,128)S(1)}, f32[16,512,1088]{1,2,0:T(8,128)}) fusion(f32[16,512]{1,0:T(8,128)S(1)} %log_add_fusion, pred[512,1088]{0,1:T(8,128)(4,1)S(1)} %pad_add_fusion, f32[16,512,64]{1,2,0:T(8,128)S(1)} %copy-done.4, f32[16,512,1024]{1,2,0:T(8,128)} %broadcast_multiply_fusion, bf16[64,16,64]{0,2,1:T(8,128)(2,1)S(1)} %copy-done.42, ...), kind=kOutput, calls=%fused_computation.15 | convolution fusion | flops 1201528832 | bytes 75203072 | tf_op jit(solution)/shard_map/qhd,khd->hqk/dot_general | solution.py:267
  332.6 28.9 %multiply_convert_fusion = bf16[16,512,1088]{1,2,0:T(8,128)(2,1)} fusion(f32[16,512,1088]{1,2,0:T(8,128)} %get-tuple-element.239, f32[16,512]{1,0:T(8,128)S(1)} %get-tuple-element.238, f32[16,512]{1,0:T(8,128)S(1)} %log_add_fusion, pred[512,1088]{0,1:T(8,128)(4,1)S(1)} %pad_add_fusion, f32[16,512,64]{1,2,0:T(8,128)S(1)} %copy-done.4, ...), kind=kLoop, calls=%fused_computation.14 | loop fusion | flops 62390272 | bytes 89751552 | tf_op jit(solution)/shard_map/convert_element_type | solution.py:269
  361.6 10.4 fusion.142
  374.2 18.4 %fusion.141 = (bf16[1088,16,64]{0,2,1:T(8,128)(2,1)S(1)}, f32[1088,16,64]{0,2,1:T(8,128)}) fusion(f32[16,512]{1,0:T(8,128)S(1)} %log_add_fusion, pred[512,1088]{0,1:T(8,128)(4,1)S(1)} %pad_add_fusion, f32[16,512,64]{1,2,0:T(8,128)S(1)} %copy-done.4, f32[16,512,1024]{1,2,0:T(8,128)} %broadcast_multiply_fusion, bf16[512,16,64]{0,2,1:T(8,128)(2,1)} %bitcast.225, ...), kind=kOutput, calls=%fused_computation.232 | convolution fusion | flops 1187053568 | bytes 43975168 | tf_op jit(solution)/shard_map/hqk,qhd->khd/dot_general | solution.py:274
  396.4 19.5 %fusion.43 = f32[16,64,512]{2,1,0:T(8,128)} fusion(f32[16,512]{1,0:T(8,128)S(1)} %log_add_fusion, pred[512,1088]{0,1:T(8,128)(4,1)S(1)} %pad_add_fusion, bf16[64,16,64]{0,2,1:T(8,128)(2,1)S(1)} %copy-done.43, bf16[512,16,64]{0,2,1:T(8,128)(2,1)} %fusion.87, bf16[512,16,64]{0,2,1:T(8,128)(2,1)} %collective-permute-done, f32[16,512,64]{1,2,0:T(8,128)S(1)} %copy-done.4, ...), kind=kOutput, calls=%fused_computation.85 | convolution fusion | flops 1192099840 | bytes 40566784 | tf_op jit(solution)/shard_map/hqk,khd->qhd/dot_general | solution.py:214
  547.0 27.1 %fusion.5 = (bf16[512,4096]{1,0:T(8,128)(2,1)}, f32[512,4096]{1,0:T(8,128)}) fusion(f32[4096]{0:T(1024)S(1)} %convert_element_type.181, bf16[1024,4096]{1,0:T(8,128)(2,1)} %all-gather.29.cloned.1.call-done, bf16[1,512,1024]{2,1,0:T(8,128)(2,1)S(1)} %copy-done.10, f32[1024]{0:T(1024)S(1)} %bitcast.262, f32[1024]{0:T(1024)S(1)} %bitcast.247, ...), kind=kOutput, calls=%fused_computation.26 | convolution fusion | flops 4436525056 | bytes 22048768 | tf_op jit(solution)/shard_map/dot_general | solution.py:244
  574.1 10.7 convert_reduce_fusion.1
  595.4 10.8 fusion.92
  607.6 18.4 %reduce-scatter.26.cloned.1.call-done = f32[512,4096]{1,0:T(8,128)} async-done(((f32[1024,4096]{1,0:T(8,128)}), f32[512,4096]{1,0:T(8,128)}) %reduce-scatter.26.cloned.1.call-update) | async-done | bytes 8388624 | tf_op jit(solution)/shard_map/reduce_scatter | solution.py:362
  626.1 29.6 %reduce-scatter.30.cloned.1.call-done = f32[2048,1024]{1,0:T(8,128)} async-done(((f32[4096,1024]{1,0:T(8,128)}), f32[2048,1024]{1,0:T(8,128)}) %reduce-scatter.30.cloned.1.call-update) | async-done | bytes 8388624 | tf_op jit(solution)/shard_map/reduce_scatter | solution.py:364
  655.8 47.5 %reduce-scatter.24.cloned.1.call-done = f32[128,1024]{1,0:T(8,128)} async-done(((f32[512,1024]{1,0:T(8,128)}), f32[128,1024]{1,0:T(8,128)}) %reduce-scatter.24.cloned.1.call-update) | async-done | bytes 524304 | tf_op jit(solution)/shard_map/reduce_scatter | solution.py:388
  703.3 112.3 %reduce-scatter.20.cloned.1.call-done = f32[128,3072]{1,0:T(8,128)} async-done(((f32[512,3072]{1,0:T(8,128)}), f32[128,3072]{1,0:T(8,128)}) %reduce-scatter.20.cloned.1.call-update) | async-done | bytes 1572880 | tf_op jit(solution)/shard_map/reduce_scatter | solution.py:386
  815.5 147.2 %reduce-scatter.28.cloned.1.call-done = f32[128,4096]{1,0:T(8,128)} async-done(((f32[512,4096]{1,0:T(8,128)}), f32[128,4096]{1,0:T(8,128)}) %reduce-scatter.28.cloned.1.call-update) | async-done | bytes 2097168 | tf_op jit(solution)/shard_map/reduce_scatter | solution.py:390
  962.8 147.4 %reduce-scatter.32.cloned.1.call-done = f32[512,1024]{1,0:T(8,128)} async-done(((f32[2048,1024]{1,0:T(8,128)}), f32[512,1024]{1,0:T(8,128)}) %reduce-scatter.32.cloned.1.call-update) | async-done | bytes 2097168 | tf_op jit(solution)/shard_map/reduce_scatter | solution.py:392
  1110.3 143.7 %all-reduce.22.cloned.1.call-done = (f32[128,3072]{1,0:T(8,128)}, f32[128,1024]{1,0:T(8,128)}, f32[128,4096]{1,0:T(8,128)}, f32[512,1024]{1,0:T(8,128)}) async-done(((f32[128,3072]{1,0:T(8,128)}, f32[128,1024]{1,0:T(8,128)}, f32[128,4096]{1,0:T(8,128)}, f32[512,1024]{1,0:T(8,128)}), (f32[128,3072]{1,0:T(8,128)}, f32[128,1024]{1,0:T(8,128)}, f32[128,4096]{1,0:T(8,128)}, ...) | async-done | bytes 6291472 | tf_op jit(solution)/shard_map/psum | solution.py:409
  1287.2 19.5 %all-reduce.14 = (f32[512]{0:T(512)S(1)}, f32[512]{0:T(512)S(1)}, f32[512]{0:T(512)S(1)}, f32[512]{0:T(512)S(1)}, f32[1536]{0:T(1024)S(1)}, /*index=5*/f32[512]{0:T(512)S(1)}, f32[2048]{0:T(1024)S(1)}) all-reduce(f32[512]{0:T(512)S(1)} %dynamic-slice.2, ...), channel_id=8, replica_groups=mesh['seq'=4,'ctx'=4,'fsdp'=2] {'ctx'}, use_global_device_ids=true, to_apply=%region_26.28.clone | all-reduce | flops 6144 | bytes 49152
  1325.6 12.0 all-gather.13
  1338.3 13.7 all-gather.15
  1378.2 13.8 all-gather.12
  1402.9 15.4 all-gather.33.cloned.1.call-done
  1418.3 149.2 %all-gather.37.cloned.1.call-done = f32[512,4096]{1,0:T(8,128)} async-done(((f32[128,4096]{1,0:T(8,128)}), f32[512,4096]{1,0:T(8,128)}) %all-gather.37.cloned.1.call-update) | async-done | bytes 8388624 | tf_op jit(solution)/shard_map/all_gather | solution.py:436
  1567.5 149.5 %all-gather.39.cloned.1.call-done = f32[2048,1024]{1,0:T(8,128)} async-done(((f32[512,1024]{1,0:T(8,128)}), f32[2048,1024]{1,0:T(8,128)}) %all-gather.39.cloned.1.call-update) | async-done | bytes 8388624 | tf_op jit(solution)/shard_map/all_gather | solution.py:438
  (399 shorter events, 368.8 us)
Async XLA Ops:
  7.2 15.7 all-gather.27.cloned.1.call-start
  8.0 34.5 %all-gather.25.cloned.1.call-start = ((), (), s32[]{:S(2)}) async-start(), calls=%async_computation.11 | async-start | bytes 9437184 | tf_op jit(solution)/shard_map/all_gather | solution.py:142
  8.7 247.5 %all-reduce.24.cloned.1.call-start = ((), (), s32[]{:S(2)}) async-start(), calls=%async_computation.31 | async-start | bytes 786432 | tf_op jit(solution)/shard_map/psum | solution.py:236
  17.1 240.5 %copy-start.29 = (pred[64,512]{1,0:T(8,128)(4,1)}, pred[64,512]{1,0:T(8,128)(4,1)S(1)}, u32[]{:S(2)}) copy-start(pred[64,512]{1,0:T(8,128)(4,1)S(1)} %broadcast_compare_fusion) | copy-start | bytes 98308
  62.3 199.7 %collective-permute-start.1 = (bf16[512,16,64]{0,2,1:T(8,128)(2,1)}, bf16[512,16,64]{0,2,1:T(8,128)(2,1)}, u32[]{:S(2)}, u32[]{:S(2)}) collective-permute-start(bf16[512,16,64]{0,2,1:T(8,128)(2,1)} %pad_maximum_fusion.2), channel_id=1, source_target_pairs={{0,2},{2,4},{4,6},{1,3},{3,5},{5,7},{8,10},{10,12},{12,14},{9,11},... | collective-permute-start | bytes 3145736 | tf_op jit(solution)/shard_map/ppermute | solution.py:23
  77.3 229.8 %collective-permute-start = (bf16[512,16,64]{0,2,1:T(8,128)(2,1)}, bf16[512,16,64]{0,2,1:T(8,128)(2,1)}, u32[]{:S(2)}, u32[]{:S(2)}) collective-permute-start(bf16[512,16,64]{0,2,1:T(8,128)(2,1)} %fusion.87), channel_id=1, source_target_pairs={{0,2},{2,4},{4,6},{1,3},{3,5},{5,7},{8,10},{10,12},{12,14},{9,11},... | collective-permute-start | bytes 3145736 | tf_op jit(solution)/shard_map/ppermute | solution.py:23
  123.4 134.2 %copy-start = (f32[16,64,512]{2,1,0:T(8,128)}, f32[16,64,512]{2,1,0:T(8,128)S(1)}, u32[]{:S(2)}) copy-start(f32[16,64,512]{2,1,0:T(8,128)S(1)} %get-tuple-element.235) | copy-start | bytes 6291460
  160.4 97.2 %copy-start.46 = (f32[16,64]{1,0:T(8,128)S(1)}, f32[16,64]{1,0:T(8,128)}, u32[]{:S(2)}) copy-start(f32[16,64]{1,0:T(8,128)} %copy-done.45) | copy-start | bytes 12292
  217.6 205.7 %reduce-scatter.34.cloned.1.call-start = ((), (), s32[]{:S(2)}) async-start(), calls=%async_computation.27 | async-start | bytes 163840
  261.9 202.0 %reduce-scatter.36.cloned.1.call-start = ((), (), s32[]{:S(2)}) async-start(), calls=%async_computation.28 | async-start | bytes 163840
  374.2 91.4 %reduce-scatter.38.cloned.1.call-start = ((), (), s32[]{:S(2)}) async-start(), calls=%async_computation.29 | async-start | bytes 163840
  394.9 152.1 %all-gather.29.cloned.1.call-start = ((), (), s32[]{:S(2)}) async-start(), calls=%async_computation.13 | async-start | bytes 12582912 | tf_op jit(solution)/shard_map/all_gather | solution.py:146
  395.6 178.5 %all-gather.31.cloned.1.call-start = ((), (), s32[]{:S(2)}) async-start(), calls=%async_computation.14 | async-start | bytes 12582912 | tf_op jit(solution)/shard_map/all_gather | solution.py:148
  396.4 209.9 %reduce-scatter.22.cloned.1.call-start = ((), (), s32[]{:S(2)}) async-start(), calls=%async_computation.18 | async-start | bytes 6291456 | tf_op jit(solution)/shard_map/reduce_scatter | solution.py:360
  423.2 183.8 %reduce-scatter.18.cloned.1.call-start = ((), (), s32[]{:S(2)}) async-start(), calls=%async_computation.15 | async-start | bytes 18874368 | tf_op jit(solution)/shard_map/reduce_scatter | solution.py:358
  427.1 39.6 %collective-permute-start.2 = (bf16[512,16,64]{0,2,1:T(8,128)(2,1)}, bf16[512,16,64]{0,2,1:T(8,128)(2,1)}, u32[]{:S(2)}, u32[]{:S(2)}) collective-permute-start(bf16[512,16,64]{0,2,1:T(8,128)(2,1)} %slice.118), channel_id=1, source_target_pairs={{2,0},{4,2},{6,4},{3,1},{5,3},{7,5},{10,8},{12,10},{14,12},{11,9},... | collective-permute-start | bytes 3145736 | tf_op jit(solution)/shard_map/ppermute | solution.py:23
  462.6 40.0 %collective-permute-start.3 = (bf16[512,16,64]{0,2,1:T(8,128)(2,1)}, bf16[512,16,64]{0,2,1:T(8,128)(2,1)}, u32[]{:S(2)}, u32[]{:S(2)}) collective-permute-start(bf16[512,16,64]{0,2,1:T(8,128)(2,1)} %slice.124), channel_id=1, source_target_pairs={{2,0},{4,2},{6,4},{3,1},{5,3},{7,5},{10,8},{12,10},{14,12},{11,9},... | collective-permute-start | bytes 3145736 | tf_op jit(solution)/shard_map/ppermute | solution.py:23
  540.9 85.1 %reduce-scatter.26.cloned.1.call-start = ((), (), s32[]{:S(2)}) async-start(), calls=%async_computation.21 | async-start | bytes 25165824 | tf_op jit(solution)/shard_map/reduce_scatter | solution.py:362
  595.3 60.4 %reduce-scatter.30.cloned.1.call-start = ((), (), s32[]{:S(2)}) async-start(), calls=%async_computation.24 | async-start | bytes 25165824 | tf_op jit(solution)/shard_map/reduce_scatter | solution.py:364
  606.2 97.0 %reduce-scatter.24.cloned.1.call-start = ((), (), s32[]{:S(2)}) async-start(), calls=%async_computation.19 | async-start | bytes 2621440 | tf_op jit(solution)/shard_map/reduce_scatter | solution.py:388
  607.0 208.6 %reduce-scatter.20.cloned.1.call-start = ((), (), s32[]{:S(2)}) async-start(), calls=%async_computation.16 | async-start | bytes 7864320 | tf_op jit(solution)/shard_map/reduce_scatter | solution.py:386
  607.6 355.2 %reduce-scatter.28.cloned.1.call-start = ((), (), s32[]{:S(2)}) async-start(), calls=%async_computation.22 | async-start | bytes 10485760 | tf_op jit(solution)/shard_map/reduce_scatter | solution.py:390
  626.1 484.2 %reduce-scatter.32.cloned.1.call-start = ((), (), s32[]{:S(2)}) async-start(), calls=%async_computation.25 | async-start | bytes 10485760 | tf_op jit(solution)/shard_map/reduce_scatter | solution.py:392
  655.8 598.3 %all-reduce.22.cloned.1.call-start = ((), (), s32[]{:S(2)}) async-start(), calls=%async_computation.30 | async-start | bytes 12582912 | tf_op jit(solution)/shard_map/psum | solution.py:409
  1110.2 145.9 %copy-start.76 = (u32[32]{0:T(128)S(1)}, u32[32]{0:T(128)}, u32[]{:S(2)}) copy-start(u32[32]{0:T(128)} %constant.184) | copy-start | bytes 388
  1110.3 148.5 %copy-start.75 = (u32[32]{0:T(128)S(1)}, u32[32]{0:T(128)}, u32[]{:S(2)}) copy-start(u32[32]{0:T(128)} %constant.188) | copy-start | bytes 388
  1110.3 151.0 %copy-start.72 = (bf16[512]{0:T(512)(128)(2,1)S(1)}, bf16[512]{0:T(512)(128)(2,1)}, u32[]{:S(2)}) copy-start(bf16[512]{0:T(512)(128)(2,1)} %param.29) | copy-start | bytes 3076
  1110.3 152.8 %copy-start.73 = (bf16[512]{0:T(512)(128)(2,1)S(1)}, bf16[512]{0:T(512)(128)(2,1)}, u32[]{:S(2)}) copy-start(bf16[512]{0:T(512)(128)(2,1)} %param.33) | copy-start | bytes 3076
  1110.3 292.6 %all-gather.35.cloned.1.call-start = ((), (), s32[]{:S(2)}) async-start(), calls=%async_computation.20 | async-start | bytes 2621440 | tf_op jit(solution)/shard_map/all_gather | solution.py:434
  1254.1 164.2 %all-gather.33.cloned.1.call-start = ((), (), s32[]{:S(2)}) async-start(), calls=%async_computation.17 | async-start | bytes 7864320 | tf_op jit(solution)/shard_map/all_gather | solution.py:432
  1254.9 312.7 %all-gather.37.cloned.1.call-start = ((), (), s32[]{:S(2)}) async-start(), calls=%async_computation.23 | async-start | bytes 10485760 | tf_op jit(solution)/shard_map/all_gather | solution.py:436
  1255.4 461.5 %all-gather.39.cloned.1.call-start = ((), (), s32[]{:S(2)}) async-start(), calls=%async_computation.26 | async-start | bytes 10485760 | tf_op jit(solution)/shard_map/all_gather | solution.py:438
  (76 other events, 824.4 us)
Sparse Core Ops, SparseCore 0:
  9.6 13.3 all-gather.26
  24.5 17.9 all-gather.24
  217.7 38.4 all-reduce.23
  262.0 18.6 reduce-scatter.33
  374.3 18.6 reduce-scatter.35
  395.2 18.4 reduce-scatter.37
  415.2 18.0 all-gather.28
  434.9 21.0 all-gather.30
  458.2 13.1 reduce-scatter.21
  541.0 24.7 reduce-scatter.17
  595.4 30.5 reduce-scatter.25
  628.2 27.5 reduce-scatter.29
  658.1 45.0 reduce-scatter.23
  705.4 110.0 reduce-scatter.19
  817.7 144.9 reduce-scatter.27
  965.0 145.1 reduce-scatter.31
  1113.8 140.2 all-reduce.21
  1255.5 46.7 all-gather.34
  1303.9 114.3 all-gather.32
  1419.7 147.7 all-gather.36
  1569.1 147.8 all-gather.38
where the time goes:
time: 1750 us; the launch traced here: 1740 us
  waiting for transfers between devices  1010 us (58%)
  matrix products  230 us (13%)
  blocking collectives  228 us (13%)
  local copies, waits for them, and re-layouts  151 us (9%)
  other arithmetic  89.2 us (5%)
  between operations  19.9 us (1%)
    all_gather x1, waiting for transfers between devices, per_device(): lax.all_gather(sum_k, 'ctx', axis=0, tiled=True)  149 us
    all_gather x1, waiting for transfers between devices, per_device(): lax.all_gather(sum_i, 'ctx', axis=0, tiled=True)  149 us
    reduce_scatter x1, waiting for transfers between devices, per_device(): lax.psum_scatter(half_k, 'ctx', scatter_dimension=0, tiled=True)  147 us
    reduce_scatter x1, waiting for transfers between devices, per_device(): lax.psum_scatter(half_i, 'ctx', scatter_dimension=0, tiled=True)  147 us
    psum x1, waiting for transfers between devices, per_device(): lax.psum((piece_a, piece_b, piece_c, piece_d, piece_e, piece_f, piece_g,...  144 us
    reduce_scatter x1, waiting for transfers between devices, per_device(): lax.psum_scatter(half_e, 'ctx', scatter_dimension=0, tiled=True)  112 us
    unnamed x212, local copies, waits for them, and re-layouts  48.7 us
    reduce_scatter x1, waiting for transfers between devices, per_device(): lax.psum_scatter(half_g, 'ctx', scatter_dimension=0, tiled=True)  47.5 us
  transfers between devices with their start and end apart: 25, of which 13 were waited for; matrix products, arithmetic and copies ran while one was open for 24% of the time, Pallas kernels for 0%

commit v1 on v0

v1 whole, which is shorter than its diff:
```python
import functools
import math

import jax
import jax.numpy as jnp
from jax import lax
from jax.experimental import pallas as pl
from jax.experimental.pallas import tpu as pltpu
from jax.sharding import PartitionSpec as P

D = 1024
H = 16
HD = 64
ROT = 16
WIN = 512
FF = 4096
HALF = D // 2
PAIR = 2 * HD
ROW = 512
TILE = 128

epsilon = 1e-05
negative = -1e30
rotary_base = 10000.0
f32 = jnp.float32
bf16 = jnp.bfloat16
VMEM = 50 * 2**20


def shape(dims, dtype):
    return jax.ShapeDtypeStruct(dims, dtype)


def params():
    return pltpu.CompilerParams(vmem_limit_bytes=VMEM)


def cost(flops, moved):
    return pl.CostEstimate(flops=int(flops), bytes_accessed=int(moved), transcendentals=0)


def dot(left, right):
    return jnp.dot(left, right, preferred_element_type=f32)


def dot_nt(left, right):
    return lax.dot_general(left, right, (((1,), (1,)), ((), ())), preferred_element_type=f32)


def pair(block):
    return lax.ppermute(block, "fsdp", [(0, 1), (1, 0)])


def exchange(block, axis, distance):
    return lax.ppermute(block, axis, [(i, i ^ distance) for i in range(lax.axis_size(axis))])


def shifted(block, distance):
    devices = range(lax.axis_size("ctx"))
    return lax.ppermute(
        block, "ctx", [(i - distance, i) for i in devices if i - distance in devices]
    )


def doubling(axis):
    distance, out = 1, []
    while distance < lax.axis_size(axis):
        out.append(distance)
        distance *= 2
    return out


def first_axis(kind):
    distance = 1 if kind == "xy" else 2
    return lambda block: exchange(block, "seq", distance)


def second_axis(kind):
    distance = 2 if kind == "xy" else 1
    return lambda block: exchange(block, "seq", distance)


def added(*parts):
    total = parts[0].astype(f32)
    for part in parts[1:]:
        total = total + part.astype(f32)
    return total.astype(bf16)


def reduced(send, keep, kind):
    first, second = first_axis(kind), second_axis(kind)
    recv = first(send)
    other = second(added(keep[0], recv[0]))
    return added(keep[1], recv[1], other)


def swapped(tile):
    return [tile[:TILE], pair(tile[:TILE])] if False else [tile[TILE:], pair(tile[:TILE])]


def spread(piece, kind):
    first, second = first_axis(kind), second_axis(kind)
    beside = second(piece)
    return piece, beside, first(piece), first(beside)


def norm_parts(x):
    center = x - jnp.mean(x, axis=-1, keepdims=True)
    inverse = lax.rsqrt(jnp.mean(center * center, axis=-1, keepdims=True) + epsilon)
    return center * inverse, inverse


def norm_body(x_ref, gain_ref, shift_ref, a_ref, at_ref):
    normal, _ = norm_parts(x_ref[...].astype(f32))
    a = (normal * gain_ref[...] + shift_ref[...]).astype(bf16)
    a_ref[...] = a
    at_ref[...] = a.T


def norm_call(x, gain, shift):
    rows, step = x.shape[0], 256
    vector = pl.BlockSpec((1, D), lambda i: (0, 0))
    return pl.pallas_call(
        norm_body,
        grid=(rows // step,),
        in_specs=[pl.BlockSpec((step, D), lambda i: (i, 0)), vector, vector],
        out_specs=[
            pl.BlockSpec((step, D), lambda i: (i, 0)),
            pl.BlockSpec((D, step), lambda i: (0, i)),
        ],
        out_shape=[shape((rows, D), bf16), shape((D, rows), bf16)],
        compiler_params=params(),
        cost_estimate=cost(rows * D * 10, rows * D * 6),
        name="norm",
    )(x, gain, shift)


def unit_body(
    n_alias,
    idx,
    a_ref,
    at_ref,
    dy_ref,
    wu_ref,
    wd_ref,
    bu_ref,
    *rest,
):
    send_ref, keep_ref, act_ref, dup_ref, bias_ref = rest[n_alias:]
    core, one, two = idx[0], idx[1], idx[2]
    step = pl.program_id(0)
    sub = one ^ (1 - step)
    rows = a_ref.shape[0]
    chunk = 256
    bias_ref[...] = jnp.zeros_like(bias_ref)

    def tokens(i, carry):
        at = pl.ds(pl.multiple_of(i * chunk, chunk), chunk)
        up = dot(a_ref[at, :], wu_ref[...]) + bu_ref[...]
        grad = dot_nt(dy_ref[at, :], wd_ref[...])
        cdf = 0.5 * (1.0 + lax.erf(up * (0.5**0.5)))
        density = jnp.exp(-0.5 * up * up) * (1.0 / math.sqrt(2.0 * math.pi))
        act_ref[at, :] = (up * cdf).astype(bf16)
        dup = (grad * (cdf + up * density)).astype(bf16)
        dup_ref[at, :] = dup
        bias_ref[...] += jnp.sum(dup.astype(f32), axis=0, keepdims=True)
        return carry

    lax.fori_loop(0, rows // chunk, tokens, 0)
    down = dot(act_ref[...].T, dy_ref[...]).astype(bf16)

    def put_down(ref):
        for r in range(2):
            ref[jnp.where(two == r, 1, 0), 1, :, :] = down[:, r * HALF : (r + 1) * HALF]

    @pl.when(step == 0)
    def _():
        put_down(send_ref)

    @pl.when(step == 1)
    def _():
        put_down(keep_ref)

    lanes = pl.ds(pl.multiple_of(sub * chunk, chunk), chunk)
    for ref, p in ((send_ref, 1 - one), (keep_ref, one)):
        for m in range(2):
            left = at_ref[m, p].reshape(2 * TILE, rows)
            up_grad = dot(left, dup_ref[...]).astype(bf16)
            for r in range(2):
                at = pl.ds(pl.multiple_of(jnp.where(core == m, TILE, 0), TILE), TILE)
                ref[jnp.where(two == r, 1, 0), 0, at, lanes] = up_grad[
                    r * TILE : (r + 1) * TILE
                ]


def unit_call(idx, f, a, at, dy, w_up, w_down, b_up, act_all, dup_all):
    rows = a.shape[0]
    sub = lambda s, idx: 2 * f + (idx[1] ^ (1 - s))
    whole = lambda s, idx: (0, 0)
    column = pl.BlockSpec((rows, 256), lambda s, idx: (0, sub(s, idx)))
    grads = pl.BlockSpec((2, 2, 256, 512), lambda s, idx: (0, 0, 0, 0))
    alias = [] if act_all is None else [act_all, dup_all]
    return pl.pallas_call(
        functools.partial(unit_body, len(alias)),
        grid_spec=pltpu.PrefetchScalarGridSpec(
            num_scalar_prefetch=1,
            grid=(2,),
            in_specs=[
                pl.BlockSpec((rows, D), whole),
                pl.BlockSpec((2, 2, 2, TILE, rows), lambda s, idx: (0, 0, 0, 0, 0)),
                pl.BlockSpec((rows, D), whole),
                pl.BlockSpec((D, 256), lambda s, idx: (0, sub(s, idx))),
                pl.BlockSpec((256, D), lambda s, idx: (sub(s, idx), 0)),
                pl.BlockSpec((1, 256), lambda s, idx: (0, sub(s, idx))),
            ]
            + [pl.BlockSpec(memory_space=pl.ANY)] * len(alias),
            out_specs=[
                grads,
                grads,
                column,
                column,
                pl.BlockSpec((1, 256), lambda s, idx: (0, idx[1] ^ (1 - s))),
            ],
        ),
        out_shape=[
            shape((2, 2, 256, 512), bf16),
            shape((2, 2, 256, 512), bf16),
            shape((rows, FF // 2), bf16),
            shape((rows, FF // 2), bf16),
            shape((1, 512), f32),
        ],
        input_output_aliases={7: 2, 8: 3} if alias else {},
        compiler_params=params(),
        cost_estimate=cost(8 * rows * D * 512, 14 * 2**20),
        name="feed_forward",
    )(idx, a, at.reshape(2, 2, 2, TILE, rows), dy, w_up, w_down, b_up, *alias)


def rotated(field, cosine, sine, direction):
    lane = lax.broadcasted_iota(jnp.int32, field.shape, 1) % HD
    partner = jnp.where(
        lane < ROT // 2,
        pltpu.roll(field, PAIR - ROT // 2, 1),
        pltpu.roll(field, ROT // 2, 1),
    )
    return field * cosine + (direction * sine) * partner


def qkv_body(x_ref, gain_ref, shift_ref, w_ref, b_ref, cos_ref, sin_ref, *outs):
    a_ref, at_ref, q_ref, k_ref, v_ref = outs
    normal, _ = norm_parts(x_ref[...].astype(f32))
    a = (normal * gain_ref[...] + shift_ref[...]).astype(bf16)
    a_ref[...] = a
    at_ref[...] = a.T
    cosine, sine = cos_ref[...], sin_ref[...]
    for t, ref in enumerate((q_ref, k_ref, v_ref)):
        part = slice(t * HALF, (t + 1) * HALF)
        lin = dot(a, w_ref[:, part]) + b_ref[:, part]
        if t == 2:
            ref[...] = lin.astype(bf16)
            continue
        for j in range(HALF // PAIR):
            lanes = slice(j * PAIR, (j + 1) * PAIR)
            ref[:, lanes] = rotated(lin[:, lanes], cosine, sine, 1.0).astype(bf16)


def qkv_call(x, gain, shift, w, b, cosine, sine, step):
    rows = x.shape[0]
    tables = cosine.shape[0] // step
    vector = pl.BlockSpec((1, D), lambda i: (0, 0))
    table = pl.BlockSpec((step, PAIR), lambda i: (i % tables, 0))
    third = pl.BlockSpec((step, HALF), lambda i: (i, 0))
    return pl.pallas_call(
        qkv_body,
        grid=(rows // step,),
        in_specs=[
            pl.BlockSpec((step, D), lambda i: (i, 0)),
            vector,
            vector,
            pl.BlockSpec((D, 3 * HALF), lambda i: (0, 0)),
            pl.BlockSpec((1, 3 * HALF), lambda i: (0, 0)),
            table,
            table,
        ],
        out_specs=[
            pl.BlockSpec((step, D), lambda i: (i, 0)),
            pl.BlockSpec((D, step), lambda i: (0, i)),
            third,
            third,
            third,
        ],
        out_shape=[shape((rows, D), bf16), shape((D, rows), bf16)]
        + [shape((rows, HALF), bf16)] * 3,
        compiler_params=params(),
        cost_estimate=cost(2 * rows * D * 3 * HALF, rows * D * 9 + 3 * 2**20),
        name="qkv",
    )(x, gain, shift, w, b, cosine, sine)


def heads_beside(block_t):
    dim = lax.broadcasted_iota(jnp.int32, block_t.shape, 0)
    zero = jnp.zeros_like(block_t)
    return jnp.concatenate(
        [jnp.where(dim < HD, block_t, zero), jnp.where(dim < HD, zero, block_t)], axis=1
    )


def heads_below(block):
    dim = lax.broadcasted_iota(jnp.int32, block.shape, 1)
    zero = jnp.zeros_like(block)
    return jnp.concatenate(
        [jnp.where(dim < HD, block, zero), jnp.where(dim < HD, zero, block)], axis=0
    )


def heads_back(both):
    n = both.shape[1] // 2
    dim = lax.broadcasted_iota(jnp.int32, (PAIR, n), 0)
    return jnp.where(dim < HD, both[:, :n], both[:, n:])


def near_body(
    info,
    q_ref,
    k_ref,
    v_ref,
    dol_ref,
    kp_ref,
    vp_ref,
    kg_ref,
    vg_ref,
    glob_ref,
    cos_ref,
    sin_ref,
    cosp_ref,
    sinp_ref,
    cosg_ref,
    sing_ref,
    o_ref,
    dq_ref,
    dk_ref,
    dv_ref,
    dkp_ref,
    dvp_ref,
    dkg_ref,
    dvg_ref,
    dk_acc,
    dv_acc,
):
    scale = HD**-0.5
    base = info[0]
    absent = jnp.where(base == 0, f32(negative), f32(0.0))
    keys = jnp.concatenate([kp_ref[...], k_ref[...]], axis=0)
    values = jnp.concatenate([vp_ref[...], v_ref[...]], axis=0)
    keys_t = keys.T
    values_t = values.T
    gkeys, gvalues = kg_ref[...], vg_ref[...]
    glob_n = gkeys.shape[0]
    gkeys_t = gkeys.astype(f32).T.astype(bf16)
    gvalues_t = gvalues.astype(f32).T.astype(bf16)
    query = (q_ref[...].astype(f32) * scale).astype(bf16)
    query_t = query.T
    dol = dol_ref[...]
    dol_t = dol.T
    dk_acc[...] = jnp.zeros_like(dk_acc)
    dv_acc[...] = jnp.zeros_like(dv_acc)
    two = 2 * TILE
    window = WIN + TILE
    cosine, sine = cos_ref[...], sin_ref[...]
    row = lax.broadcasted_iota(jnp.int32, (TILE, two), 0)
    lane = lax.broadcasted_iota(jnp.int32, (TILE, two), 1) % TILE
    glane = lax.broadcasted_iota(jnp.int32, (glob_n, two), 1) % TILE
    gpos = jnp.concatenate([glob_ref[0], glob_ref[0]], axis=1)
    dkg = jnp.zeros((glob_n, PAIR), f32)
    dvg = jnp.zeros((glob_n, PAIR), f32)
    for t in range(ROW // TILE):
        rows = slice(t * TILE, (t + 1) * TILE)
        span = slice(t * TILE, t * TILE + window)
        cut = WIN - t * TILE
        q_beside = heads_beside(query_t[:, rows])
        d_beside = heads_beside(dol_t[:, rows])
        q_below = heads_below(query[rows])
        d_below = heads_below(dol[rows])
        score = dot(keys[span], q_beside)
        far = dot(gkeys, q_beside)
        parts = [
            jnp.where(row > lane, score[:TILE] + absent, negative),
        ]
        if cut > TILE:
            parts.append(score[TILE:cut] + absent)
        parts.append(score[cut:WIN])
        if t == 0:
            parts.pop()
        parts.append(jnp.where(row <= lane, score[WIN:], negative))
        score = jnp.concatenate(parts, axis=0)
        far = jnp.where(base + t * TILE + glane - gpos >= WIN, far, negative)
        top = jnp.maximum(
            jnp.max(score, axis=0, keepdims=True), jnp.max(far, axis=0, keepdims=True)
        )
        prob = jnp.exp(score - top)
        far_prob = jnp.exp(far - top)
        total = jnp.sum(prob, axis=0, keepdims=True) + jnp.sum(far_prob, axis=0, keepdims=True)
        inverse = 1.0 / total
        prob = prob * inverse
        far_prob = far_prob * inverse
        low, far_low = prob.astype(bf16), far_prob.astype(bf16)
        out_t = dot(values_t[:, span], low) + dot(gvalues_t, far_low)
        o_ref[rows, :] = heads_back(out_t).T.astype(bf16)
        d_prob = dot(values[span], d_beside)
        d_far = dot(gvalues, d_beside)
        delta = jnp.sum(prob * d_prob, axis=0, keepdims=True) + jnp.sum(
            far_prob * d_far, axis=0, keepdims=True
        )
        d_score = (prob * (d_prob - delta)).astype(bf16)
        d_far = (far_prob * (d_far - delta)).astype(bf16)
        dq_t = dot(keys_t[:, span], d_score) + dot(gkeys_t, d_far)
        dq = heads_back(dq_t).T * scale
        dq_ref[rows, :] = rotated(dq, cosine[rows], sine[rows], -1.0).astype(bf16)
        dk_acc[span, :] += dot(d_score, q_below)
        dv_acc[span, :] += dot(low, d_below)
        dkg = dkg + dot(d_far, q_below)
        dvg = dvg + dot(far_low, d_below)
    dk_ref[...] = dk_acc[ROW:, :]
    dv_ref[...] = dv_acc[ROW:, :]
    dkp_ref[...] = rotated(dk_acc[:ROW, :], cosp_ref[...], sinp_ref[...], -1.0).astype(bf16)
    dvp_ref[...] = dv_acc[:ROW, :].astype(bf16)
    dkg_ref[...] = rotated(dkg, cosg_ref[...], sing_ref[...], -1.0).astype(bf16)
    dvg_ref[...] = dvg.astype(bf16)


def near_call(info, q, k, v, dol, k2, v2, glob_wide, tables, tables2):
    glob_n = glob_wide.shape[1]
    own = pl.BlockSpec((ROW, PAIR), lambda j, h, info: (j, h))
    first = 2 * ROW // glob_n
    glob = pl.BlockSpec((glob_n, PAIR), lambda j, h, info: (first + j, h))
    glob_out = pl.BlockSpec((glob_n, PAIR), lambda j, h, info: (j, h))
    table = pl.BlockSpec((ROW, PAIR), lambda j, h, info: (0, 0))
    gtable = pl.BlockSpec((glob_n, PAIR), lambda j, h, info: (first + j, 0))
    rows = q.shape[0]
    own_low, own_high = shape((rows, HALF), bf16), shape((rows, HALF), f32)
    glob_low = shape((2 * glob_n, HALF), bf16)
    return pl.pallas_call(
        near_body,
        grid_spec=pltpu.PrefetchScalarGridSpec(
            num_scalar_prefetch=1,
            grid=(2, HALF // PAIR),
            in_specs=[own] * 6
            + [glob] * 2
            + [pl.BlockSpec((1, glob_n, PAIR), lambda j, h, info: (j, 0, 0))]
            + [table] * 4
            + [gtable] * 2,
            out_specs=[own] * 6 + [glob_out] * 2,
            scratch_shapes=[pltpu.VMEM((2 * ROW, PAIR), f32)] * 2,
        ),
        out_shape=[own_low, own_low, own_high, own_high, own_low, own_low, glob_low, glob_low],
        compiler_params=params(),
        cost_estimate=cost(8 * 4 * 6 * 2 * 704 * 256 * 256, 16 * 2**20),
        name="near",
    )(
        info,
        q,
        k,
        v,
        dol,
        k2,
        v2,
        k2,
        v2,
        glob_wide,
        tables[0],
        tables[1],
        tables2[0],
        tables2[1],
        tables2[0],
        tables2[1],
    )


def glob_first_body(info, qg_ref, k_ref, v_ref, glob_ref, out_ref):
    glob_n = qg_ref.shape[0]
    query = qg_ref[...].astype(f32) * HD**-0.5
    beside = heads_beside(query.T).astype(bf16)
    score = dot(k_ref[...], beside)
    key_pos = info[0] + lax.broadcasted_iota(jnp.int32, score.shape, 0)
    mask = key_pos <= glob_ref[0][0:1]
    masked = jnp.where(mask, score, negative)
    top = jnp.max(masked, axis=0, keepdims=True)
    prob = jnp.where(mask, jnp.exp(masked - top), 0.0)
    total = jnp.sum(prob, axis=0, keepdims=True)
    both = dot(v_ref[...].T, prob.astype(bf16))
    lane = lax.broadcasted_iota(jnp.int32, (HD, 2 * glob_n), 1)
    out_ref[0, 0:HD, :] = jnp.where(lane < glob_n, both[:HD], both[HD:])
    out_ref[0, HD : HD + 1, :] = top
    out_ref[0, HD + 1 : HD + 2, :] = total
    out_ref[0, HD + 2 : HD + 8, :] = jnp.zeros((6, 2 * glob_n), f32)


def glob_first_call(info, q2, k, v, glob_row):
    glob_n = glob_row.shape[2] // 2
    first = 2 * ROW // glob_n
    own = pl.BlockSpec((ROW, PAIR), lambda j, h, info: (j, h))
    pairs = HALF // PAIR
    return pl.pallas_call(
        glob_first_body,
        grid_spec=pltpu.PrefetchScalarGridSpec(
            num_scalar_prefetch=1,
            grid=(2, pairs),
            in_specs=[
                pl.BlockSpec((glob_n, PAIR), lambda j, h, info: (first + j, h)),
                own,
                own,
                pl.BlockSpec((1, 8, 2 * glob_n), lambda j, h, info: (j, 0, 0)),
            ],
            out_specs=pl.BlockSpec(
                (1, HD + 8, 2 * glob_n), lambda j, h, info: (j * pairs + h, 0, 0)
            ),
        ),
        out_shape=shape((2 * pairs, HD + 8, 2 * glob_n), f32),
        compiler_params=params(),
        cost_estimate=cost(8 * 2 * 2 * 512 * 128 * 256, 3 * 2**20),
        name="glob_first",
    )(info, q2, k, v, glob_row)


def merged(first, second):
    top_a, top_b = first[:, HD : HD + 1], second[:, HD : HD + 1]
    top = jnp.maximum(top_a, top_b)
    weight_a, weight_b = jnp.exp(top_a - top), jnp.exp(top_b - top)
    total = first[:, HD + 1 : HD + 2] * weight_a + second[:, HD + 1 : HD + 2] * weight_b
    out = first[:, :HD] * weight_a + second[:, :HD] * weight_b
    return jnp.concatenate([out, top, total, first[:, HD + 2 :]], axis=1)


def glob_second_body(
    info,
    qg_ref,
    dolg_ref,
    k_ref,
    v_ref,
    stat_ref,
    glob_ref,
    near_ref,
    dk_in,
    dv_in,
    cos_ref,
    sin_ref,
    cosg_ref,
    sing_ref,
    o_ref,
    ot_ref,
    dk_ref,
    dv_ref,
    dqg_ref,
):
    scale = HD**-0.5
    glob_n = qg_ref.shape[0]
    keys, values = k_ref[...], v_ref[...]
    query = qg_ref[...].astype(f32) * scale
    q_beside = heads_beside(query.T).astype(bf16)
    q_below = heads_below(query.astype(bf16))
    dol = dolg_ref[...]
    dol_t = dol.astype(f32).T
    d_beside = heads_beside(dol_t).astype(bf16)
    d_below = heads_below(dol)
    out_t = stat_ref[0, 0:HD, :]
    top = stat_ref[0, HD : HD + 1, :]
    total = stat_ref[0, HD + 1 : HD + 2, :]
    out_t = out_t * (1.0 / total)
    lse = top + jnp.log(total)
    delta = jnp.sum(
        out_t * jnp.concatenate([dol_t[:HD], dol_t[HD:]], axis=1), axis=0, keepdims=True
    )
    score = dot(keys, q_beside)
    key_pos = info[0] + lax.broadcasted_iota(jnp.int32, score.shape, 0)
    positions = glob_ref[0][0:1]
    mask = key_pos <= positions
    prob = jnp.where(mask, jnp.exp(jnp.where(mask, score, negative) - lse), 0.0)
    d_prob = dot(values, d_beside)
    d_score = (prob * (d_prob - delta)).astype(bf16)
    low = prob.astype(bf16)
    dk = dk_in[...] + dot(d_score, q_below)
    dv = dv_in[...] + dot(low, d_below)
    dk_ref[...] = rotated(dk, cos_ref[...], sin_ref[...], -1.0).astype(bf16)
    dv_ref[...] = dv.astype(bf16)
    dq_both = dot(keys.T, d_score)
    dq_t = jnp.concatenate([dq_both[:HD, :glob_n], dq_both[HD:, glob_n:]], axis=0)
    dqg_ref[...] = rotated(dq_t.T * scale, cosg_ref[...], sing_ref[...], -1.0).astype(bf16)
    rows = jnp.concatenate([out_t[:, :glob_n], out_t[:, glob_n:]], axis=0).T.astype(bf16)
    place = (key_pos[:, :glob_n] == positions[:, :glob_n]).astype(f32)
    hit = jnp.sum(place, axis=1, keepdims=True) > 0.0
    out = jnp.where(hit, dot(place.astype(bf16), rows).astype(bf16), near_ref[...])
    o_ref[...] = out
    ot_ref[...] = out.T


def glob_second_call(info, q2, dolg, k, v, stats, glob_row, near, dk, dv, tables, tables2):
    glob_n = glob_row.shape[2] // 2
    first = 2 * ROW // glob_n
    pairs = HALF // PAIR
    rows = k.shape[0]
    own = pl.BlockSpec((ROW, PAIR), lambda j, h, info: (j, h))
    glob = pl.BlockSpec((glob_n, PAIR), lambda j, h, info: (j, h))
    gtable = pl.BlockSpec((glob_n, PAIR), lambda j, h, info: (first + j, 0))
    table = pl.BlockSpec((ROW, PAIR), lambda j, h, info: (0, 0))
    return pl.pallas_call(
        glob_second_body,
        grid_spec=pltpu.PrefetchScalarGridSpec(
            num_scalar_prefetch=1,
            grid=(2, pairs),
            in_specs=[
                pl.BlockSpec((glob_n, PAIR), lambda j, h, info: (first + j, h)),
                glob,
                own,
                own,
                pl.BlockSpec((1, HD + 8, 2 * glob_n), lambda j, h, info: (j * pairs + h, 0, 0)),
                pl.BlockSpec((1, 8, 2 * glob_n), lambda j, h, info: (j, 0, 0)),
                own,
                own,
                own,
                table,
                table,
                gtable,
                gtable,
            ],
            out_specs=[
                own,
                pl.BlockSpec((PAIR, ROW), lambda j, h, info: (h, j)),
                own,
                own,
                glob,
            ],
        ),
        out_shape=[
            shape((rows, HALF), bf16),
            shape((HALF, rows), bf16),
            shape((rows, HALF), bf16),
            shape((rows, HALF), bf16),
            shape((2 * glob_n, HALF), bf16),
        ],
        compiler_params=params(),
        cost_estimate=cost(8 * 5 * 2 * 512 * 128 * 256, 10 * 2**20),
        name="glob_second",
    )(
        info,
        q2,
        dolg,
        k,
        v,
        stats,
        glob_row,
        near,
        dk,
        dv,
        tables[0],
        tables[1],
        tables2[0],
        tables2[1],
    )


def split_rows(idx, step, ref, wide, tile, core, two):
    for m in range(2):
        at = pl.ds(pl.multiple_of(jnp.where(core == m, TILE, 0), TILE), TILE)
        for r in range(2):
            begin = (2 * m + r) * TILE
            ref[jnp.where(two == r, 1, 0), tile, at, :] = wide[begin : begin + TILE]


def weights_body(sources, idx, *refs):
    core, two = idx[0], idx[2]
    step = pl.program_id(0)
    send_ref, keep_ref = refs[-2:]

    def run(ref):
        at = 0
        for tile, (kind, count) in enumerate(sources):
            total = None
            for _ in range(count):
                left = refs[at][...]
                if kind == "spread":
                    left = left.reshape(4 * TILE, left.shape[-1])
                term = dot(left, refs[at + 1][...])
                total = term if total is None else total + term
                at += 2
            total = total.astype(bf16)
            if kind == "spread":
                split_rows(idx, step, ref, total, tile, core, two)
            else:
                for r in range(2):
                    ref[jnp.where(two == r, 1, 0), tile, :, :] = total[
                        :, r * HALF : (r + 1) * HALF
                    ]

    @pl.when(step == 0)
    def _():
        run(send_ref)

    @pl.when(step == 1)
    def _():
        run(keep_ref)


def weights_call(idx, tiles):
    part = lambda s, idx: idx[1] ^ (1 - s)
    operands, specs, sources, flops = [], [], [], 0
    for kind, products in tiles:
        sources.append((kind, len(products)))
        for left, right in products:
            n = left.shape[1]
            if kind == "spread":
                left = left.reshape(2, 2, 2, TILE, n)
                specs.append(
                    pl.BlockSpec(
                        (2, 1, 2, TILE, n), lambda s, idx: (0, part(s, idx), 0, 0, 0)
                    )
                )
            else:
                specs.append(pl.BlockSpec((256, n), lambda s, idx: (part(s, idx), 0)))
            specs.append(pl.BlockSpec(right.shape, lambda s, idx: (0, 0)))
            operands += [left, right]
            flops += 2 * n * 512 * 1024
    out = pl.BlockSpec((2, 2, 256, 512), lambda s, idx: (0, 0, 0, 0))
    return pl.pallas_call(
        functools.partial(weights_body, tuple(sources)),
        grid_spec=pltpu.PrefetchScalarGridSpec(
            num_scalar_prefetch=1, grid=(2,), in_specs=specs, out_specs=[out, out]
        ),
        out_shape=[shape((2, 2, 256, 512), bf16)] * 2,
        compiler_params=params(),
        cost_estimate=cost(flops, 10 * 2**20),
        name="weight_grads",
    )(idx, *operands)


def input_body(thirds, with_more, *refs):
    refs = list(refs)
    x_ref, gain_ref, w_ref = refs[:3]
    parts = refs[3 : 3 + thirds]
    at = 3 + thirds
    more_ref = refs[at] if with_more else None
    g_ref, sums_ref, bias_ref = refs[-3:]

    @pl.when(pl.program_id(0) == 0)
    def _():
        sums_ref[...] = jnp.zeros_like(sums_ref)
        bias_ref[...] = jnp.zeros_like(bias_ref)

    grad = None
    width = parts[0].shape[1]
    first = 3 - thirds if thirds < 3 and width == HALF else 0
    for i, ref in enumerate(parts):
        part = ref[...]
        lanes = slice((first + i) * width, (first + i + 1) * width)
        term = dot_nt(part, w_ref[:, lanes])
        grad = term if grad is None else grad + term
        bias_ref[0:1, lanes] += jnp.sum(part.astype(f32), axis=0, keepdims=True)
    normal, _ = norm_parts(x_ref[...].astype(f32))
    sums_ref[0:1, :] += jnp.sum(grad * normal, axis=0, keepdims=True)
    sums_ref[1:2, :] += jnp.sum(grad, axis=0, keepdims=True)
    g = grad * gain_ref[...]
    if with_more:
        g = g + more_ref[...].astype(f32)
    g_ref[...] = g.astype(g_ref.dtype)


def input_call(x, at_block, rows, step, gain, w, parts, more, kind):
    width = parts[0].shape[1]
    vector = pl.BlockSpec((1, D), lambda i: (0, 0))
    specs = [
        pl.BlockSpec((step, D), lambda i: (at_block + i, 0)),
        vector,
        pl.BlockSpec(w.shape, lambda i: (0, 0)),
    ] + [pl.BlockSpec((step, width), lambda i: (i, 0))] * len(parts)
    operands = [x, gain, w, *parts]
    if more is not None:
        specs.append(pl.BlockSpec((step, D), lambda i: (i, 0)))
        operands.append(more)
    return pl.pallas_call(
        functools.partial(input_body, len(parts), more is not None),
        grid=(rows // step,),
        in_specs=specs,
        out_specs=[
            pl.BlockSpec((step, D), lambda i: (i, 0)),
            pl.BlockSpec((8, D), lambda i: (0, 0)),
            pl.BlockSpec((8, w.shape[1]), lambda i: (0, 0)),
        ],
        out_shape=[
            shape((rows, D), kind),
            shape((8, D), f32),
            shape((8, w.shape[1]), f32),
        ],
        compiler_params=params(),
        cost_estimate=cost(2 * rows * D * width * len(parts), rows * D * 8 + 4 * 2**20),
        name="input_grads",
    )(*operands)


def place_body(kinds, n_alias, idx, *refs):
    pieces = refs[:4]
    outs = refs[4 + n_alias :]
    half = pl.program_id(1)

    for g in range(4):

        @pl.when(pl.program_id(0) == g)
        def _(g=g):
            for tile, out in enumerate(outs):
                at = pl.ds(pl.multiple_of(tile * 256 + half * TILE, TILE), TILE)
                out[...] = pieces[g][at, :].astype(f32)


def place_call(idx, pieces, targets):
    def mapped(where):
        def index(g, h, idx):
            return where(idx[1] ^ (g // 2), idx[2] ^ (g % 2), h, idx[0])

        return index

    alias = [buf for buf, _, _ in targets if buf is not None]
    aliases, at = {}, 5
    for out, (buf, _, _) in enumerate(targets):
        if buf is not None:
            aliases[at] = out
            at += 1
    whole = pl.BlockSpec((512, 512), lambda g, h, idx: (0, 0))
    return pl.pallas_call(
        functools.partial(place_body, None, len(alias)),
        grid_spec=pltpu.PrefetchScalarGridSpec(
            num_scalar_prefetch=1,
            grid=(4, 2),
            in_specs=[whole] * 4 + [pl.BlockSpec(memory_space=pl.ANY)] * len(alias),
            out_specs=[pl.BlockSpec((TILE, 512), mapped(where)) for _, _, where in targets],
        ),
        out_shape=[shape(dims, f32) for _, dims, _ in targets],
        input_output_aliases=aliases,
        compiler_params=params(),
        cost_estimate=cost(0, 6 * 2**20),
        name="place",
    )(idx, *pieces, *alias)


def rotary_tables(positions):
    lane = jnp.arange(PAIR, dtype=jnp.int32) % HD
    half = ROT // 2
    freqs = rotary_base ** (-2.0 * (lane % half).astype(f32) / ROT)
    angles = positions.astype(f32)[:, None] * freqs[None, :]
    active = (lane < ROT)[None, :]
    sign = jnp.where(lane < half, -1.0, 1.0)[None, :]
    return jnp.where(active, jnp.cos(angles), 1.0), jnp.where(active, jnp.sin(angles) * sign, 0.0)


def per_device(
    tokens,
    cotangent,
    global_pos,
    attn_gain,
    attn_shift,
    mlp_gain,
    mlp_shift,
    qkv_weight,
    qkv_bias,
    proj_weight,
    proj_bias,
    up_weight,
    up_bias,
    down_weight,
    down_bias,
):
    n_ctx = lax.axis_size("ctx")
    core = lax.axis_index("fsdp")
    seq = lax.axis_index("seq")
    ctx = lax.axis_index("ctx")
    x_bit, y_bit = seq & 1, seq >> 1
    base = ctx * ROW
    own_x = tokens[0]
    own_dy = cotangent[0]
    glob_n = global_pos.shape[1]
    share = glob_n // n_ctx
    info = jnp.stack([base]).astype(jnp.int32)
    index = {
        "xy": jnp.stack([core, x_bit, y_bit]).astype(jnp.int32),
        "yx": jnp.stack([core, y_bit, x_bit]).astype(jnp.int32),
    }

    other_x = pair(own_x)
    up_halves = up_weight.reshape(HALF, 2, FF // 2)
    up_recv = pair(lax.dynamic_index_in_dim(up_halves, 1 - core, 1, False))
    other_dy = pair(own_dy)
    vectors = jnp.concatenate(
        [
            v.reshape(-1, 512)
            for v in (attn_gain, attn_shift, mlp_gain, mlp_shift, proj_bias, down_bias, qkv_bias)
        ],
        axis=0,
    )
    vectors_recv = pair(vectors)
    prev_x = shifted(own_x, 1)
    own_glob = lax.dynamic_slice_in_dim(global_pos[0], ctx * share, share, 0)
    pick = (own_glob[:, None] - base == jnp.arange(ROW, dtype=jnp.int32)[None, :]).astype(bf16)
    picked = jnp.stack([dot(pick, own_x), dot(pick, own_dy)]).astype(bf16)[None]
    qkv_halves = qkv_weight.reshape(HALF, 3, 2, HALF)
    qkv_recv = pair(lax.dynamic_index_in_dim(qkv_halves, 1 - core, 2, False))
    pos_pair = jnp.stack([global_pos[0], pair(global_pos[0])])
    other_prev = pair(prev_x)
    for distance in doubling("ctx"):
        beside = exchange(picked, "ctx", distance)
        picked = jnp.concatenate([picked, beside], axis=0)
    picked = jnp.take(picked, jnp.arange(n_ctx, dtype=jnp.int32) ^ ctx, axis=0)
    picked = jnp.transpose(picked, (1, 0, 2, 3)).reshape(2, glob_n, D)
    other_picked = pair(picked)

    low_first = core == 0

    def whole(mine, recv):
        return jnp.where(
            low_first,
            jnp.concatenate([mine, recv], axis=0),
            jnp.concatenate([recv, mine], axis=0),
        )

    both = jnp.where(
        low_first,
        jnp.stack([vectors, vectors_recv], axis=1),
        jnp.stack([vectors_recv, vectors], axis=1),
    ).astype(f32)
    gain_a, shift_a, gain_m, shift_m, bias_p, bias_d = (
        both[i].reshape(1, D) for i in range(6)
    )
    bias_qkv = jnp.swapaxes(both[6:9], 0, 1).reshape(3, 2, HALF)
    bias_qkv = lax.dynamic_index_in_dim(bias_qkv, core, 1, False).reshape(1, 3 * HALF)
    bias_up = up_bias.astype(f32).reshape(1, FF // 2)

    x = jnp.concatenate([own_x, other_x], axis=0)
    dy = jnp.concatenate([own_dy, other_dy], axis=0)
    w_up = whole(lax.dynamic_index_in_dim(up_halves, core, 1, False), up_recv)
    a_mlp, a_mlp_t = norm_call(x, gain_m, shift_m)
    kinds = ("xy", "yx", "xy", "yx", "xy", "yx")
    act = dup = None
    grads, up_sums = [], []
    for f in range(4):
        send, keep, act, dup, sums = unit_call(
            index[kinds[f]], f, a_mlp, a_mlp_t, dy, w_up, down_weight, bias_up, act, dup
        )
        grads.append((send, keep))
        up_sums.append(sums)

    tables = rotary_tables(base + jnp.arange(ROW, dtype=jnp.int32))
    before = base - ROW + jnp.arange(ROW, dtype=jnp.int32)
    tables2 = rotary_tables(jnp.concatenate([before, before, pos_pair.reshape(-1)]))
    w_qkv = whole(
        lax.dynamic_index_in_dim(qkv_halves, core, 2, False).reshape(HALF, 3 * HALF),
        qkv_recv.reshape(HALF, 3 * HALF),
    )
    a1, a1_t, q1, k1, v1 = qkv_call(x, gain_a, shift_a, w_qkv, bias_qkv, *tables, 256)
    x2 = jnp.concatenate([prev_x, other_prev, picked[0], other_picked[0]], axis=0)
    a2, a2_t, q2, k2, v2 = qkv_call(x2, gain_a, shift_a, w_qkv, bias_qkv, *tables2, 384)
    row_pos = base + jnp.arange(ROW, dtype=jnp.int32)
    is_glob = jnp.any(row_pos[None, :, None] == pos_pair[:, None, :], axis=2).reshape(2 * ROW, 1)
    dol = jnp.where(is_glob, 0.0, dot_nt(dy, proj_weight)).astype(bf16)
    dolg = dot_nt(
        jnp.concatenate([picked[1], other_picked[1]], axis=0), proj_weight
    ).astype(bf16)
    glob_row = jnp.broadcast_to(
        jnp.concatenate([pos_pair, pos_pair], axis=1)[:, None, :], (2, 8, 2 * glob_n)
    )
    glob_wide = jnp.broadcast_to(pos_pair[:, :, None], (2, glob_n, PAIR))
    stats = glob_first_call(info, q2, k1, v1, glob_row)
    for distance in doubling("ctx"):
        stats = merged(stats, exchange(stats, "ctx", distance))
    near, dq1, dk1, dv1, dkp, dvp, dkg, dvg = near_call(
        info, q1, k1, v1, dol, k2, v2, glob_wide, tables, tables2
    )
    ol, ol_t, dk1, dv1, dqg = glob_second_call(
        info, q2, dolg, k1, v1, stats, glob_row, near, dk1, dv1, tables, tables2
    )
    a2p_t, a2g_t = a2_t[:, : 2 * ROW], a2_t[:, 2 * ROW :]
    grads.append(
        weights_call(
            index[kinds[4]],
            [
                ("spread", [(a1_t, dv1), (a2p_t, dvp), (a2g_t, dvg)]),
                ("rows", [(ol_t, dy)]),
            ],
        )
    )
    grads.append(
        weights_call(
            index[kinds[5]],
            [
                ("spread", [(a1_t, dq1), (a2g_t, dqg)]),
                ("spread", [(a1_t, dk1), (a2p_t, dkp), (a2g_t, dkg)]),
            ],
        )
    )

    up_out = down_out = qkv_out = proj_out = None
    up_dims, down_dims = (HALF, FF), (FF // 2, D)
    qkv_dims, proj_dims = (HALF, 3 * D), (HALF, D)
    last = None
    for u, (send, keep) in enumerate(grads):
        kind = kinds[u]
        quarter = reduced(send, keep, kind)
        tiles = []
        for tile in range(2):
            if (tile == 0) or u == 5:
                tiles += [quarter[tile, TILE:], pair(quarter[tile, :TILE])]
            else:
                tiles.append(quarter[tile])
        piece = jnp.concatenate(tiles, axis=0)
        if last is not None:
            piece, _ = lax.optimization_barrier((piece, last))
        piece = lax.psum(piece, "ctx")
        last = piece
        pieces = spread(piece, kind)
        if u < 4:
            up_out, down_out = place_call(
                index[kind],
                pieces,
                [
                    (up_out, up_dims, lambda p, r, h, c, u=u: (p * 2 + r, (c ^ h) * 4 + u)),
                    (down_out, down_dims, lambda p, r, h, c, u=u: (u * 4 + p * 2 + h, r)),
                ],
            )
        elif u == 4:
            qkv_out, proj_out = place_call(
                index[kind],
                pieces,
                [
                    (None, qkv_dims, lambda p, r, h, c: (p * 2 + r, 4 + (c ^ h))),
                    (None, proj_dims, lambda p, r, h, c: (p * 2 + h, r)),
                ],
            )
        else:
            for t in range(2):
                rows = [jnp.concatenate([v[t * 256 : (t + 1) * 256]] * 2, axis=0) for v in pieces]
                (qkv_out,) = place_call(
                    index[kind],
                    rows,
                    [(qkv_out, qkv_dims, lambda p, r, h, c, t=t: (p * 2 + r, 2 * t + (c ^ h)))],
                )

    part = (dot(act, down_weight) + dot(ol, proj_weight)).astype(bf16)
    result = own_x.astype(f32) + part[:ROW].astype(f32) + pair(part[ROW:]).astype(f32)
    layer_out = (result + bias_p + bias_d).astype(bf16)[None]

    g_mlp, sums_m, _ = input_call(x, 0, 2 * ROW, 256, gain_m, w_up, [dup], None, f32)
    g_own, sums_1, bias_1 = input_call(
        x, 0, 2 * ROW, 256, gain_a, w_qkv, [dq1, dk1, dv1], g_mlp, bf16
    )
    g_prev, sums_2, bias_2 = input_call(x2, 0, 2 * ROW, 256, gain_a, w_qkv, [dkp, dvp], None, bf16)
    g_glob, sums_3, bias_3 = input_call(
        x2, 2 * ROW // 128, 2 * glob_n, 128, gain_a, w_qkv, [dqg, dkg, dvg], None, bf16
    )
    from_prev = shifted(added(g_prev[:ROW], pair(g_prev[ROW:])), -1)
    glob_sum = added(g_glob[:glob_n], pair(g_glob[glob_n:]))
    for distance in doubling("ctx"):
        glob_sum = added(glob_sum, exchange(glob_sum, "ctx", distance))
    place = (row_pos[:, None] == global_pos[0][None, :]).astype(bf16)
    g = (
        g_own[:ROW].astype(f32)
        + pair(g_own[ROW:]).astype(f32)
        + from_prev.astype(f32)
        + dot(place, glob_sum)
    )
    normal, inverse = norm_parts(own_x.astype(f32))
    lower = inverse * (
        g
        - jnp.mean(g, axis=-1, keepdims=True)
        - normal * jnp.mean(g * normal, axis=-1, keepdims=True)
    )
    tokens_grad = (own_dy.astype(f32) + lower)[None]

    sums_a = sums_1[:2] + sums_2[:2] + sums_3[:2]
    dy_sum = jnp.sum(own_dy.astype(f32), axis=0)
    qkv_sum = (bias_1[0] + bias_2[0] + bias_3[0]).reshape(3, 1, HALF)
    mine = jnp.arange(2, dtype=jnp.int32)[None, :, None] == core
    qkv_sum = jnp.where(mine, qkv_sum, 0.0).reshape(2, 3, 512)
    split = jnp.concatenate(
        [
            sums_a.reshape(2, 2, 512).swapaxes(0, 1),
            sums_m[:2].reshape(2, 2, 512).swapaxes(0, 1),
            dy_sum.reshape(2, 1, 512),
            qkv_sum,
        ],
        axis=1,
    )
    kept = lax.dynamic_index_in_dim(split, core, 0, False)
    given = lax.dynamic_index_in_dim(split, 1 - core, 0, False)
    total = jnp.concatenate([kept + pair(given)] + up_sums, axis=0)
    for axis in ("seq", "ctx"):
        for distance in doubling(axis):
            total = total + exchange(total, axis, distance)
    return (
        layer_out,
        tokens_grad,
        total[0],
        total[1],
        total[2],
        total[3],
        qkv_out,
        total[5:8].reshape(-1),
        proj_out,
        total[4],
        up_out,
        total[8:12].reshape(-1),
        down_out,
        total[4],
    )


def solution(mesh):
    rows = P(("seq", "fsdp"), "ctx", None)
    vector, matrix = P("fsdp"), P("fsdp", None)
    return jax.shard_map(
        per_device,
        mesh=mesh,
        in_specs=(
            rows,
            rows,
            P(("seq", "fsdp"), None),
            vector,
            vector,
            vector,
            vector,
            matrix,
            vector,
            matrix,
            vector,
            matrix,
            vector,
            matrix,
            vector,
        ),
        out_specs=(
            rows,
            rows,
            vector,
            vector,
            vector,
            vector,
            matrix,
            vector,
            matrix,
            vector,
            matrix,
            vector,
            matrix,
            vector,
        ),
        check_vma=False,
    )
```

time: 1750 us -> 759 us (0.43)
  waiting for transfers between devices: 1010 us -> 301 us
  blocking collectives: 228 us -> 0 us
  Pallas kernels: 0 us -> 211 us
  matrix products: 230 us -> 22.2 us
  local copies, waits for them, and re-layouts: 151 us -> 85.8 us
  starting transfers between devices: 11.4 us -> 54.9 us
  other arithmetic: 89.2 us -> 57.7 us
    reduce_scatter x8 -> x0, waiting for transfers between devices: 503 us -> none  [the longest x1 147 us: per_device(): lax.psum_scatter(half_k, 'ctx', scatter_dimension=0, tiled=True)]
    all_gather x8 -> x0, waiting for transfers between devices: 326 us -> none  [the longest x1 149 us: per_device(): lax.all_gather(sum_k, 'ctx', axis=0, tiled=True)]
    pallas_call x0 -> x23, Pallas kernels: none -> 211 us  [the longest x4 49.5 us: unit_call(): pl.pallas_call(functools.partial(unit_body, len(alias)), grid_spec=pltpu....]
    dot_general x26 -> x7, matrix products: 230 us -> 22.2 us  [the longest x5 17.9 us: dot(): return jnp.dot(left, right, preferred_element_type=f32)]
    all_gather x21 -> x0, blocking collectives: 196 us -> none  [the longest x1 35.2 us: per_device(): lax.all_gather(jnp.take(query, own_index, axis=0), 'ctx', axis=0, tiled=T...]
    ppermute x4 -> x62, waiting for transfers between devices: 0.01 us -> 145 us  [the longest x40 141 us: exchange(): lax.ppermute(block, axis, [(i, i ^ distance) for i in range(lax.axis_size...]
    ppermute x4 -> x62, starting transfers between devices: 10.6 us -> 54.4 us  [the longest x40 44.4 us: exchange(): lax.ppermute(block, axis, [(i, i ^ distance) for i in range(lax.axis_size...]
    psum x2 -> x6, waiting for transfers between devices: 180 us -> 155 us  [per_device(): piece = lax.psum(piece, 'ctx')]
  transfers between devices with their start and end apart: 25 -> 68, of which waited for: 13 -> 22; matrix products, arithmetic and copies ran while one was open for 24% -> 20% of each run, Pallas kernels for 0% -> 27%
where the time goes in v1:
time: 759 us; the launch traced here: 748 us
  waiting for transfers between devices  301 us (40%)
  Pallas kernels  211 us (28%)
  local copies, waits for them, and re-layouts  85.8 us (11%)
  other arithmetic  57.7 us (8%)
  starting transfers between devices  54.9 us (7%)
  matrix products  22.2 us (3%)
  between operations  15.6 us (2%)
    psum x6, waiting for transfers between devices, per_device(): piece = lax.psum(piece, 'ctx')  155 us
    ppermute x40, waiting for transfers between devices, exchange(): lax.ppermute(block, axis, [(i, i ^ distance) for i in range(lax.axis_size...  141 us
    pallas_call x4, Pallas kernels, unit_call(): pl.pallas_call(functools.partial(unit_body, len(alias)), grid_spec=pltpu....  49.5 us
    pallas_call x1, Pallas kernels, near_call(): pl.pallas_call(near_body, grid_spec=pltpu.PrefetchScalarGridSpec(num_scal...  46 us
    ppermute x40, starting transfers between devices, exchange(): lax.ppermute(block, axis, [(i, i ^ distance) for i in range(lax.axis_size...  44.4 us
    pallas_call x7, Pallas kernels, place_call(): pl.pallas_call(functools.partial(place_body, None, len(alias)), grid_spec...  34.2 us
    pallas_call x4, Pallas kernels, input_call(): pl.pallas_call(functools.partial(input_body, len(parts), more is not None...  27.9 us
    unnamed x128, local copies, waits for them, and re-layouts  26.6 us
  transfers between devices with their start and end apart: 68, of which 22 were waited for; matrix products, arithmetic and copies ran while one was open for 20% of the time, Pallas kernels for 27%

profile of v1, /device:TPU:0, one launch (start us, length us, event | category | flops | bytes accessed | tf_op | source)
XLA Modules:
  0.0 748.2 jit_solution(928170244332871757)
XLA Ops:
  36.1 7.8 %reshape.345 = bf16[512,2,2048]{2,1,0:T(2,128)(2,1)} reshape(bf16[512,4096]{1,0:T(8,128)(2,1)} %param.26) | data formatting | bytes 8388608 | tf_op jit(solution)/shard_map/reshape | solution.py:886
  43.9 11.7 %constant_dynamic-slice_fusion.5 = (bf16[512,1,2048]{2,1,0:T(2,128)(2,1)}, bf16[512,1,2048]{2,1,0:T(2,128)(2,1)}) fusion(bf16[512,2,2048]{2,1,0:T(2,128)(2,1)} %reshape.345, s32[]{:T(128)S(6)} %select_n.148, s32[]{:T(128)S(6)} %select_n.149), kind=kLoop, calls=%fused_computation.165 | loop fusion | bytes 8388616 | tf_op jit(solution)/shard_map/jit(dynamic_index_in_dim)/dynamic_slice | solution.py:935
  70.9 8.3 %collective-permute-done.7 = bf16[2,2,16,1024]{3,2,1,0:T(8,128)(2,1)S(1)} collective-permute-done((bf16[2,2,16,1024]{3,2,1,0:T(8,128)(2,1)S(1)}, bf16[2,2,16,1024]{3,2,1,0:T(8,128)(2,1)S(1)}, u32[]{:S(2)}, u32[]{:S(2)}) %collective-permute-start.7) | collective-permute-done | bytes 131104 | tf_op jit(solution)/shard_map/ppermute | solution.py:55
  109.5 8.3 %qkv.3 = (bf16[1024,1024]{1,0:T(8,128)(2,1)}, bf16[1024,1024]{1,0:T(8,128)(2,1)}, bf16[1024,512]{1,0:T(8,128)(2,1)S(1)}, bf16[1024,512]{1,0:T(8,128)(2,1)S(1)}, bf16[1024,512]{1,0:T(8,128)(2,1)S(1)}) custom-call(bf16[1024,1024]{1,0:T(8,128)(2,1)} %pad_maximum_fusion.1.x_ref.refs_0_, f32[1,1024]{1,0:T(1,128)S(1)} %bitcast.176, f32[1,1024]{1,0:T(1,128)S(1)} %bitcast.186, ...), custom_call_target="tpu_custom_call" | custom-call | flops 3221225472 | bytes 12582912 | tf_op jit(solution)/shard_map/qkv/pallas_call | solution.py:273
  121.6 8.8 %qkv.2 = (bf16[1152,1024]{1,0:T(8,128)(2,1)}, bf16[1024,1152]{1,0:T(8,128)(2,1)}, bf16[1152,512]{1,0:T(8,128)(2,1)S(1)}, bf16[1152,512]{1,0:T(8,128)(2,1)S(1)}, bf16[1152,512]{1,0:T(8,128)(2,1)}) custom-call(bf16[1152,1024]{1,0:T(8,128)(2,1)} %pad_maximum_fusion.x_ref.refs_0_, f32[1,1024]{1,0:T(1,128)S(1)} %bitcast.177, f32[1,1024]{1,0:T(1,128)S(1)} %bitcast.187, ...), custom_call_target="tpu_custom_call" | custom-call | flops 3623878656 | bytes 13762560 | tf_op jit(solution)/shard_map/qkv/pallas_call | solution.py:273
  141.1 46.0 %near.1 = (bf16[1024,512]{1,0:T(8,128)(2,1)S(1)}, bf16[1024,512]{1,0:T(8,128)(2,1)}, f32[1024,512]{1,0:T(8,128)}, f32[1024,512]{1,0:T(8,128)}, bf16[1024,512]{1,...) custom-call(s32[1]{0:T(128)} %bitcast.13.info, ...), custom_call_target="tpu_custom_call" | custom-call | flops 17716740096 | bytes 16777216 | tf_op jit(solution)/shard_map/near/pallas_call | solution.py:442
  190.5 6.7 input_grads.6
  205.3 12.4 %feed_forward.4 = (bf16[2,2,256,512]{3,2,1,0:T(8,128)(2,1)}, bf16[2,2,256,512]{3,2,1,0:T(8,128)(2,1)S(1)}, bf16[1024,2048]{1,0:T(8,128)(2,1)}, bf16[1024,2048]{1,0:T(8,128)(2,1)}, f32[1,512]{1,0:T(1,128)S(1)}) custom-call(s32[3]{0:T(128)S(1)} %pad_add_fusion.2.idx, bf16[1024,1024]{1,0:T(8,128)(2,1)} %copy-done.2, bf16[2,2,2,128,1024]{4,3,2,1,0:T(8,128)(2,1)} %bitcast.191, ...), custom_call_target="tpu_custom_call" | custom-call | flops 4294967296 | bytes 14680064 | tf_op jit(solution)/shard_map/feed_forward/pallas_call | solution.py:203
  220.2 12.5 %feed_forward.5 = (bf16[2,2,256,512]{3,2,1,0:T(8,128)(2,1)}, bf16[2,2,256,512]{3,2,1,0:T(8,128)(2,1)S(1)}, bf16[1024,2048]{1,0:T(8,128)(2,1)}, bf16[1024,2048]{1,0:T(8,128)(2,1)}, f32[1,512]{1,0:T(1,128)S(1)}) custom-call(s32[3]{0:T(128)S(1)} %pad_add_fusion.1.idx, bf16[1024,1024]{1,0:T(8,128)(2,1)} %copy-done.2, ...), custom_call_target="tpu_custom_call", output_to_operand_aliasing={{2}: (7, {}), {3}: (8, {})} | custom-call | flops 4294967296 | bytes 14680064 | tf_op jit(solution)/shard_map/feed_forward/pallas_call | solution.py:203
  235.2 12.1 %feed_forward.6 = (bf16[2,2,256,512]{3,2,1,0:T(8,128)(2,1)S(1)}, bf16[2,2,256,512]{3,2,1,0:T(8,128)(2,1)S(1)}, bf16[1024,2048]{1,0:T(8,128)(2,1)}, bf16[1024,2048]{1,0:T(8,128)(2,1)}, f32[1,512]{1,0:T(1,128)S(1)}) custom-call(s32[3]{0:T(128)S(1)} %pad_add_fusion.2.idx, bf16[1024,1024]{1,0:T(8,128)(2,1)} %copy-done.2, ...), custom_call_target="tpu_custom_call", output_to_operand_aliasing={{2}: (7, {}), {3}: (8, {})} | custom-call | flops 4294967296 | bytes 14680064 | tf_op jit(solution)/shard_map/feed_forward/pallas_call | solution.py:203
  249.4 12.5 %feed_forward.7 = (bf16[2,2,256,512]{3,2,1,0:T(8,128)(2,1)}, bf16[2,2,256,512]{3,2,1,0:T(8,128)(2,1)S(1)}, bf16[1024,2048]{1,0:T(8,128)(2,1)}, bf16[1024,2048]{1,0:T(8,128)(2,1)}, f32[1,512]{1,0:T(1,128)S(1)}) custom-call(s32[3]{0:T(128)S(1)} %pad_add_fusion.1.idx, bf16[1024,1024]{1,0:T(8,128)(2,1)} %copy-done.2, ...), custom_call_target="tpu_custom_call", output_to_operand_aliasing={{2}: (7, {}), {3}: (8, {})} | custom-call | flops 4294967296 | bytes 14680064 | tf_op jit(solution)/shard_map/feed_forward/pallas_call | solution.py:203
  265.4 9.7 %input_grads.4 = (f32[1024,1024]{1,0:T(8,128)}, f32[8,1024]{1,0:T(8,128)S(1)}, f32[8,2048]{1,0:T(8,128)}) custom-call(bf16[1024,1024]{1,0:T(8,128)(2,1)S(1)} %copy-done.3, f32[1,1024]{1,0:T(1,128)S(1)} %bitcast.182, bf16[1024,2048]{1,0:T(8,128)(2,1)} %maximum_select_fusion.wu_ref.refs_2_, bf16[1024,2048]{1,0:T(8,128)(2,1)} %get-tuple-element.109.refs_3_), custom_call_target="tpu_custom_call" | custom-call | flops 4294967296 | bytes 12582912 | tf_op jit(solution)/shard_map/input_grads/pallas_call | solution.py:778
  279.1 11.0 %glob_second.1 = (bf16[1024,512]{1,0:T(8,128)(2,1)S(1)}, bf16[512,1024]{1,0:T(8,128)(2,1)}, bf16[1024,512]{1,0:T(8,128)(2,1)}, bf16[1024,512]{1,0:T(8,128)(2,1)}, bf16[128,512]{1,0:T(8,128)(2,1)S(1)}) custom-call(s32[1]{0:T(128)} %bitcast.13.info, bf16[1152,512]{1,0:T(8,128)(2,1)} %copy-done.5, bf16[128,512]{1,0:T(8,128)(2,1)S(1)} %convolution_convert_fusion.dolg_ref, ...), custom_call_target="tpu_custom_call" | custom-call | flops 1342177280 | bytes 10485760 | tf_op jit(solution)/shard_map/glob_second/pallas_call | solution.py:605
  296.6 7.5 weight_grads.3
  305.1 7.5 %weight_grads.2 = (bf16[2,2,256,512]{3,2,1,0:T(8,128)(2,1)S(1)}, bf16[2,2,256,512]{3,2,1,0:T(8,128)(2,1)S(1)}) custom-call(s32[3]{0:T(128)S(1)} %pad_add_fusion.1.idx, bf16[2,2,2,128,1024]{4,3,2,1,0:T(8,128)(2,1)} %bitcast.229, bf16[1024,512]{1,0:T(8,128)(2,1)S(1)} %copy-done.8, bf16[2,2,2,128,128]{4,3,2,1,0:T(8,128)(2,1)S(1)} %bitcast.170, ...), custom_call_target="tpu_custom_call" | custom-call | flops 3489660928 | bytes 10485760 | tf_op jit(solution)/shard_map/weight_grads/pallas_call | solution.py:723
  313.6 8.6 %add_convert_fusion = bf16[1024,1024]{1,0:T(8,128)(2,1)} fusion(f32[1024,1024]{1,0:T(8,128)} %fusion.69, bf16[1024,2048]{1,0:T(8,128)(2,1)} %get-tuple-element.95, bf16[2048,1024]{1,0:T(8,128)(2,1)S(1)} %copy-done.35), kind=kOutput, calls=%fused_computation.2 | convolution fusion | flops 4297064448 | bytes 14680064 | tf_op jit(solution)/shard_map/dot_general | solution.py:43
  322.2 8.3 %input_grads.5 = (bf16[1024,1024]{1,0:T(8,128)(2,1)}, f32[8,1024]{1,0:T(8,128)S(1)}, f32[8,1536]{1,0:T(8,128)S(1)}) custom-call(bf16[1024,1024]{1,0:T(8,128)(2,1)} %pad_maximum_fusion.1.x_ref.refs_0_, f32[1,1024]{1,0:T(1,128)S(1)} %bitcast.180, bf16[1024,1536]{1,0:T(8,128)(2,1)} %maximum_select_fusion.1.w_ref.refs_2_, bf16[1024,512]{1,0:T(8,128)(2,1)S(1)} %copy-done.8, ...), custom_call_target="tpu_custom_call" | custom-call | flops 3221225472 | bytes 12582912 | tf_op jit(solution)/shard_map/input_grads/pallas_call | solution.py:778
  335.6 5.8 collective-permute-done.18
  352.6 14.9 %collective-permute-done.35 = bf16[2,2,256,512]{3,2,1,0:T(8,128)(2,1)S(1)} collective-permute-done((bf16[2,2,256,512]{3,2,1,0:T(8,128)(2,1)S(1)}, bf16[2,2,256,512]{3,2,1,0:T(8,128)(2,1)S(1)}, u32[]{:S(2)}, u32[]{:S(2)}) %collective-permute-start.35) | collective-permute-done | bytes 1048608 | tf_op jit(solution)/shard_map/ppermute | solution.py:55
  368.2 12.7 %collective-permute-done.42 = bf16[2,256,512]{2,1,0:T(8,128)(2,1)S(1)} collective-permute-done((bf16[2,256,512]{2,1,0:T(8,128)(2,1)S(1)}, bf16[2,256,512]{2,1,0:T(8,128)(2,1)S(1)}, u32[]{:S(2)}, u32[]{:S(2)}) %collective-permute-start.42) | collective-permute-done | bytes 524320 | tf_op jit(solution)/shard_map/ppermute | solution.py:55
  382.7 18.5 %collective-permute-done.39 = bf16[2,256,512]{2,1,0:T(8,128)(2,1)S(1)} collective-permute-done((bf16[2,256,512]{2,1,0:T(8,128)(2,1)S(1)}, bf16[2,256,512]{2,1,0:T(8,128)(2,1)S(1)}, u32[]{:S(2)}, u32[]{:S(2)}) %collective-permute-start.39) | collective-permute-done | bytes 524320 | tf_op jit(solution)/shard_map/ppermute | solution.py:55
  403.2 8.0 %collective-permute-done.33 = bf16[2,256,512]{2,1,0:T(8,128)(2,1)S(1)} collective-permute-done((bf16[2,256,512]{2,1,0:T(8,128)(2,1)S(1)}, bf16[2,256,512]{2,1,0:T(8,128)(2,1)S(1)}, u32[]{:S(2)}, u32[]{:S(2)}) %collective-permute-start.33) | collective-permute-done | bytes 524320 | tf_op jit(solution)/shard_map/ppermute | solution.py:55
  414.4 9.4 %collective-permute-done.36 = bf16[2,256,512]{2,1,0:T(8,128)(2,1)S(1)} collective-permute-done((bf16[2,256,512]{2,1,0:T(8,128)(2,1)S(1)}, bf16[2,256,512]{2,1,0:T(8,128)(2,1)S(1)}, u32[]{:S(2)}, u32[]{:S(2)}) %collective-permute-start.36) | collective-permute-done | bytes 524320 | tf_op jit(solution)/shard_map/ppermute | solution.py:55
  435.8 27.6 %collective-permute-done.19 = bf16[64,1024]{1,0:T(8,128)(2,1)} collective-permute-done((bf16[64,1024]{1,0:T(8,128)(2,1)}, bf16[64,1024]{1,0:T(8,128)(2,1)}, u32[]{:S(2)}, u32[]{:S(2)}) %collective-permute-start.19) | collective-permute-done | bytes 131104 | tf_op jit(solution)/shard_map/ppermute | solution.py:55
  479.5 37.0 %all-reduce.9.cloned.1.call-done.refs_0_ = bf16[512,512]{1,0:T(8,128)(2,1)} async-done(((bf16[512,512]{1,0:T(8,128)(2,1)}), bf16[512,512]{1,0:T(8,128)(2,1)}) %all-reduce.9.cloned.1.call-update) | async-done | bytes 524304 | tf_op jit(solution)/shard_map/psum | solution.py:1012
  522.7 35.0 %all-reduce.11.cloned.1.call-done.refs_0_ = bf16[512,512]{1,0:T(8,128)(2,1)} async-done(((bf16[512,512]{1,0:T(8,128)(2,1)}), bf16[512,512]{1,0:T(8,128)(2,1)}) %all-reduce.11.cloned.1.call-update) | async-done | bytes 524304 | tf_op jit(solution)/shard_map/psum | solution.py:1012
  568.2 30.6 %all-reduce.13.cloned.1.call-done.refs_0_ = bf16[512,512]{1,0:T(8,128)(2,1)} async-done(((bf16[512,512]{1,0:T(8,128)(2,1)}), bf16[512,512]{1,0:T(8,128)(2,1)}) %all-reduce.13.cloned.1.call-update) | async-done | bytes 524304 | tf_op jit(solution)/shard_map/psum | solution.py:1012
  605.7 34.1 %all-reduce.15.cloned.1.call-done.refs_0_ = bf16[512,512]{1,0:T(8,128)(2,1)} async-done(((bf16[512,512]{1,0:T(8,128)(2,1)}), bf16[512,512]{1,0:T(8,128)(2,1)}) %all-reduce.15.cloned.1.call-update) | async-done | bytes 524304 | tf_op jit(solution)/shard_map/psum | solution.py:1012
  646.1 8.7 %collective-permute-done.57.refs_2_ = bf16[512,512]{1,0:T(8,128)(2,1)} collective-permute-done((bf16[512,512]{1,0:T(8,128)(2,1)S(1)}, bf16[512,512]{1,0:T(8,128)(2,1)}, u32[]{:S(2)}, u32[]{:S(2)}) %collective-permute-start.57) | collective-permute-done | bytes 524320 | tf_op jit(solution)/shard_map/ppermute | solution.py:55
  656.3 9.8 %collective-permute-done.58.refs_3_ = bf16[512,512]{1,0:T(8,128)(2,1)} collective-permute-done((bf16[512,512]{1,0:T(8,128)(2,1)}, bf16[512,512]{1,0:T(8,128)(2,1)}, u32[]{:S(2)}, u32[]{:S(2)}) %collective-permute-start.58) | collective-permute-done | bytes 524320 | tf_op jit(solution)/shard_map/ppermute | solution.py:55
  668.1 14.3 %all-reduce.17.cloned.1.call-done = bf16[512,512]{1,0:T(8,128)(2,1)} async-done(((bf16[512,512]{1,0:T(8,128)(2,1)}), bf16[512,512]{1,0:T(8,128)(2,1)}) %all-reduce.17.cloned.1.call-update) | async-done | bytes 524304 | tf_op jit(solution)/shard_map/psum | solution.py:1012
  717.8 8.8 %collective-permute-done.49.refs_3_ = bf16[512,512]{1,0:T(8,128)(2,1)S(1)} collective-permute-done((bf16[512,512]{1,0:T(8,128)(2,1)}, bf16[512,512]{1,0:T(8,128)(2,1)S(1)}, u32[]{:S(2)}, u32[]{:S(2)}) %collective-permute-start.49) | collective-permute-done | bytes 524320 | tf_op jit(solution)/shard_map/ppermute | solution.py:55
  (408 shorter events, 257.7 us)
Async XLA Ops:
  7.2 468.6 %all-reduce.7.cloned.1.call-start = ((), (), s32[]{:S(2)}) async-start(), calls=%async_computation | async-start | bytes 1048576 | tf_op jit(solution)/shard_map/psum | solution.py:1012
  7.3 77.1 %collective-permute-start = (bf16[512,1024]{1,0:T(8,128)(2,1)}, bf16[512,1024]{1,0:T(8,128)(2,1)}, u32[]{:S(2)}, u32[]{:S(2)}) collective-permute-start(bf16[512,1024]{1,0:T(8,128)(2,1)} %bitcast.188), channel_id=1, source_target_pairs={{0,1},{1,0},{2,3},{3,2},{4,5},{5,4},{6,7},{7,6},{8,9},{9,8},{10,11... | collective-permute-start | bytes 3145736 | tf_op jit(solution)/shard_map/ppermute | solution.py:51
  7.8 76.1 %collective-permute-start.4 = (bf16[512,1024]{1,0:T(8,128)(2,1)}, bf16[512,1024]{1,0:T(8,128)(2,1)}, u32[]{:S(2)}, u32[]{:S(2)}) collective-permute-start(bf16[512,1024]{1,0:T(8,128)(2,1)} %bitcast.189), channel_id=1, source_target_pairs={{0,2},{2,4},{4,6},{1,3},{3,5},{5,7},{8,10},{10,12},{12,14},{9,11},... | collective-permute-start | bytes 3145736 | tf_op jit(solution)/shard_map/ppermute | solution.py:60
  13.4 52.4 %collective-permute-start.10 = (s32[64]{0:T(128)}, s32[64]{0:T(128)S(1)}, u32[]{:S(2)}, u32[]{:S(2)}) collective-permute-start(s32[64]{0:T(128)} %bitcast.220), channel_id=1, source_target_pairs={{0,1},{1,0},{2,3},{3,2},{4,5},{5,4},{6,7},{7,6},{8,9},{9,8},{10,11... | collective-permute-start | bytes 776 | tf_op jit(solution)/shard_map/ppermute | solution.py:51
  18.4 51.0 %collective-permute-start.1 = (bf16[9,512]{1,0:T(8,128)(2,1)S(1)}, bf16[9,512]{1,0:T(8,128)(2,1)S(1)}, u32[]{:S(2)}, u32[]{:S(2)}) collective-permute-start(bf16[9,512]{1,0:T(8,128)(2,1)S(1)} %concatenate.109), channel_id=1, source_target_pairs={{0,1},{1,0},{2,3},{3,2},{4,5},{5,4},{6,7},{7,6},{8,9},{9,8},{10,11... | collective-permute-start | bytes 27656 | tf_op jit(solution)/shard_map/ppermute | solution.py:51
  22.7 47.0 %collective-permute-start.6 = (bf16[1,2,16,1024]{3,2,1,0:T(8,128)(2,1)S(1)}, bf16[1,2,16,1024]{3,2,1,0:T(8,128)(2,1)S(1)}, u32[]{:S(2)}, u32[]{:S(2)}) collective-permute-start(bf16[1,2,16,1024]{3,2,1,0:T(8,128)(2,1)S(1)} %pad_maximum_fusion.21), channel_id=1, source_target_pairs={{0,2},{2,0},{4,6},{6,4},{1,3},{3,1},{5,7},{7,5},{8,10},{10,8},{12,... | collective-permute-start | bytes 196616 | tf_op jit(solution)/shard_map/ppermute | solution.py:55
  83.2 116.6 %collective-permute-start.3 = (bf16[512,2048]{1,0:T(8,128)(2,1)}, bf16[512,2048]{1,0:T(8,128)(2,1)}, u32[]{:S(2)}, u32[]{:S(2)}) collective-permute-start(bf16[512,2048]{1,0:T(8,128)(2,1)} %bitcast.199), channel_id=1, source_target_pairs={{0,1},{1,0},{2,3},{3,2},{4,5},{5,4},{6,7},{7,6},{8,9},{9,8},{10,11... | collective-permute-start | bytes 6291464 | tf_op jit(solution)/shard_map/ppermute | solution.py:51
  141.0 121.9 %collective-permute-start.11 = (f32[8,72,128]{2,1,0:T(8,128)S(1)}, f32[8,72,128]{2,1,0:T(8,128)S(1)}, u32[]{:S(2)}, u32[]{:S(2)}) collective-permute-start(f32[8,72,128]{2,1,0:T(8,128)S(1)} %glob_first.1), channel_id=1, source_target_pairs={{0,2},{2,0},{4,6},{6,4},{1,3},{3,1},{5,7},{7,5},{8,10},{10,8},{12,... | collective-permute-start | bytes 884744 | tf_op jit(solution)/shard_map/ppermute | solution.py:55
  199.7 147.5 %collective-permute-start.15 = (bf16[512,1024]{1,0:T(8,128)(2,1)}, bf16[512,1024]{1,0:T(8,128)(2,1)}, u32[]{:S(2)}, u32[]{:S(2)}) collective-permute-start(bf16[512,1024]{1,0:T(8,128)(2,1)} %slice.317), channel_id=1, source_target_pairs={{0,1},{1,0},{2,3},{3,2},{4,5},{5,4},{6,7},{7,6},{8,9},{9,8},{10,11... | collective-permute-start | bytes 3145736 | tf_op jit(solution)/shard_map/ppermute | solution.py:51
  218.7 124.0 %collective-permute-start.41 = (bf16[2,2,256,512]{3,2,1,0:T(8,128)(2,1)}, bf16[2,2,256,512]{3,2,1,0:T(8,128)(2,1)}, u32[]{:S(2)}, u32[]{:S(2)}) collective-permute-start(bf16[2,2,256,512]{3,2,1,0:T(8,128)(2,1)} %get-tuple-element.144), channel_id=1, source_target_pairs={{0,8},{8,0},{16,24},{24,16},{1,9},{9,1},{17,25},{25,17},{2,10},{10... | collective-permute-start | bytes 3145736 | tf_op jit(solution)/shard_map/ppermute | solution.py:55
  233.7 111.7 %collective-permute-start.38 = (bf16[2,2,256,512]{3,2,1,0:T(8,128)(2,1)}, bf16[2,2,256,512]{3,2,1,0:T(8,128)(2,1)}, u32[]{:S(2)}, u32[]{:S(2)}) collective-permute-start(bf16[2,2,256,512]{3,2,1,0:T(8,128)(2,1)} %get-tuple-element.142), channel_id=1, source_target_pairs={{0,16},{8,24},{16,0},{24,8},{1,17},{9,25},{17,1},{25,9},{2,18},{10... | collective-permute-start | bytes 3145736 | tf_op jit(solution)/shard_map/ppermute | solution.py:55
  275.2 74.7 %collective-permute-start.32 = (bf16[2,2,256,512]{3,2,1,0:T(8,128)(2,1)}, bf16[2,2,256,512]{3,2,1,0:T(8,128)(2,1)}, u32[]{:S(2)}, u32[]{:S(2)}) collective-permute-start(bf16[2,2,256,512]{3,2,1,0:T(8,128)(2,1)} %get-tuple-element.138), channel_id=1, source_target_pairs={{0,16},{8,24},{16,0},{24,8},{1,17},{9,25},{17,1},{25,9},{2,18},{10... | collective-permute-start | bytes 3145736 | tf_op jit(solution)/shard_map/ppermute | solution.py:55
  293.2 42.2 %collective-permute-start.17 = (bf16[64,1024]{1,0:T(8,128)(2,1)S(1)}, bf16[64,1024]{1,0:T(8,128)(2,1)S(1)}, u32[]{:S(2)}, u32[]{:S(2)}) collective-permute-start(bf16[64,1024]{1,0:T(8,128)(2,1)S(1)} %slice.319), channel_id=1, source_target_pairs={{0,1},{1,0},{2,3},{3,2},{4,5},{5,4},{6,7},{7,6},{8,9},{9,8},{10,11... | collective-permute-start | bytes 393224 | tf_op jit(solution)/shard_map/ppermute | solution.py:51
  342.7 84.1 %collective-permute-start.29 = (bf16[2,2,256,512]{3,2,1,0:T(8,128)(2,1)S(1)}, bf16[2,2,256,512]{3,2,1,0:T(8,128)(2,1)S(1)}, u32[]{:S(2)}, u32[]{:S(2)}) collective-permute-start(bf16[2,2,256,512]{3,2,1,0:T(8,128)(2,1)S(1)} %copy-done.30), channel_id=1, source_target_pairs={{0,8},{8,0},{16,24},{24,16},{1,9},{9,1},{17,25},{25,17},{2,10},{10... | collective-permute-start | bytes 3145736 | tf_op jit(solution)/shard_map/ppermute | solution.py:55
  345.4 82.5 %collective-permute-start.25 = (bf16[2,2,256,512]{3,2,1,0:T(8,128)(2,1)S(1)}, bf16[2,2,256,512]{3,2,1,0:T(8,128)(2,1)S(1)}, u32[]{:S(2)}, u32[]{:S(2)}) collective-permute-start(bf16[2,2,256,512]{3,2,1,0:T(8,128)(2,1)S(1)} %copy-done.28), channel_id=1, source_target_pairs={{0,16},{8,24},{16,0},{24,8},{1,17},{9,25},{17,1},{25,9},{2,18},{10... | collective-permute-start | bytes 3145736 | tf_op jit(solution)/shard_map/ppermute | solution.py:55
  347.2 120.4 %collective-permute-start.13 = (bf16[512,1024]{1,0:T(8,128)(2,1)}, bf16[512,1024]{1,0:T(8,128)(2,1)}, u32[]{:S(2)}, u32[]{:S(2)}) collective-permute-start(bf16[512,1024]{1,0:T(8,128)(2,1)} %slice.409), channel_id=1, source_target_pairs={{0,1},{1,0},{2,3},{3,2},{4,5},{5,4},{6,7},{7,6},{8,9},{9,8},{10,11... | collective-permute-start | bytes 3145736 | tf_op jit(solution)/shard_map/ppermute | solution.py:51
  401.2 62.2 %collective-permute-start.14 = (bf16[512,1024]{1,0:T(8,128)(2,1)}, bf16[512,1024]{1,0:T(8,128)(2,1)}, u32[]{:S(2)}, u32[]{:S(2)}) collective-permute-start(bf16[512,1024]{1,0:T(8,128)(2,1)} %slice.315), channel_id=1, source_target_pairs={{0,1},{1,0},{2,3},{3,2},{4,5},{5,4},{6,7},{7,6},{8,9},{9,8},{10,11... | collective-permute-start | bytes 3145736 | tf_op jit(solution)/shard_map/ppermute | solution.py:51
  433.4 83.0 %all-reduce.9.cloned.1.call-start = ((), (), s32[]{:S(2)}) async-start(), calls=%async_computation.1 | async-start | bytes 1048576 | tf_op jit(solution)/shard_map/psum | solution.py:1012
  433.8 82.8 %collective-permute-start.34 = (bf16[128,512]{1,0:T(8,128)(2,1)}, bf16[128,512]{1,0:T(8,128)(2,1)}, u32[]{:S(2)}, u32[]{:S(2)}) collective-permute-start(bf16[128,512]{1,0:T(8,128)(2,1)} %get-tuple-element.192), channel_id=1, source_target_pairs={{0,1},{1,0},{2,3},{3,2},{4,5},{5,4},{6,7},{7,6},{8,9},{9,8},{10,11... | collective-permute-start | bytes 393224 | tf_op jit(solution)/shard_map/ppermute | solution.py:51
  463.4 56.4 %collective-permute-start.30 = (bf16[2,256,512]{2,1,0:T(8,128)(2,1)}, bf16[2,256,512]{2,1,0:T(8,128)(2,1)}, u32[]{:S(2)}, u32[]{:S(2)}) collective-permute-start(bf16[2,256,512]{2,1,0:T(8,128)(2,1)} %fusion.26), channel_id=1, source_target_pairs={{0,16},{8,24},{16,0},{24,8},{1,17},{9,25},{17,1},{25,9},{2,18},{10... | collective-permute-start | bytes 1572872 | tf_op jit(solution)/shard_map/ppermute | solution.py:55
  464.0 93.8 %collective-permute-start.26 = (bf16[2,256,512]{2,1,0:T(8,128)(2,1)}, bf16[2,256,512]{2,1,0:T(8,128)(2,1)}, u32[]{:S(2)}, u32[]{:S(2)}) collective-permute-start(bf16[2,256,512]{2,1,0:T(8,128)(2,1)} %fusion.25), channel_id=1, source_target_pairs={{0,8},{8,0},{16,24},{24,16},{1,9},{9,1},{17,25},{25,17},{2,10},{10... | collective-permute-start | bytes 1572872 | tf_op jit(solution)/shard_map/ppermute | solution.py:55
  475.9 81.8 %all-reduce.11.cloned.1.call-start = ((), (), s32[]{:S(2)}) async-start(), calls=%async_computation.2 | async-start | bytes 1048576 | tf_op jit(solution)/shard_map/psum | solution.py:1012
  516.5 82.3 %all-reduce.13.cloned.1.call-start = ((), (), s32[]{:S(2)}) async-start(), calls=%async_computation.3 | async-start | bytes 1048576 | tf_op jit(solution)/shard_map/psum | solution.py:1012
  518.3 41.8 %collective-permute-start.22 = (f32[12,512]{1,0:T(8,128)S(1)}, f32[12,512]{1,0:T(8,128)S(1)}, u32[]{:S(2)}, u32[]{:S(2)}) collective-permute-start(f32[12,512]{1,0:T(8,128)S(1)} %add.352), channel_id=1, source_target_pairs={{0,16},{8,24},{16,0},{24,8},{1,17},{9,25},{17,1},{25,9},{2,18},{10... | collective-permute-start | bytes 73736 | tf_op jit(solution)/shard_map/ppermute | solution.py:55
  522.1 43.1 %collective-permute-start.59 = (bf16[512,512]{1,0:T(8,128)(2,1)S(1)}, bf16[512,512]{1,0:T(8,128)(2,1)S(1)}, u32[]{:S(2)}, u32[]{:S(2)}) collective-permute-start(bf16[512,512]{1,0:T(8,128)(2,1)S(1)} %copy-done.20), channel_id=1, source_target_pairs={{0,16},{8,24},{16,0},{24,8},{1,17},{9,25},{17,1},{25,9},{2,18},{10... | collective-permute-start | bytes 1572872 | tf_op jit(solution)/shard_map/ppermute | solution.py:55
  557.7 82.1 %all-reduce.15.cloned.1.call-start = ((), (), s32[]{:S(2)}) async-start(), calls=%async_computation.4 | async-start | bytes 1048576 | tf_op jit(solution)/shard_map/psum | solution.py:1012
  561.4 80.4 %collective-permute-start.60 = (bf16[512,512]{1,0:T(8,128)(2,1)S(1)}, bf16[512,512]{1,0:T(8,128)(2,1)S(1)}, u32[]{:S(2)}, u32[]{:S(2)}) collective-permute-start(bf16[512,512]{1,0:T(8,128)(2,1)S(1)} %copy-done.20), channel_id=1, source_target_pairs={{0,8},{8,0},{16,24},{24,16},{1,9},{9,1},{17,25},{25,17},{2,10},{10... | collective-permute-start | bytes 1572872 | tf_op jit(solution)/shard_map/ppermute | solution.py:55
  564.7 76.6 %collective-permute-start.56 = (bf16[512,512]{1,0:T(8,128)(2,1)S(1)}, bf16[512,512]{1,0:T(8,128)(2,1)}, u32[]{:S(2)}, u32[]{:S(2)}) collective-permute-start(bf16[512,512]{1,0:T(8,128)(2,1)S(1)} %copy-done.21), channel_id=1, source_target_pairs={{0,8},{8,0},{16,24},{24,16},{1,9},{9,1},{17,25},{25,17},{2,10},{10... | collective-permute-start | bytes 1572872 | tf_op jit(solution)/shard_map/ppermute | solution.py:55
  565.2 78.1 %collective-permute-start.61 = (bf16[512,512]{1,0:T(8,128)(2,1)S(1)}, bf16[512,512]{1,0:T(8,128)(2,1)}, u32[]{:S(2)}, u32[]{:S(2)}) collective-permute-start(bf16[512,512]{1,0:T(8,128)(2,1)S(1)} %collective-permute-done.59.refs_1_), channel_id=1, source_target_pairs={{0,8},{8,0},{16,24},{24,16},{1,9},{9,1},{17,25},{25,17},{2,10},{10... | collective-permute-start | bytes 1572872 | tf_op jit(solution)/shard_map/ppermute | solution.py:55
  566.7 77.2 %collective-permute-start.53 = (bf16[512,512]{1,0:T(8,128)(2,1)S(1)}, bf16[512,512]{1,0:T(8,128)(2,1)}, u32[]{:S(2)}, u32[]{:S(2)}) collective-permute-start(bf16[512,512]{1,0:T(8,128)(2,1)S(1)} %copy-done.22), channel_id=1, source_target_pairs={{0,16},{8,24},{16,0},{24,8},{1,17},{9,25},{17,1},{25,9},{2,18},{10... | collective-permute-start | bytes 1572872 | tf_op jit(solution)/shard_map/ppermute | solution.py:55
  598.8 83.5 %all-reduce.17.cloned.1.call-start = ((), (), s32[]{:S(2)}) async-start(), calls=%async_computation.5 | async-start | bytes 1048576 | tf_op jit(solution)/shard_map/psum | solution.py:1012
  654.8 48.0 %collective-permute-start.51 = (bf16[512,512]{1,0:T(8,128)(2,1)S(1)}, bf16[512,512]{1,0:T(8,128)(2,1)}, u32[]{:S(2)}, u32[]{:S(2)}) collective-permute-start(bf16[512,512]{1,0:T(8,128)(2,1)S(1)} %copy-done.23), channel_id=1, source_target_pairs={{0,16},{8,24},{16,0},{24,8},{1,17},{9,25},{17,1},{25,9},{2,18},{10... | collective-permute-start | bytes 1572872 | tf_op jit(solution)/shard_map/ppermute | solution.py:55
  (97 other events, 1629.6 us)
Sparse Core Ops, SparseCore 0:
  433.6 42.2 all-reduce.6
  478.2 38.2 all-reduce.8
  519.4 38.2 all-reduce.10
  560.5 38.2 all-reduce.12
  601.5 38.2 all-reduce.14
  644.0 38.2 all-reduce.16

commit v2 on v1

v2 whole, which is shorter than its diff:
```python
import functools
import math

import jax
import jax.numpy as jnp
from jax import lax
from jax.experimental import pallas as pl
from jax.experimental.pallas import tpu as pltpu
from jax.sharding import PartitionSpec as P

D = 1024
H = 16
HD = 64
ROT = 16
WIN = 512
FF = 4096
HALF = D // 2
PAIR = 2 * HD
ROW = 512
TILE = 128

epsilon = 1e-05
negative = -1e30
rotary_base = 10000.0
f32 = jnp.float32
bf16 = jnp.bfloat16
VMEM = 60 * 2**20
KINDS = ("xy", "yx")
COST = 1000


def shape(dims, dtype):
    return jax.ShapeDtypeStruct(dims, dtype)


def params():
    return pltpu.CompilerParams(vmem_limit_bytes=VMEM)


def cost(flops, moved):
    return pl.CostEstimate(flops=int(flops) // COST, bytes_accessed=int(moved) // COST, transcendentals=0)


def dot(left, right):
    return jnp.dot(left, right, preferred_element_type=f32)


def dot_nt(left, right):
    return lax.dot_general(left, right, (((1,), (1,)), ((), ())), preferred_element_type=f32)


def dot_tn(left, right):
    return lax.dot_general(left, right, (((0,), (0,)), ((), ())), preferred_element_type=f32)


def lanes_of(block, width):
    return pl.ds(pl.multiple_of(block * width, width), width)


def pair(block):
    return lax.ppermute(block, "fsdp", [(0, 1), (1, 0)])


def exchange(block, axis, distance):
    return lax.ppermute(block, axis, [(i, i ^ distance) for i in range(lax.axis_size(axis))])


def shifted(block, distance):
    devices = range(lax.axis_size("ctx"))
    return lax.ppermute(
        block, "ctx", [(i - distance, i) for i in devices if i - distance in devices]
    )


def doubling(axis):
    distance, out = 1, []
    while distance < lax.axis_size(axis):
        out.append(distance)
        distance *= 2
    return out


def first_axis(kind):
    distance = 1 if kind == "xy" else 2
    return lambda block: exchange(block, "seq", distance)


def second_axis(kind):
    distance = 2 if kind == "xy" else 1
    return lambda block: exchange(block, "seq", distance)


def added(*parts):
    total = parts[0].astype(f32)
    for part in parts[1:]:
        total = total + part.astype(f32)
    return total.astype(bf16)


class Order:
    def __init__(self):
        self.token = None

    def gate(self, *arrays):
        if self.token is None:
            return arrays if len(arrays) > 1 else arrays[0]
        out = lax.optimization_barrier((*arrays, self.token))[:-1]
        return out if len(out) > 1 else out[0]

    def mark(self, array):
        self.token = array
        return array


class Reduction:
    def __init__(self, order, idx, parts):
        self.order, self.idx = order, idx
        self.tiles = parts[0][0].shape[1]
        self.keeps = [keep for _, keep in parts]
        self.recv = [first_axis(kind)(send) for kind, (send, _) in zip(KINDS, parts)]

    def second(self):
        gated = self.order.gate(*self.keeps, *self.recv)
        self.keeps, self.recv = gated[:2], gated[2:]
        sums = halves_call(*self.keeps, *self.recv)
        self.order.mark(sums[0])
        self.other = [second_axis(kind)(part) for kind, part in zip(KINDS, sums)]

    def over_ctx(self):
        gated = self.order.gate(*self.keeps, *self.recv, *self.other)
        outs = quarters_call(self.idx, *gated)
        self.order.mark(outs[0])
        if len(outs) == 2:
            self.total = lax.psum(tuple(outs), "ctx")
            return
        self.own = outs[0]
        self.recv = [exchange(part, "ctx", k + 1) for k, part in enumerate(outs[1:])]

    def ctx_sum(self):
        if lax.axis_size("ctx") != 4:
            return
        self.own = self.order.mark(added(*self.order.gate(self.own, *self.recv)))
        self.recv = [exchange(self.own, "ctx", k) for k in (1, 2, 3)]

    def gather(self):
        if lax.axis_size("ctx") != 4:
            total = self.order.gate(*self.total)
        else:
            total = regroup_call(self.idx, *self.order.gate(self.own, *self.recv))
            self.order.mark(total[0])
        self.total = [part.reshape(self.tiles, 256, 512) for part in total]
        self.beside = [second_axis(k)(part) for k, part in zip(KINDS, self.total)]
        self.across = [first_axis(k)(part) for k, part in zip(KINDS, self.total)]

    def gather_rest(self):
        self.beside = self.order.gate(*self.beside)
        self.order.mark(self.beside[0])
        self.both = [first_axis(k)(beside) for k, beside in zip(KINDS, self.beside)]

    def swap(self, tiles):
        pieces = [
            [self.total[u], self.beside[u], self.across[u], self.both[u]] for u in range(2)
        ]
        flat = self.order.gate(*pieces[0], *pieces[1])
        self.pieces = [flat[:4], flat[4:]]
        given = swap_call([(self.pieces[u][k], t) for u, t in tiles for k in range(4)])
        self.swapped = pair(self.order.mark(given))


def halves_body(keep_a, keep_b, recv_a, recv_b, out_a, out_b):
    for keep, recv, out in ((keep_a, recv_a, out_a), (keep_b, recv_b, out_b)):
        out[...] = (keep[0].astype(f32) + recv[0].astype(f32)).astype(bf16)


def halves_call(keep_a, keep_b, recv_a, recv_b):
    tiles = keep_a.shape[1]
    block = pl.BlockSpec((1, 1, 256, 512), lambda t: (0, t, 0, 0))
    out = pl.BlockSpec((1, 256, 512), lambda t: (t, 0, 0))
    return pl.pallas_call(
        halves_body,
        grid=(tiles,),
        in_specs=[block] * 4,
        out_specs=[out] * 2,
        out_shape=[shape((tiles, 256, 512), bf16)] * 2,
        compiler_params=params(),
        cost_estimate=cost(10**6, 3 * 2**20),
        name="halves",
    )(keep_a, keep_b, recv_a, recv_b)


def quarters_body(idx, keep_a, keep_b, recv_a, recv_b, other_a, other_b, *outs):
    for u, refs in enumerate(((keep_a, recv_a, other_a), (keep_b, recv_b, other_b))):
        keep, recv, other = refs
        total = keep[0, 0].astype(f32) + recv[0, 0].astype(f32) + other[0].astype(f32)
        total = total.astype(bf16)
        if len(outs) == 2:
            outs[u][0] = total
            continue
        for k, out in enumerate(outs):

            @pl.when(pl.program_id(0) == k)
            def _(out=out, total=total):
                out[u] = total


def quarters_call(idx, keep_a, keep_b, recv_a, recv_b, other_a, other_b):
    split = lax.axis_size("ctx") == 4
    rows = keep_a.shape[1] * 256 // 4
    order = (lambda k, idx: idx[3] ^ k) if split else (lambda k, idx: k)
    block = pl.BlockSpec((1, 1, rows, 512), lambda k, idx: (1, order(k, idx), 0, 0))
    other = pl.BlockSpec((1, rows, 512), lambda k, idx: (order(k, idx), 0, 0))
    if split:
        out_specs = [pl.BlockSpec((2, rows, 512), lambda k, idx: (0, 0, 0))] * 4
        out_shape = [shape((2, rows, 512), bf16)] * 4
    else:
        out_specs, out_shape = [other] * 2, [shape((4, rows, 512), bf16)] * 2
    views = [v.reshape(2, 4, rows, 512) for v in (keep_a, keep_b, recv_a, recv_b)]
    views += [v.reshape(4, rows, 512) for v in (other_a, other_b)]
    return pl.pallas_call(
        quarters_body,
        grid_spec=pltpu.PrefetchScalarGridSpec(
            num_scalar_prefetch=1,
            grid=(4,),
            in_specs=[block] * 4 + [other] * 2,
            out_specs=out_specs,
        ),
        out_shape=out_shape,
        compiler_params=params(),
        cost_estimate=cost(10**6, 4 * 2**20),
        name="quarters",
    )(idx, *views)


def regroup_body(idx, *refs):
    for k in range(4):

        @pl.when(pl.program_id(0) == k)
        def _(k=k):
            for u in range(2):
                refs[4 + u][0] = refs[k][u]


def regroup_call(idx, *parts):
    rows = parts[0].shape[1]
    return pl.pallas_call(
        regroup_body,
        grid_spec=pltpu.PrefetchScalarGridSpec(
            num_scalar_prefetch=1,
            grid=(4,),
            in_specs=[pl.BlockSpec((2, rows, 512), lambda k, idx: (0, 0, 0))] * 4,
            out_specs=[pl.BlockSpec((1, rows, 512), lambda k, idx: (idx[3] ^ k, 0, 0))] * 2,
        ),
        out_shape=[shape((4, rows, 512), bf16)] * 2,
        compiler_params=params(),
        cost_estimate=cost(10**6, 2 * 2**20),
        name="regroup",
    )(idx, *parts)


def swap_body(*refs):
    for k, ref in enumerate(refs[:-1]):
        refs[-1][k] = ref[0]


def swap_call(blocks):
    return pl.pallas_call(
        swap_body,
        grid=(1,),
        in_specs=[
            pl.BlockSpec((1, TILE, 512), lambda i, t=t: (t, 0, 0)) for _, t in blocks
        ],
        out_specs=pl.BlockSpec((len(blocks), TILE, 512), lambda i: (0, 0, 0)),
        out_shape=shape((len(blocks), TILE, 512), bf16),
        compiler_params=params(),
        cost_estimate=cost(10**6, 2 * 2**20),
        name="swap",
    )(*[piece for piece, _ in blocks])


def norm_parts(x):
    center = x - jnp.mean(x, axis=-1, keepdims=True)
    inverse = lax.rsqrt(jnp.mean(center * center, axis=-1, keepdims=True) + epsilon)
    return center * inverse, inverse


def vector(ref, i):
    part = slice(i * HALF, (i + 1) * HALF)
    return jnp.concatenate([ref[0:1, part], ref[1:2, part]], axis=1)


def norm_body(x_ref, other_ref, dy_ref, dy_other_ref, vec_ref, *outs):
    a_ref, x_out, dy_out = outs

    def run(x_in, dy_in):
        block = x_in[...]
        normal, _ = norm_parts(block.astype(f32))
        a = (normal * vector(vec_ref, 2) + vector(vec_ref, 3)).astype(bf16)
        a_ref[...] = a
        x_out[...] = block
        dy_out[...] = dy_in[...]

    half = pl.num_programs(0) // 2

    @pl.when(pl.program_id(0) < half)
    def _():
        run(x_ref, dy_ref)

    @pl.when(pl.program_id(0) >= half)
    def _():
        run(other_ref, dy_other_ref)


def norm_call(x, other, dy, dy_other, vectors):
    rows, step = 2 * x.shape[0], 256
    half = x.shape[0] // step
    mine = pl.BlockSpec((step, D), lambda i: (jnp.minimum(i, half - 1), 0))
    theirs = pl.BlockSpec((step, D), lambda i: (jnp.maximum(i - half, 0), 0))
    block = pl.BlockSpec((step, D), lambda i: (i, 0))
    return pl.pallas_call(
        norm_body,
        grid=(rows // step,),
        in_specs=[mine, theirs, mine, theirs, pl.BlockSpec(vectors.shape, lambda i: (0, 0))],
        out_specs=[block] * 3,
        out_shape=[shape((rows, D), bf16)] * 3,
        compiler_params=params(),
        cost_estimate=cost(rows * D * 10, rows * D * 12),
        name="norm",
    )(x, other, dy, dy_other, vectors)


def rows_of(core):
    return pl.ds(pl.multiple_of(core * HALF, HALF), HALF)


def place_of(bit, value):
    return jnp.where(bit == value, 1, 0)


def spread_rows(ref, tile, grad, m, core, two, lanes):
    at = pl.ds(pl.multiple_of(jnp.where(core == m, TILE, 0), TILE), TILE)
    for r in range(2):
        ref[place_of(two, r), tile, at, lanes] = grad[r * TILE : (r + 1) * TILE]


def unit_body(n_alias, idx, a_ref, dy_ref, wu_mine, wu_recv, wd_ref, bu_ref, *rest):
    sends, keeps = rest[n_alias : n_alias + 4 : 2], rest[n_alias + 1 : n_alias + 4 : 2]
    act_ref, dup_ref, bias_ref, wu_ref = rest[n_alias + 4 :]
    core = idx[0]
    wu_ref[rows_of(core), :] = wu_mine[...]
    wu_ref[rows_of(1 - core), :] = wu_recv[...]
    rows = a_ref.shape[0]
    chunk = 256
    bias = jnp.zeros((1, chunk), f32)
    for i in range(rows // chunk):
        at = slice(i * chunk, (i + 1) * chunk)
        up = dot(a_ref[at, :], wu_ref[...]) + bu_ref[...]
        grad = dot_nt(dy_ref[at, :], wd_ref[...])
        cdf = 0.5 * (1.0 + lax.erf(up * (0.5**0.5)))
        density = jnp.exp(-0.5 * up * up) * (1.0 / math.sqrt(2.0 * math.pi))
        act_ref[at, :] = (up * cdf).astype(bf16)
        dup = (grad * (cdf + up * density)).astype(bf16)
        dup_ref[at, :] = dup
        bias = bias + jnp.sum(dup.astype(f32), axis=0, keepdims=True)
    bias_ref[...] = bias
    down = dot_tn(act_ref[...], dy_ref[...]).astype(bf16)

    for u in range(2):
        one, two = idx[1 + u], idx[2 - u]

        @pl.when(pl.program_id(0) // 2 == u)
        def _(u=u, one=one, two=two):
            step = pl.program_id(0) % 2
            for half, ref in ((0, sends[u]), (1, keeps[u])):

                @pl.when(step == half)
                def _(ref=ref):
                    for r in range(2):
                        ref[place_of(two, r), 1, :, :] = down[:, r * HALF : (r + 1) * HALF]

                p = one ^ (1 - half)
                for m in range(2):
                    left = a_ref[:, lanes_of(2 * m + p, chunk)]
                    grad = dot_tn(left, dup_ref[...]).astype(bf16)
                    spread_rows(ref, 0, grad, m, core, two, lanes_of(one ^ (1 - step), chunk))


def unit_call(idx, first, a, dy, up_mine, up_recv, w_down, b_up, act_all, dup_all):
    rows = a.shape[0]

    def sub(s, idx):
        u = s // 2
        return 2 * (first + u) + (idx[1 + u] ^ (1 - s % 2))

    whole = lambda s, idx: (0, 0)
    column = pl.BlockSpec((rows, 256), lambda s, idx: (0, sub(s, idx)))
    grads = pl.BlockSpec((2, 2, 256, 512), lambda s, idx: (0, 0, 0, 0))
    alias = [] if act_all is None else [act_all, dup_all]
    return pl.pallas_call(
        functools.partial(unit_body, len(alias)),
        grid_spec=pltpu.PrefetchScalarGridSpec(
            num_scalar_prefetch=1,
            grid=(4,),
            in_specs=[
                pl.BlockSpec((rows, D), whole),
                pl.BlockSpec((rows, D), whole),
                pl.BlockSpec((HALF, 256), lambda s, idx: (0, idx[0] * 8 + sub(s, idx))),
                pl.BlockSpec((HALF, 256), lambda s, idx: (0, sub(s, idx))),
                pl.BlockSpec((256, D), lambda s, idx: (sub(s, idx), 0)),
                pl.BlockSpec((1, 256), lambda s, idx: (0, sub(s, idx))),
            ]
            + [pl.BlockSpec(memory_space=pl.ANY)] * len(alias),
            out_specs=[grads] * 4
            + [
                column,
                column,
                pl.BlockSpec((1, 256), lambda s, idx: (0, sub(s, idx) - 2 * first)),
            ],
            scratch_shapes=[pltpu.VMEM((D, 256), bf16)],
        ),
        out_shape=[shape((2, 2, 256, 512), bf16)] * 4
        + [
            shape((rows, FF // 2), bf16),
            shape((rows, FF // 2), bf16),
            shape((1, 1024), f32),
        ],
        input_output_aliases={7: 4, 8: 5} if alias else {},
        compiler_params=params(),
        cost_estimate=cost(16 * rows * D * 512, 14 * 2**20),
        name="feed_forward",
    )(idx, a, dy, up_mine, up_recv, w_down, b_up, *alias)


def rotated(field, cosine, sine, direction):
    lane = lax.broadcasted_iota(jnp.int32, field.shape, 1) % HD
    partner = jnp.where(
        lane < ROT // 2,
        pltpu.roll(field, PAIR - ROT // 2, 1),
        pltpu.roll(field, ROT // 2, 1),
    )
    return field * cosine + (direction * sine) * partner


def whole_qkv(core, mine, recv_ref, w_ref):
    for t in range(3):
        w_ref[rows_of(core), t * HALF : (t + 1) * HALF] = mine[t][...]
    w_ref[rows_of(1 - core), :] = recv_ref[...]


def qkv_specs():
    return [
        pl.BlockSpec((HALF, HALF), lambda i, idx, t=t: (0, 2 * t + idx[0])) for t in range(3)
    ] + [pl.BlockSpec((HALF, 3 * HALF), lambda i, idx: (0, 0))]


def qkv_body(
    idx,
    x_ref,
    prev_ref,
    other_prev_ref,
    glob_ref,
    vec_ref,
    wq,
    wk,
    wv,
    recv_ref,
    cos_ref,
    sin_ref,
    cosp_ref,
    sinp_ref,
    cosg_ref,
    sing_ref,
    *outs,
):
    a1, q1, k1, v1, a2, k2, v2, a3, q3, k3, v3, w_ref = outs
    step = pl.program_id(0)
    first = idx[0] == 0

    def bias(t):
        at = [((2 * t + core) // 3, 6 + (2 * t + core) % 3) for core in range(2)]
        low, high = (vec_ref[h : h + 1, i * HALF : (i + 1) * HALF] for h, i in at)
        return jnp.where(first, low, high)

    @pl.when(step == 0)
    def _():
        whole_qkv(idx[0], (wq, wk, wv), recv_ref, w_ref)

    def run(x, cosine, sine, a_ref, refs):
        normal, _ = norm_parts(x.astype(f32))
        a = (normal * vector(vec_ref, 0) + vector(vec_ref, 1)).astype(bf16)
        a_ref[...] = a
        cosine, sine = cosine[...], sine[...]
        for t, ref in enumerate(refs):
            if ref is None:
                continue
            part = slice(t * HALF, (t + 1) * HALF)
            lin = dot(a, w_ref[:, part]) + bias(t)
            if t == 2:
                ref[...] = lin.astype(bf16)
                continue
            for j in range(HALF // PAIR):
                lanes = slice(j * PAIR, (j + 1) * PAIR)
                ref[:, lanes] = rotated(lin[:, lanes], cosine, sine, 1.0).astype(bf16)

    @pl.when(step < 4)
    def _():
        run(x_ref[...], cos_ref, sin_ref, a1, (q1, k1, v1))

    @pl.when((step >= 4) & (step < 6))
    def _():
        run(prev_ref[...], cosp_ref, sinp_ref, a2, (None, k2, v2))

    @pl.when((step >= 6) & (step < 8))
    def _():
        run(other_prev_ref[...], cosp_ref, sinp_ref, a2, (None, k2, v2))

    @pl.when(step == 8)
    def _():
        run(glob_ref[...], cosg_ref, sing_ref, a3, (q3, k3, v3))


def clamped(i, low, count):
    return jnp.clip(i - low, 0, count - 1)


def qkv_call(idx, x, prev, other_prev, glob, vectors, mine, recv, tables, before, far):
    step, rows = 256, x.shape[0]
    glob_n = glob.shape[0]

    def block(low, count, width, period=None):
        at = lambda i: clamped(i, low, count)
        if period:
            return pl.BlockSpec((step, width), lambda i, idx: (at(i) % period, 0))
        return pl.BlockSpec((step, width), lambda i, idx: (at(i), 0))

    whole = lambda width: pl.BlockSpec((glob_n, width), lambda i, idx: (0, 0))
    own, third = block(0, 4, D), block(0, 4, HALF)
    return pl.pallas_call(
        qkv_body,
        grid_spec=pltpu.PrefetchScalarGridSpec(
            num_scalar_prefetch=1,
            grid=(9,),
            in_specs=[own, block(4, 2, D), block(6, 2, D), whole(D)]
            + [pl.BlockSpec(vectors.shape, lambda i, idx: (0, 0))]
            + qkv_specs()
            + [block(0, 4, PAIR, 2)] * 2
            + [block(4, 4, PAIR, 2)] * 2
            + [whole(PAIR)] * 2,
            out_specs=[own, third, third, third, block(4, 4, D)]
            + [block(4, 4, HALF)] * 2
            + [whole(D)]
            + [whole(HALF)] * 3,
            scratch_shapes=[pltpu.VMEM((D, 3 * HALF), bf16)],
        ),
        out_shape=[shape((rows, D), bf16)]
        + [shape((rows, HALF), bf16)] * 3
        + [shape((rows, D), bf16)]
        + [shape((rows, HALF), bf16)] * 2
        + [shape((glob_n, D), bf16)]
        + [shape((glob_n, HALF), bf16)] * 3,
        compiler_params=params(),
        cost_estimate=cost(2 * rows * D * 5 * HALF, 22 * 2**20),
        name="qkv",
    )(idx, x, prev, other_prev, glob, vectors, mine, mine, mine, recv, *tables, *before, *far)


def heads_beside(block_t):
    dim = lax.broadcasted_iota(jnp.int32, block_t.shape, 0)
    zero = jnp.zeros_like(block_t)
    return jnp.concatenate(
        [jnp.where(dim < HD, block_t, zero), jnp.where(dim < HD, zero, block_t)], axis=1
    )


def heads_below(block):
    dim = lax.broadcasted_iota(jnp.int32, block.shape, 1)
    zero = jnp.zeros_like(block)
    return jnp.concatenate(
        [jnp.where(dim < HD, block, zero), jnp.where(dim < HD, zero, block)], axis=0
    )


def heads_back(both):
    n = both.shape[1] // 2
    dim = lax.broadcasted_iota(jnp.int32, (PAIR, n), 0)
    return jnp.where(dim < HD, both[:, :n], both[:, n:])


def near_body(
    info,
    q_ref,
    k_ref,
    v_ref,
    dol_ref,
    kp_ref,
    vp_ref,
    kg_ref,
    vg_ref,
    glob_ref,
    cos_ref,
    sin_ref,
    cosp_ref,
    sinp_ref,
    cosg_ref,
    sing_ref,
    *rest,
):
    o_ref, dq_ref, dk_ref, dv_ref, dkp_ref, dvp_ref, dkg_ref, dvg_ref, dk_acc, dv_acc = rest
    scale = HD**-0.5
    base = info[0]
    absent = jnp.where(base == 0, f32(negative), f32(0.0))
    keys = jnp.concatenate([kp_ref[...], k_ref[...]], axis=0)
    values = jnp.concatenate([vp_ref[...], v_ref[...]], axis=0)
    keys_t = keys.T
    values_t = values.T
    gkeys, gvalues = kg_ref[...], vg_ref[...]
    glob_n = gkeys.shape[0]
    gkeys_t = gkeys.astype(f32).T.astype(bf16)
    gvalues_t = gvalues.astype(f32).T.astype(bf16)
    keys_values = jnp.concatenate([keys, values], axis=1)
    gkeys_values = jnp.concatenate([gkeys, gvalues], axis=1)
    query = (q_ref[...].astype(f32) * scale).astype(bf16)
    query_t = query.T
    dol = dol_ref[...]
    dol_t = dol.T
    two = 2 * TILE
    window = WIN + TILE
    cosine, sine = cos_ref[...], sin_ref[...]
    row = lax.broadcasted_iota(jnp.int32, (TILE, two), 0)
    lane = lax.broadcasted_iota(jnp.int32, (TILE, two), 1) % TILE
    glane = lax.broadcasted_iota(jnp.int32, (glob_n, two), 1) % TILE
    gpos = jnp.concatenate([glob_ref[0], glob_ref[0]], axis=1)
    dkg = jnp.zeros((glob_n, PAIR), f32)
    dvg = jnp.zeros((glob_n, PAIR), f32)
    kk, vv = [None] * 8, [None] * 8
    for t in range(ROW // TILE):
        rows = slice(t * TILE, (t + 1) * TILE)
        span = slice(t * TILE, t * TILE + window)
        cut = WIN - t * TILE
        q_beside = heads_beside(query_t[:, rows])
        d_beside = heads_beside(dol_t[:, rows])
        q_below = heads_below(query[rows])
        d_below = heads_below(dol[rows])
        blank = jnp.zeros_like(q_beside)
        right = jnp.concatenate(
            [
                jnp.concatenate([q_beside, blank], axis=1),
                jnp.concatenate([blank, d_beside], axis=1),
            ],
            axis=0,
        )
        both = dot(keys_values[span], right)
        far_both = dot(gkeys_values, right)
        score, d_prob = both[:, :two], both[:, two:]
        far, d_far = far_both[:, :two], far_both[:, two:]
        parts = [
            jnp.where(row > lane, score[:TILE] + absent, negative),
        ]
        if cut > TILE:
            parts.append(score[TILE:cut] + absent)
        parts.append(score[cut:WIN])
        if t == 0:
            parts.pop()
        parts.append(jnp.where(row <= lane, score[WIN:], negative))
        score = jnp.concatenate(parts, axis=0)
        far = jnp.where(base + t * TILE + glane - gpos >= WIN, far, negative)
        top = jnp.maximum(
            jnp.max(score, axis=0, keepdims=True), jnp.max(far, axis=0, keepdims=True)
        )
        prob = jnp.exp(score - top)
        far_prob = jnp.exp(far - top)
        total = jnp.sum(prob, axis=0, keepdims=True) + jnp.sum(far_prob, axis=0, keepdims=True)
        delta = jnp.sum(prob * d_prob, axis=0, keepdims=True) + jnp.sum(
            far_prob * d_far, axis=0, keepdims=True
        )
        inverse = 1.0 / total
        delta = delta * inverse
        prob = prob * inverse
        far_prob = far_prob * inverse
        low, far_low = prob.astype(bf16), far_prob.astype(bf16)
        d_score = (prob * (d_prob - delta)).astype(bf16)
        d_far = (far_prob * (d_far - delta)).astype(bf16)
        out_t = dot(values_t[:, span], low) + dot(gvalues_t, far_low)
        o_ref[rows, :] = heads_back(out_t).T.astype(bf16)
        dq_t = dot(keys_t[:, span], d_score) + dot(gkeys_t, d_far)
        dq = heads_back(dq_t).T * scale
        dq_ref[rows, :] = rotated(dq, cosine[rows], sine[rows], -1.0).astype(bf16)
        tk, tv = dot(d_score, q_below), dot(low, d_below)
        for b in range(5):
            bk, bv = tk[b * TILE : (b + 1) * TILE], tv[b * TILE : (b + 1) * TILE]
            kk[t + b] = bk if kk[t + b] is None else kk[t + b] + bk
            vv[t + b] = bv if vv[t + b] is None else vv[t + b] + bv
        dkg = dkg + dot(d_far, q_below)
        dvg = dvg + dot(far_low, d_below)
    for b in range(8):
        dk_acc[b * TILE : (b + 1) * TILE, :] = kk[b]
        dv_acc[b * TILE : (b + 1) * TILE, :] = vv[b]
    dk_ref[...] = dk_acc[ROW:, :]
    dv_ref[...] = dv_acc[ROW:, :]
    dkp_ref[...] = rotated(dk_acc[:ROW, :], cosp_ref[...], sinp_ref[...], -1.0).astype(bf16)
    dvp_ref[...] = dv_acc[:ROW, :].astype(bf16)
    dkg_ref[...] = rotated(dkg, cosg_ref[...], sing_ref[...], -1.0).astype(bf16)
    dvg_ref[...] = dvg.astype(bf16)


def near_call(info, q, k, v, dol, k2, v2, kg, vg, glob_wide, tables, before, far):
    glob_n = glob_wide.shape[1]
    own = pl.BlockSpec((ROW, PAIR), lambda j, h, info: (j, h))
    glob = pl.BlockSpec((glob_n, PAIR), lambda j, h, info: (j, h))
    table = pl.BlockSpec((ROW, PAIR), lambda j, h, info: (0, 0))
    gtable = pl.BlockSpec((glob_n, PAIR), lambda j, h, info: (j, 0))
    rows = q.shape[0]
    own_low, own_high = shape((rows, HALF), bf16), shape((rows, HALF), f32)
    glob_low = shape((2 * glob_n, HALF), bf16)
    return pl.pallas_call(
        near_body,
        grid_spec=pltpu.PrefetchScalarGridSpec(
            num_scalar_prefetch=1,
            grid=(2, HALF // PAIR),
            in_specs=[own] * 6
            + [glob] * 2
            + [pl.BlockSpec((1, glob_n, PAIR), lambda j, h, info: (j, 0, 0))]
            + [table] * 4
            + [gtable] * 2,
            out_specs=[own] * 6 + [glob] * 2,
            scratch_shapes=[pltpu.VMEM((2 * ROW, PAIR), f32)] * 2,
        ),
        out_shape=[own_low, own_low, own_high, own_high, own_low, own_low, glob_low, glob_low],
        compiler_params=params(),
        cost_estimate=cost(8 * 4 * 6 * 2 * 704 * 256 * 256, 16 * 2**20),
        name="near",
    )(info, q, k, v, dol, k2, v2, kg, vg, glob_wide, *tables, *before, *far)


def glob_first_body(info, qg_ref, k_ref, v_ref, glob_ref, out_ref):
    glob_n = qg_ref.shape[0]
    query = qg_ref[...].astype(f32) * HD**-0.5
    beside = heads_beside(query.T).astype(bf16)
    score = dot(k_ref[...], beside)
    key_pos = info[0] + lax.broadcasted_iota(jnp.int32, score.shape, 0)
    mask = key_pos <= glob_ref[0][0:1]
    masked = jnp.where(mask, score, negative)
    top = jnp.max(masked, axis=0, keepdims=True)
    prob = jnp.where(mask, jnp.exp(masked - top), 0.0)
    total = jnp.sum(prob, axis=0, keepdims=True)
    both = dot(v_ref[...].T, prob.astype(bf16))
    lane = lax.broadcasted_iota(jnp.int32, (HD, 2 * glob_n), 1)
    out_ref[0, 0:HD, :] = jnp.where(lane < glob_n, both[:HD], both[HD:])
    out_ref[0, HD : HD + 1, :] = top
    out_ref[0, HD + 1 : HD + 2, :] = total
    out_ref[0, HD + 2 : HD + 8, :] = jnp.zeros((6, 2 * glob_n), f32)


def glob_first_call(info, qg, k, v, glob_row):
    glob_n = glob_row.shape[2] // 2
    own = pl.BlockSpec((ROW, PAIR), lambda j, h, info: (j, h))
    pairs = HALF // PAIR
    return pl.pallas_call(
        glob_first_body,
        grid_spec=pltpu.PrefetchScalarGridSpec(
            num_scalar_prefetch=1,
            grid=(2, pairs),
            in_specs=[
                pl.BlockSpec((glob_n, PAIR), lambda j, h, info: (j, h)),
                own,
                own,
                pl.BlockSpec((1, 8, 2 * glob_n), lambda j, h, info: (j, 0, 0)),
            ],
            out_specs=pl.BlockSpec(
                (1, HD + 8, 2 * glob_n), lambda j, h, info: (j * pairs + h, 0, 0)
            ),
        ),
        out_shape=shape((2 * pairs, HD + 8, 2 * glob_n), f32),
        compiler_params=params(),
        cost_estimate=cost(8 * 2 * 2 * 512 * 128 * 256, 3 * 2**20),
        name="glob_first",
    )(info, qg, k, v, glob_row)


def merged(first, second):
    top_a, top_b = first[:, HD : HD + 1], second[:, HD : HD + 1]
    top = jnp.maximum(top_a, top_b)
    weight_a, weight_b = jnp.exp(top_a - top), jnp.exp(top_b - top)
    total = first[:, HD + 1 : HD + 2] * weight_a + second[:, HD + 1 : HD + 2] * weight_b
    out = first[:, :HD] * weight_a + second[:, :HD] * weight_b
    return jnp.concatenate([out, top, total, first[:, HD + 2 :]], axis=1)


def glob_second_body(
    info,
    qg_ref,
    dolg_ref,
    k_ref,
    v_ref,
    stat_ref,
    glob_ref,
    near_ref,
    dk_in,
    dv_in,
    cos_ref,
    sin_ref,
    cosg_ref,
    sing_ref,
    o_ref,
    dk_ref,
    dv_ref,
    dqg_ref,
):
    scale = HD**-0.5
    glob_n = qg_ref.shape[0]
    keys, values = k_ref[...], v_ref[...]
    query = qg_ref[...].astype(f32) * scale
    q_beside = heads_beside(query.T).astype(bf16)
    q_below = heads_below(query.astype(bf16))
    dol = dolg_ref[...]
    dol_t = dol.astype(f32).T
    d_beside = heads_beside(dol_t).astype(bf16)
    d_below = heads_below(dol)
    out_t = stat_ref[0, 0:HD, :]
    top = stat_ref[0, HD : HD + 1, :]
    total = stat_ref[0, HD + 1 : HD + 2, :]
    out_t = out_t * (1.0 / total)
    lse = top + jnp.log(total)
    delta = jnp.sum(
        out_t * jnp.concatenate([dol_t[:HD], dol_t[HD:]], axis=1), axis=0, keepdims=True
    )
    score = dot(keys, q_beside)
    key_pos = info[0] + lax.broadcasted_iota(jnp.int32, score.shape, 0)
    positions = glob_ref[0][0:1]
    mask = key_pos <= positions
    prob = jnp.where(mask, jnp.exp(jnp.where(mask, score, negative) - lse), 0.0)
    d_prob = dot(values, d_beside)
    d_score = (prob * (d_prob - delta)).astype(bf16)
    low = prob.astype(bf16)
    dk = dk_in[...] + dot(d_score, q_below)
    dv = dv_in[...] + dot(low, d_below)
    dk_ref[...] = rotated(dk, cos_ref[...], sin_ref[...], -1.0).astype(bf16)
    dv_ref[...] = dv.astype(bf16)
    dq_both = dot(keys.T, d_score)
    dq_t = jnp.concatenate([dq_both[:HD, :glob_n], dq_both[HD:, glob_n:]], axis=0)
    dqg_ref[...] = rotated(dq_t.T * scale, cosg_ref[...], sing_ref[...], -1.0).astype(bf16)
    rows = jnp.concatenate([out_t[:, :glob_n], out_t[:, glob_n:]], axis=0).T.astype(bf16)
    place = (key_pos[:, :glob_n] == positions[:, :glob_n]).astype(f32)
    hit = jnp.sum(place, axis=1, keepdims=True) > 0.0
    o_ref[...] = jnp.where(hit, dot(place.astype(bf16), rows).astype(bf16), near_ref[...])


def glob_second_call(info, qg, dolg, k, v, stats, glob_row, near, dk, dv, tables, far):
    glob_n = glob_row.shape[2] // 2
    pairs = HALF // PAIR
    rows = k.shape[0]
    own = pl.BlockSpec((ROW, PAIR), lambda j, h, info: (j, h))
    glob = pl.BlockSpec((glob_n, PAIR), lambda j, h, info: (j, h))
    gtable = pl.BlockSpec((glob_n, PAIR), lambda j, h, info: (j, 0))
    table = pl.BlockSpec((ROW, PAIR), lambda j, h, info: (0, 0))
    return pl.pallas_call(
        glob_second_body,
        grid_spec=pltpu.PrefetchScalarGridSpec(
            num_scalar_prefetch=1,
            grid=(2, pairs),
            in_specs=[
                pl.BlockSpec((glob_n, PAIR), lambda j, h, info: (j, h)),
                glob,
                own,
                own,
                pl.BlockSpec((1, HD + 8, 2 * glob_n), lambda j, h, info: (j * pairs + h, 0, 0)),
                pl.BlockSpec((1, 8, 2 * glob_n), lambda j, h, info: (j, 0, 0)),
                own,
                own,
                own,
                table,
                table,
                gtable,
                gtable,
            ],
            out_specs=[
                own,
                own,
                own,
                glob,
            ],
        ),
        out_shape=[
            shape((rows, HALF), bf16),
            shape((rows, HALF), bf16),
            shape((rows, HALF), bf16),
            shape((2 * glob_n, HALF), bf16),
        ],
        compiler_params=params(),
        cost_estimate=cost(8 * 5 * 2 * 512 * 128 * 256, 10 * 2**20),
        name="glob_second",
    )(info, qg, dolg, k, v, stats, glob_row, near, dk, dv, *tables, *far)


def weights_body(units, idx, *refs):
    sends, keeps = refs[-4::2], refs[-3::2]
    core = idx[0]

    def run(u, ref):
        two = idx[2 - u]
        kind, *operands = units[u]
        if kind == "rows":
            left, right = operands
            total = dot_tn(refs[left][...], refs[right][...]).astype(bf16)
            for r in range(2):
                ref[place_of(two, r), 0, :, :] = total[:, r * HALF : (r + 1) * HALF]
            return
        for m in range(2):
            total = None
            for left, right in operands[0]:
                term = dot_tn(refs[left + m][...], refs[right][...])
                total = term if total is None else total + term
            spread_rows(ref, 0, total.astype(bf16), m, core, two, slice(None))

    for u in range(2):
        for half, ref in ((0, sends[u]), (1, keeps[u])):

            @pl.when(pl.program_id(0) == 2 * u + half)
            def _(u=u, ref=ref):
                run(u, ref)


def weights_call(idx, units):
    specs, operands, table, lefts = [], [], [], {}

    def add(array, spec):
        specs.append(spec)
        operands.append(array)
        return len(operands) - 1

    def whole(array):
        return add(array, pl.BlockSpec(array.shape, lambda s, idx: (0, 0)))

    def part(s, idx):
        return idx[1 + s // 2] ^ (1 - s % 2)

    def left_of(array):
        if id(array) not in lefts:
            lefts[id(array)] = [
                add(
                    array,
                    pl.BlockSpec(
                        (array.shape[0], 256), lambda s, idx, m=m: (0, 2 * m + part(s, idx))
                    ),
                )
                for m in range(2)
            ][0]
        return lefts[id(array)]

    for kind, products in units:
        if kind == "rows":
            left, right = products
            spec = pl.BlockSpec((left.shape[0], 256), lambda s, idx: (0, part(s, idx)))
            table.append((kind, add(left, spec), whole(right)))
        else:
            table.append((kind, tuple((left_of(left), whole(right)) for left, right in products)))
    out = pl.BlockSpec((2, 1, 256, 512), lambda s, idx: (0, 0, 0, 0))
    return pl.pallas_call(
        functools.partial(weights_body, tuple(table)),
        grid_spec=pltpu.PrefetchScalarGridSpec(
            num_scalar_prefetch=1, grid=(4,), in_specs=specs, out_specs=[out] * 4
        ),
        out_shape=[shape((2, 1, 256, 512), bf16)] * 4,
        compiler_params=params(),
        cost_estimate=cost(4 * 10**9, 12 * 2**20),
        name="weight_grads",
    )(idx, *operands)


def input_body(idx, *refs):
    x_ref, xp_ref, xop_ref, xg_ref, vec_ref = refs[:5]
    weights, up_mine, up_recv = refs[5:9], refs[9], refs[10]
    dq1, dk1, dv1, dkp, dvp, dqg, dkg, dvg, dup_ref = refs[11:20]
    own, own_other, prev, prev_other, glob, sums_a, sums_m, bias_ref, w_ref, wu_ref = refs[20:]
    step = pl.program_id(0)

    @pl.when(step == 0)
    def _():
        sums_a[...] = jnp.zeros_like(sums_a)
        sums_m[...] = jnp.zeros_like(sums_m)
        bias_ref[...] = jnp.zeros_like(bias_ref)
        whole_qkv(idx[0], weights[:3], weights[3], w_ref)
        wu_ref[rows_of(idx[0]), :] = up_mine[...]
        wu_ref[rows_of(1 - idx[0]), :] = up_recv[...]

    def gather(sums, grad, normal):
        sums[0:1, :] += jnp.sum(grad * normal, axis=0, keepdims=True)
        sums[1:2, :] += jnp.sum(grad, axis=0, keepdims=True)

    def attn(x, parts):
        grad = None
        for t, ref in enumerate(parts):
            if ref is None:
                continue
            part = ref[...]
            lanes = slice(t * HALF, (t + 1) * HALF)
            term = dot_nt(part, w_ref[:, lanes])
            grad = term if grad is None else grad + term
            bias_ref[0:1, lanes] += jnp.sum(part.astype(f32), axis=0, keepdims=True)
        normal, _ = norm_parts(x[...].astype(f32))
        gather(sums_a, grad, normal)
        return grad * vector(vec_ref, 0), normal

    def own_rows(out):
        g, normal = attn(x_ref, (dq1, dk1, dv1))
        grad = dot_nt(dup_ref[...], wu_ref[...])
        gather(sums_m, grad, normal)
        out[...] = (g + grad * vector(vec_ref, 2)).astype(bf16)

    @pl.when(step < 2)
    def _():
        own_rows(own)

    @pl.when((step >= 2) & (step < 4))
    def _():
        own_rows(own_other)

    @pl.when((step >= 4) & (step < 6))
    def _():
        prev[...] = attn(xp_ref, (None, dkp, dvp))[0].astype(bf16)

    @pl.when((step >= 6) & (step < 8))
    def _():
        prev_other[...] = attn(xop_ref, (None, dkp, dvp))[0].astype(bf16)

    @pl.when(step == 8)
    def _():
        glob[...] = attn(xg_ref, (dqg, dkg, dvg))[0].astype(bf16)


def input_call(idx, x, prev, other_prev, glob, vectors, mine, recv, up_mine, up_recv, grads):
    step, rows, glob_n = 256, x.shape[0], glob.shape[0]

    def block(low, count, width):
        return pl.BlockSpec((step, width), lambda i, idx: (clamped(i, low, count), 0))

    whole = lambda rows, width: pl.BlockSpec((rows, width), lambda i, idx: (0, 0))
    return pl.pallas_call(
        input_body,
        grid_spec=pltpu.PrefetchScalarGridSpec(
            num_scalar_prefetch=1,
            grid=(9,),
            in_specs=[block(0, 4, D), block(4, 2, D), block(6, 2, D), whole(glob_n, D)]
            + [whole(*vectors.shape)]
            + qkv_specs()
            + [
                pl.BlockSpec((HALF, FF // 2), lambda i, idx: (0, idx[0])),
                whole(HALF, FF // 2),
            ]
            + [block(0, 4, HALF)] * 3
            + [block(4, 4, HALF)] * 2
            + [whole(glob_n, HALF)] * 3
            + [block(0, 4, FF // 2)],
            out_specs=[
                block(0, 2, D),
                block(2, 2, D),
                block(4, 2, D),
                block(6, 2, D),
                whole(glob_n, D),
                whole(8, D),
                whole(8, D),
                whole(8, 3 * HALF),
            ],
            scratch_shapes=[pltpu.VMEM((D, 3 * HALF), bf16), pltpu.VMEM((D, FF // 2), bf16)],
        ),
        out_shape=[shape((rows // 2, D), bf16)] * 4
        + [
            shape((glob_n, D), bf16),
            shape((8, D), f32),
            shape((8, D), f32),
            shape((8, 3 * HALF), f32),
        ],
        compiler_params=params(),
        cost_estimate=cost(2 * rows * D * (5 * HALF + FF // 2), 30 * 2**20),
        name="input_grads",
    )(
        idx,
        x,
        prev,
        other_prev,
        glob,
        vectors,
        mine,
        mine,
        mine,
        recv,
        up_mine,
        up_recv,
        *grads,
    )


def result_body(act_ref, wd_ref, ol_ref, wp_ref, mine_ref, other_ref):
    part = (dot(act_ref[...], wd_ref[...]) + dot(ol_ref[...], wp_ref[...])).astype(bf16)
    half = pl.num_programs(0) // 2

    @pl.when(pl.program_id(0) < half)
    def _():
        mine_ref[...] = part

    @pl.when(pl.program_id(0) >= half)
    def _():
        other_ref[...] = part


def result_call(act, w_down, ol, w_proj):
    rows, step = act.shape[0], 256
    half = rows // step // 2
    return pl.pallas_call(
        result_body,
        grid=(rows // step,),
        in_specs=[
            pl.BlockSpec((step, act.shape[1]), lambda i: (i, 0)),
            pl.BlockSpec(w_down.shape, lambda i: (0, 0)),
            pl.BlockSpec((step, HALF), lambda i: (i, 0)),
            pl.BlockSpec(w_proj.shape, lambda i: (0, 0)),
        ],
        out_specs=[
            pl.BlockSpec((step, D), lambda i: (jnp.minimum(i, half - 1), 0)),
            pl.BlockSpec((step, D), lambda i: (jnp.maximum(i - half, 0), 0)),
        ],
        out_shape=[shape((rows // 2, D), bf16)] * 2,
        compiler_params=params(),
        cost_estimate=cost(2 * rows * D * (FF // 2 + HALF), 14 * 2**20),
        name="result",
    )(act, w_down, ol, w_proj)


def place_body(spreads, rows, n_alias, idx, *refs):
    pieces, swapped = (refs[:4], refs[4:8]), refs[8]
    outs = list(refs[9 + n_alias :])
    spread_out = outs.pop(0) if spreads else None
    rows_out = outs.pop(0) if rows else None
    half = pl.program_id(2)

    for i in range(max(len(spreads), len(rows))):
        for g in range(2):

            @pl.when((pl.program_id(0) == i) & (pl.program_id(1) == g))
            def _(i=i, g=g):
                for beside in range(2):
                    if i < len(spreads):
                        u, tile = spreads[i]
                        r = idx[2 - u] ^ beside
                        at = pl.ds(pl.multiple_of(r * TILE, TILE), TILE)
                        piece = pieces[u][2 * g + beside]

                        @pl.when(half == 0)
                        def _():
                            spread_out[at, :] = piece[tile, TILE:, :].astype(f32)

                        @pl.when(half == 1)
                        def _():
                            spread_out[at, :] = swapped[4 * i + 2 * g + beside].astype(f32)

                    if i < len(rows):
                        u, tile = rows[i]
                        r = idx[2 - u] ^ beside
                        at = pl.ds(pl.multiple_of(half * TILE, TILE), TILE)
                        part = pieces[u][2 * g + beside][tile, at, :]
                        rows_out[:, lanes_of(r, HALF)] = part.astype(f32)


def place_call(idx, work, spreads, rows, spread_target, rows_target):
    targets = [target for target in (spread_target, rows_target) if target is not None]
    alias = [buf for buf, _, _ in targets if buf is not None]
    aliases, at = {}, 10
    for out, (buf, _, _) in enumerate(targets):
        if buf is not None:
            aliases[at] = out
            at += 1

    def index(tiles, where):
        def block(i, g, h, idx):
            last = len(tiles) - 1
            over = i > last
            i, g, h = jnp.where(over, last, i), jnp.where(over, 1, g), jnp.where(over, 1, h)
            unit = tiles[0][0]
            for k, (u, _) in enumerate(tiles):
                unit = jnp.where(i == k, u, unit)
            return where(i, jnp.where(unit == 0, idx[1], idx[2]) ^ g, h, idx[0])

        return block

    out_specs = []
    if spreads:
        out_specs.append(pl.BlockSpec((2 * TILE, HALF), index(spreads, spread_target[2])))
    if rows:
        out_specs.append(pl.BlockSpec((TILE, D), index(rows, rows_target[2])))
    whole = lambda array: pl.BlockSpec(array.shape, lambda i, g, h, idx: (0, 0, 0))
    operands = [*work.pieces[0], *work.pieces[1], work.swapped]
    return pl.pallas_call(
        functools.partial(place_body, spreads, rows, len(alias)),
        grid_spec=pltpu.PrefetchScalarGridSpec(
            num_scalar_prefetch=1,
            grid=(max(len(spreads), len(rows)), 2, 2),
            in_specs=[whole(array) for array in operands]
            + [pl.BlockSpec(memory_space=pl.ANY)] * len(alias),
            out_specs=out_specs,
        ),
        out_shape=[shape(dims, f32) for _, dims, _ in targets],
        input_output_aliases=aliases,
        compiler_params=params(),
        cost_estimate=cost(0, 14 * 2**20),
        name="place",
    )(idx, *operands, *alias)


def rotary_tables(positions):
    lane = jnp.arange(PAIR, dtype=jnp.int32) % HD
    half = ROT // 2
    freqs = rotary_base ** (-2.0 * (lane % half).astype(f32) / ROT)
    angles = positions.astype(f32)[:, None] * freqs[None, :]
    active = (lane < ROT)[None, :]
    sign = jnp.where(lane < half, -1.0, 1.0)[None, :]
    return jnp.where(active, jnp.cos(angles), 1.0), jnp.where(active, jnp.sin(angles) * sign, 0.0)


def per_device(
    tokens,
    cotangent,
    global_pos,
    attn_gain,
    attn_shift,
    mlp_gain,
    mlp_shift,
    qkv_weight,
    qkv_bias,
    proj_weight,
    proj_bias,
    up_weight,
    up_bias,
    down_weight,
    down_bias,
):
    n_ctx = lax.axis_size("ctx")
    core = lax.axis_index("fsdp")
    seq = lax.axis_index("seq")
    ctx = lax.axis_index("ctx")
    x_bit, y_bit = seq & 1, seq >> 1
    base = ctx * ROW
    own_x = tokens[0]
    own_dy = cotangent[0]
    glob_n = global_pos.shape[1]
    share = glob_n // n_ctx
    info = jnp.stack([base]).astype(jnp.int32)
    idx = jnp.stack([core, x_bit, y_bit, ctx]).astype(jnp.int32)
    order = Order()

    other_x = pair(own_x)
    mine = jnp.concatenate(
        [attn_gain, attn_shift, mlp_gain, mlp_shift, proj_bias, down_bias, qkv_bias]
    )
    theirs = pair(mine)
    up_recv = pair(lax.dynamic_slice_in_dim(up_weight, (1 - core) * (FF // 2), FF // 2, 1))
    other_dy = pair(own_dy)
    halves = jnp.stack([mine, theirs])
    vectors = jnp.where(core == 0, halves, halves[::-1]).astype(f32)
    bias_up = up_bias.astype(f32).reshape(1, FF // 2)

    a_mlp, x, dy = norm_call(own_x, other_x, own_dy, other_dy, vectors)
    order.mark(a_mlp)
    prev_x = shifted(order.gate(own_x), 1)
    positions, w_in, x_in, dy_in = order.gate(global_pos[0], qkv_weight, own_x, own_dy)
    own_glob = lax.dynamic_slice_in_dim(positions, ctx * share, share, 0)
    pick = (own_glob[:, None] - base == jnp.arange(ROW, dtype=jnp.int32)[None, :]).astype(bf16)
    picked = jnp.stack([dot(pick, x_in), dot(pick, dy_in)]).astype(bf16)
    picked = order.mark(picked)[None]
    pos_pair = jnp.stack([positions, pair(positions)])
    if n_ctx == 4:
        picked_parts = [picked] + [exchange(picked, "ctx", k) for k in (1, 2, 3)]
    act = dup = None
    up_sums = []

    def units(first, act, dup):
        a = order.gate(a_mlp)
        *four, act, dup, sums = unit_call(
            idx, first, a, dy, up_weight, up_recv, down_weight, bias_up, act, dup
        )
        order.mark(sums)
        up_sums.append(sums.reshape(2, 512))
        return Reduction(order, idx, [four[:2], four[2:]]), act, dup

    work0, act, dup = units(0, act, dup)
    qkv_recv = pair(
        jnp.concatenate(
            [
                lax.dynamic_slice_in_dim(w_in, (2 * t + 1 - core) * HALF, HALF, 1)
                for t in range(3)
            ],
            axis=1,
        )
    )
    other_prev = pair(order.gate(prev_x))
    if n_ctx == 4:
        picked = jnp.concatenate(order.gate(*picked_parts), axis=0)
    else:
        for distance in doubling("ctx"):
            picked = jnp.concatenate([picked, exchange(picked, "ctx", distance)], axis=0)
    picked = jnp.take(picked, jnp.arange(n_ctx, dtype=jnp.int32) ^ ctx, axis=0)
    picked = order.mark(jnp.transpose(picked, (1, 0, 2, 3)).reshape(2, glob_n, D))
    other_picked = pair(picked)
    row_pos = base + jnp.arange(ROW, dtype=jnp.int32)
    work1, act, dup = units(2, act, dup)
    work0.second()

    tables = rotary_tables(order.gate(row_pos))
    before = rotary_tables(order.gate(row_pos) - ROW)
    far = rotary_tables(order.gate(pos_pair).reshape(-1))
    x_glob = jnp.concatenate([picked[0], other_picked[0]], axis=0)
    a1, q1, k1, v1, a2, k2, v2, a3, q3, k3, v3 = qkv_call(
        idx,
        order.gate(x),
        prev_x,
        other_prev,
        x_glob,
        vectors,
        qkv_weight,
        qkv_recv,
        tables,
        before,
        far,
    )
    order.mark(q3)
    is_glob = jnp.any(row_pos[None, :, None] == pos_pair[:, None, :], axis=2).reshape(2 * ROW, 1)
    glob_row = jnp.broadcast_to(
        jnp.concatenate([pos_pair, pos_pair], axis=1)[:, None, :], (2, 8, 2 * glob_n)
    )
    glob_wide = jnp.broadcast_to(pos_pair[:, :, None], (2, glob_n, PAIR))
    stats = order.mark(glob_first_call(info, order.gate(q3), k1, v1, glob_row))
    stats_beside = exchange(stats, "ctx", 1)
    dol = order.mark(
        jnp.where(is_glob, 0.0, dot_nt(order.gate(dy), proj_weight)).astype(bf16)
    )
    dolg = order.mark(
        dot_nt(
            jnp.concatenate([order.gate(picked)[1], other_picked[1]], axis=0), proj_weight
        ).astype(bf16)
    )
    work0.over_ctx()
    stats, stats_beside = order.gate(stats, stats_beside)
    stats = order.mark(merged(stats, stats_beside))
    for distance in doubling("ctx")[1:]:
        stats_beside = exchange(stats, "ctx", distance)
        if distance > 2:
            stats = merged(stats, stats_beside)
    work1.second()
    outs = near_call(
        info, order.gate(q1), k1, v1, dol, k2, v2, k3, v3, glob_wide, tables, before, far
    )
    near, dq1, dk1, dv1, dkp, dvp, dkg, dvg = outs
    order.mark(dkg)
    work0.ctx_sum()
    work1.over_ctx()
    if n_ctx <= 4:
        stats = order.mark(merged(*order.gate(stats, stats_beside)))
    ol, dk1, dv1, dqg = glob_second_call(
        info, q3, dolg, k1, v1, order.gate(stats), glob_row, near, dk1, dv1, tables, far
    )
    order.mark(dqg)
    lin_grads = (dq1, dk1, dv1, dkp, dvp, dqg, dkg, dvg)
    four = weights_call(
        idx,
        [
            ("spread", ((a1, order.gate(dv1)), (a2, dvp), (a3, dvg))),
            ("spread", ((a1, dq1), (a3, dqg))),
        ],
    )
    order.mark(four[0])
    work2 = Reduction(order, idx, [four[:2], four[2:]])
    four = weights_call(
        idx,
        [
            ("rows", (order.gate(ol), dy)),
            ("spread", ((a1, dk1), (a2, dkp), (a3, dkg))),
        ],
    )
    order.mark(four[0])
    work3 = Reduction(order, idx, [four[:2], four[2:]])
    work0.gather()
    work1.ctx_sum()
    work2.second()

    g_own, g_own_other, g_prev, g_prev_other, g_globs, sums_a, sums_m, bias = input_call(
        idx,
        order.gate(x),
        prev_x,
        other_prev,
        x_glob,
        vectors,
        qkv_weight,
        qkv_recv,
        up_weight,
        up_recv,
        (*lin_grads, dup),
    )
    order.mark(bias)
    prev_beside = pair(g_prev_other)
    own_beside = pair(g_own_other)
    glob_sum = added(g_globs[:glob_n], pair(g_globs[glob_n:]))
    work2.over_ctx()
    work3.second()
    work0.gather_rest()
    work1.gather()
    from_prev = shifted(order.mark(added(*order.gate(g_prev, prev_beside))), -1)

    part, part_other = result_call(order.gate(act), down_weight, ol, proj_weight)
    order.mark(part)
    part_beside = pair(part_other)
    work2.ctx_sum()
    work3.over_ctx()

    up_dims, down_dims = (HALF, FF), (FF // 2, D)

    def place_units(work, first, up_out, down_out):
        up_out, down_out = place_call(
            idx,
            work,
            ((0, 0), (1, 0)),
            ((0, 1), (1, 1)),
            (up_out, up_dims, lambda i, p, h, c: (p, (c ^ h) * 4 + first + i)),
            (down_out, down_dims, lambda i, p, h, c: ((first + i) * 4 + p * 2 + h, 0)),
        )
        order.mark(up_out[:8, :128])
        return up_out, down_out

    work0.swap([(0, 0), (1, 0)])
    work1.gather_rest()
    own, part, part_beside = order.gate(own_x, part, part_beside)
    result = own.astype(f32) + part.astype(f32) + part_beside.astype(f32)
    biases = [vectors[:, i * HALF : (i + 1) * HALF].reshape(1, D) for i in (4, 5)]
    layer_out = order.mark((result + biases[0] + biases[1]).astype(bf16))[None]
    work2.gather()
    work3.ctx_sum()
    up_out, down_out = place_units(work0, 0, None, None)

    for distance in doubling("ctx"):
        beside = exchange(glob_sum, "ctx", distance)
        glob_sum, beside = order.gate(glob_sum, beside)
        glob_sum = order.mark(added(glob_sum, beside))
    place = (row_pos[:, None] == global_pos[0][None, :]).astype(bf16)
    own, g_own, own_beside, from_prev = order.gate(own_x, g_own, own_beside, from_prev)
    g = (
        g_own.astype(f32)
        + own_beside.astype(f32)
        + from_prev.astype(f32)
        + dot(place, glob_sum)
    )
    normal, inverse = norm_parts(own.astype(f32))
    lower = inverse * (
        g
        - jnp.mean(g, axis=-1, keepdims=True)
        - normal * jnp.mean(g * normal, axis=-1, keepdims=True)
    )
    tokens_grad = order.mark(own_dy.astype(f32) + lower)[None]
    work2.gather_rest()
    work3.gather()
    work1.swap([(0, 0), (1, 0)])

    dy_sum = jnp.sum(order.gate(own_dy).astype(f32), axis=0)
    qkv_sum = bias[0].reshape(3, 1, HALF)
    mine = jnp.arange(2, dtype=jnp.int32)[None, :, None] == core
    qkv_sum = jnp.where(mine, qkv_sum, 0.0).reshape(2, 3, 512)
    split = jnp.concatenate(
        [
            sums_a[:2].reshape(2, 2, 512).swapaxes(0, 1),
            sums_m[:2].reshape(2, 2, 512).swapaxes(0, 1),
            dy_sum.reshape(2, 1, 512),
            qkv_sum,
        ],
        axis=1,
    )
    kept = lax.dynamic_index_in_dim(split, core, 0, False)
    given = lax.dynamic_index_in_dim(split, 1 - core, 0, False)
    total = jnp.concatenate([kept + pair(given)] + up_sums, axis=0)
    for axis in ("seq", "ctx"):
        for distance in doubling(axis):
            total = total + exchange(total, axis, distance)

    work3.gather_rest()
    up_out, down_out = place_units(work1, 2, up_out, down_out)
    work2.swap([(0, 0), (1, 0)])
    qkv_dims = (HALF, 3 * D)
    (qkv_out,) = place_call(
        idx,
        work2,
        ((0, 0), (1, 0)),
        (),
        (None, qkv_dims, lambda i, p, h, c: (p, jnp.where(i == 0, 4, 0) + (c ^ h))),
        None,
    )
    order.mark(qkv_out[:8, :128])
    work3.swap([(1, 0)])
    qkv_out, proj_out = place_call(
        idx,
        work3,
        ((1, 0),),
        ((0, 0),),
        (qkv_out, qkv_dims, lambda i, p, h, c: (p, 2 + (c ^ h))),
        (None, (HALF, D), lambda i, p, h, c: (p * 2 + h, 0)),
    )
    return (
        layer_out,
        tokens_grad,
        total[0],
        total[1],
        total[2],
        total[3],
        qkv_out,
        total[5:8].reshape(-1),
        proj_out,
        total[4],
        up_out,
        total[8:12].reshape(-1),
        down_out,
        total[4],
    )


def solution(mesh):
    rows = P(("seq", "fsdp"), "ctx", None)
    vector, matrix = P("fsdp"), P("fsdp", None)
    return jax.shard_map(
        per_device,
        mesh=mesh,
        in_specs=(
            rows,
            rows,
            P(("seq", "fsdp"), None),
            vector,
            vector,
            vector,
            vector,
            matrix,
            vector,
            matrix,
            vector,
            matrix,
            vector,
            matrix,
            vector,
        ),
        out_specs=(
            rows,
            rows,
            vector,
            vector,
            vector,
            vector,
            matrix,
            vector,
            matrix,
            vector,
            matrix,
            vector,
            matrix,
            vector,
        ),
        check_vma=False,
    )
```

time: 759 us -> 488 us (0.64)
  waiting for transfers between devices: 301 us -> 61 us
  local copies, waits for them, and re-layouts: 85.8 us -> 30.4 us
  starting transfers between devices: 54.9 us -> 105 us
  Pallas kernels: 211 us -> 246 us
  other arithmetic: 57.7 us -> 28.1 us
  between operations: 15.6 us -> 2.01 us
  matrix products: 22.2 us -> 9.67 us
    psum x6 -> x0, waiting for transfers between devices: 155 us -> none  [per_device(): piece = lax.psum(piece, 'ctx')]
    ppermute x40 -> x75, waiting for transfers between devices: 141 us -> 61 us  [exchange(): lax.ppermute(block, axis, [(i, i ^ distance) for i in range(lax.axis_size...]
    pallas_call x16 -> x26, Pallas kernels: 99.1 us -> 155 us  [the longest x4 26.8 us: place_call(): pl.pallas_call(functools.partial(place_body, spreads, rows, len(alias)),...]
    ppermute x40 -> x75, starting transfers between devices: 44.4 us -> 96.3 us  [exchange(): lax.ppermute(block, axis, [(i, i ^ distance) for i in range(lax.axis_size...]
    reshape x11 -> x2, local copies, waits for them, and re-layouts: 17.8 us -> 0.02 us  [units(): up_sums.append(sums.reshape(2, 512))]
    concatenate x20 -> x5, other arithmetic: 19.7 us -> 2.11 us  [the longest x1 1.3 us: per_device(): jnp.concatenate([lax.dynamic_slice_in_dim(w_in, (2 * t + 1 - core) * HALF...]
    dynamic_slice x4 -> x2, local copies, waits for them, and re-layouts: 16.7 us -> 3.35 us  [the longest x1 3.17 us: per_device(): lax.dynamic_slice_in_dim(up_weight, (1 - core) * (FF // 2), FF // 2, 1)]
    pallas_call x1, Pallas kernels: 46 us -> 34.3 us  [near_call(): pl.pallas_call(near_body, grid_spec=pltpu.PrefetchScalarGridSpec(num_scal...]
  transfers between devices with their start and end apart: 68 -> 94, of which waited for: 22 -> 16; matrix products, arithmetic and copies ran while one was open for 20% -> 10% of each run, Pallas kernels for 27% -> 50%
where the time goes in v2:
time: 488 us; the launch traced here: 482 us
  Pallas kernels  246 us (50%)
  starting transfers between devices  105 us (22%)
  waiting for transfers between devices  61 us (12%)
  local copies, waits for them, and re-layouts  30.4 us (6%)
  other arithmetic  28.1 us (6%)
  matrix products  9.67 us (2%)
    ppermute x75, starting transfers between devices, exchange(): lax.ppermute(block, axis, [(i, i ^ distance) for i in range(lax.axis_size...  96.3 us
    ppermute x75, waiting for transfers between devices, exchange(): lax.ppermute(block, axis, [(i, i ^ distance) for i in range(lax.axis_size...  61 us
    pallas_call x2, Pallas kernels, unit_call(): pl.pallas_call(functools.partial(unit_body, len(alias)), grid_spec=pltpu....  38.1 us
    pallas_call x1, Pallas kernels, near_call(): pl.pallas_call(near_body, grid_spec=pltpu.PrefetchScalarGridSpec(num_scal...  34.3 us
    pallas_call x4, Pallas kernels, place_call(): pl.pallas_call(functools.partial(place_body, spreads, rows, len(alias)),...  26.8 us
    pallas_call x1, Pallas kernels, input_call(): pl.pallas_call(input_body, grid_spec=pltpu.PrefetchScalarGridSpec(num_sca...  23.9 us
    pallas_call x2, Pallas kernels, weights_call(): pl.pallas_call(functools.partial(weights_body, tuple(table)), grid_spec=p...  21.6 us
    unnamed x180, local copies, waits for them, and re-layouts  18.2 us
  transfers between devices with their start and end apart: 94, of which 16 were waited for; matrix products, arithmetic and copies ran while one was open for 10% of the time, Pallas kernels for 50%

profile of v2, /device:TPU:0, one launch (start us, length us, event | category | flops | bytes accessed | tf_op | source)
XLA Modules:
  0.0 482.3 jit_solution(5771938357330201176)
XLA Ops:
  14.6 6.0 %norm.1 = (bf16[1024,1024]{1,0:T(8,128)(2,1)}, bf16[1024,1024]{1,0:T(8,128)(2,1)}, bf16[1024,1024]{1,0:T(8,128)(2,1)}) custom-call(bf16[512,1024]{1,0:T(8,128)(2,1)} %bitcast.x_ref, bf16[512,1024]{1,0:T(8,128)(2,1)} %copy-done.29, bf16[512,1024]{1,0:T(8,128)(2,1)} %bitcast.98, bf16[512,1024]{1,0:T(8,128)(2,1)} %collective-permute-done.1.dy_other_ref, ...), custom_call_target="tpu_custom_call" | custom-call | flops 10485 | bytes 12582 | tf_op jit(solution)/shard_map/norm/pallas_call | solution.py:319
  29.5 4.1 collective-permute-start.9
  35.1 19.0 %feed_forward.2 = (bf16[2,2,256,512]{3,2,1,0:T(8,128)(2,1)}, bf16[2,2,256,512]{3,2,1,0:T(8,128)(2,1)}, bf16[2,2,256,512]{3,2,1,0:T(8,128)(2,1)}, bf16[2,2,256,51...) custom-call(s32[4]{0:T(128)} %pad_add_fusion.1.idx, ...), custom_call_target="tpu_custom_call" | custom-call | flops 8589934 | bytes 14680 | tf_op jit(solution)/shard_map/feed_forward/pallas_call | solution.py:398
  59.4 19.1 %feed_forward.3 = (bf16[2,2,256,512]{3,2,1,0:T(8,128)(2,1)}, bf16[2,2,256,512]{3,2,1,0:T(8,128)(2,1)}, bf16[2,2,256,512]{3,2,1,0:T(8,128)(2,1)}, bf16[2,2,256,51...) custom-call(s32[4]{0:T(128)} %pad_add_fusion.1.idx, ...), custom_call_target="tpu_custom_call", output_to_operand_aliasing={{4}: (7, {}), {5}: (8, {})} | custom-call | flops 8589934 | bytes 14680 | tf_op jit(solution)/shard_map/feed_forward/pallas_call | solution.py:398
  90.6 17.5 %qkv.1 = (bf16[1024,1024]{1,0:T(8,128)(2,1)}, bf16[1024,512]{1,0:T(8,128)(2,1)}, bf16[1024,512]{1,0:T(8,128)(2,1)}, bf16[1024,512]{1,0:T(8,128)(2,1)}, bf16[1024...) custom-call(s32[4]{0:T(128)} %pad_add_fusion.1.idx, ...), custom_call_target="tpu_custom_call" | custom-call | flops 5368709 | bytes 23068 | tf_op jit(solution)/shard_map/qkv/pallas_call | solution.py:537
  108.7 7.8 %glob_first.1 = f32[8,72,128]{2,1,0:T(8,128)} custom-call(s32[1]{0:T(128)} %bitcast.17.info, bf16[128,512]{1,0:T(8,128)(2,1)} %get-tuple-element.295.qg_ref, bf16[1024,512]{1,0:T(8,128)(2,1)} %get-tuple-element.296.k_ref, bf16[1024,512]{1,0:T(8,128)(2,1)} %get-tuple-element.297.v_ref, s32[2,8,128]{2,1,0:T(8,128)} %broadcast_in_dim.170.glob_ref), custom_call_target="tpu_custom_call" | custom-call | flops 536870 | bytes 3145 | tf_op jit(solution)/shard_map/glob_first/pallas_call | solution.py:757
  121.9 7.7 %collective-permute-done.16 = bf16[2,256,512]{2,1,0:T(8,128)(2,1)S(1)} collective-permute-done((bf16[2,256,512]{2,1,0:T(8,128)(2,1)}, bf16[2,256,512]{2,1,0:T(8,128)(2,1)S(1)}, u32[]{:S(2)}, u32[]{:S(2)}) %collective-permute-start.16) | collective-permute-done | bytes 524320 | tf_op jit(solution)/shard_map/ppermute | solution.py:65
  130.4 4.7 quarters.4
  146.8 34.3 %near.1 = (bf16[1024,512]{1,0:T(8,128)(2,1)}, bf16[1024,512]{1,0:T(8,128)(2,1)}, f32[1024,512]{1,0:T(8,128)}, f32[1024,512]{1,0:T(8,128)}, bf16[1024,512]{1,0:T(...) custom-call(s32[1]{0:T(128)} %bitcast.17.info, ...), custom_call_target="tpu_custom_call" | custom-call | flops 17716740 | bytes 16777 | tf_op jit(solution)/shard_map/near/pallas_call | solution.py:714
  186.9 4.7 quarters.5
  192.4 11.0 %glob_second.1 = (bf16[1024,512]{1,0:T(8,128)(2,1)}, bf16[1024,512]{1,0:T(8,128)(2,1)}, bf16[1024,512]{1,0:T(8,128)(2,1)}, bf16[128,512]{1,0:T(8,128)(2,1)}) custom-call(s32[1]{0:T(128)} %bitcast.17.info, bf16[128,512]{1,0:T(8,128)(2,1)} %get-tuple-element.295.qg_ref, bf16[128,512]{1,0:T(8,128)(2,1)} %convolution_convert_fusion.dolg_ref, ...), custom_call_target="tpu_custom_call" | custom-call | flops 1342177 | bytes 10485 | tf_op jit(solution)/shard_map/glob_second/pallas_call | solution.py:855
  203.5 10.5 %weight_grads.2 = (bf16[2,1,256,512]{3,2,1,0:T(8,128)(2,1)}, bf16[2,1,256,512]{3,2,1,0:T(8,128)(2,1)}, bf16[2,1,256,512]{3,2,1,0:T(8,128)(2,1)}, bf16[2,1,256,512]{3,2,1,0:T(8,128)(2,1)}) custom-call(s32[4]{0:T(128)} %pad_add_fusion.1.idx, bf16[1024,1024]{1,0:T(8,128)(2,1)} %get-tuple-element.293.refs_0_.refs_1_.refs_2_.refs_3_, ...), custom_call_target="tpu_custom_call" | custom-call | flops 4000000 | bytes 12582 | tf_op jit(solution)/shard_map/weight_grads/pallas_call | solution.py:957
  220.6 11.1 %weight_grads.3 = (bf16[2,1,256,512]{3,2,1,0:T(8,128)(2,1)}, bf16[2,1,256,512]{3,2,1,0:T(8,128)(2,1)}, bf16[2,1,256,512]{3,2,1,0:T(8,128)(2,1)}, bf16[2,1,256,512]{3,2,1,0:T(8,128)(2,1)}) custom-call(s32[4]{0:T(128)} %pad_add_fusion.1.idx, bf16[1024,512]{1,0:T(8,128)(2,1)} %get-tuple-element.362.refs_0_.ol_ref, ...), custom_call_target="tpu_custom_call" | custom-call | flops 4000000 | bytes 12582 | tf_op jit(solution)/shard_map/weight_grads/pallas_call | solution.py:957
  231.8 3.5 regroup.4
  241.1 23.9 %input_grads.1 = (bf16[512,1024]{1,0:T(8,128)(2,1)}, bf16[512,1024]{1,0:T(8,128)(2,1)}, bf16[512,1024]{1,0:T(8,128)(2,1)}, bf16[512,1024]{1,0:T(8,128)(2,1)}, bf...) custom-call(s32[4]{0:T(128)} %pad_add_fusion.1.idx, ...), custom_call_target="tpu_custom_call" | custom-call | flops 9663676 | bytes 31457 | tf_op jit(solution)/shard_map/input_grads/pallas_call | solution.py:1037
  269.8 9.7 %collective-permute-done.38.refs_5_ = bf16[2,256,512]{2,1,0:T(8,128)(2,1)S(1)} collective-permute-done((bf16[2,256,512]{2,1,0:T(8,128)(2,1)S(1)}, bf16[2,256,512]{2,1,0:T(8,128)(2,1)S(1)}, u32[]{:S(2)}, u32[]{:S(2)}) %collective-permute-start.38) | collective-permute-done | bytes 524320 | tf_op jit(solution)/shard_map/ppermute | solution.py:65
  289.6 3.9 quarters.6
  297.2 3.4 regroup.5
  307.9 3.6 collective-permute-done.53
  316.9 10.4 %result.1 = (bf16[512,1024]{1,0:T(8,128)(2,1)}, bf16[512,1024]{1,0:T(8,128)(2,1)}) custom-call(bf16[1024,2048]{1,0:T(8,128)(2,1)} %get-tuple-element.410.act_ref, bf16[2048,1024]{1,0:T(8,128)(2,1)} %wd_ref.5, bf16[1024,512]{1,0:T(8,128)(2,1)} %get-tuple-element.362.refs_0_.ol_ref, bf16[512,1024]{1,0:T(8,128)(2,1)} %wp_ref.1), custom_call_target="tpu_custom_call" | custom-call | flops 5368709 | bytes 14680 | tf_op jit(solution)/shard_map/result/pallas_call | solution.py:1108
  335.1 4.1 quarters.7
  349.7 3.6 add_convert_fusion
  353.2 7.4 %collective-permute-done.67.refs_1_ = bf16[2,64,512]{2,1,0:T(8,128)(2,1)S(1)} collective-permute-done((bf16[2,64,512]{2,1,0:T(8,128)(2,1)S(1)}, bf16[2,64,512]{2,1,0:T(8,128)(2,1)S(1)}, u32[]{:S(2)}, u32[]{:S(2)}) %collective-permute-start.67) | collective-permute-done | bytes 131104 | tf_op jit(solution)/shard_map/ppermute | solution.py:65
  389.3 5.7 %collective-permute-done.74.refs_5_ = bf16[1,256,512]{2,1,0:T(8,128)(2,1)} collective-permute-done((bf16[1,256,512]{2,1,0:T(8,128)(2,1)}, bf16[1,256,512]{2,1,0:T(8,128)(2,1)}, u32[]{:S(2)}, u32[]{:S(2)}) %collective-permute-start.74) | collective-permute-done | bytes 262176 | tf_op jit(solution)/shard_map/ppermute | solution.py:65
  396.5 3.4 fusion.7
  419.3 4.4 collective-permute-done.80.refs_1_
  431.9 5.7 %collective-permute-done.83.refs_3_ = bf16[1,256,512]{2,1,0:T(8,128)(2,1)S(1)} collective-permute-done((bf16[1,256,512]{2,1,0:T(8,128)(2,1)}, bf16[1,256,512]{2,1,0:T(8,128)(2,1)S(1)}, u32[]{:S(2)}, u32[]{:S(2)}) %collective-permute-start.83) | collective-permute-done | bytes 262176 | tf_op jit(solution)/shard_map/ppermute | solution.py:65
  446.0 3.9 collective-permute-done.78
  450.8 7.8 %place.6 = (f32[512,4096]{1,0:T(8,128)}, f32[2048,1024]{1,0:T(8,128)}) custom-call(s32[4]{0:T(128)} %pad_add_fusion.1.idx, bf16[2,256,512]{2,1,0:T(8,128)(2,1)} %bitcast.117, bf16[2,256,512]{2,1,0:T(8,128)(2,1)} %copy-done.15, bf16[2,256,512]{2,1,0:T(8,128)(2,1)} %copy-done.17, bf16[2,256,512]{2,1,0:T(8,128)(2,1)} %copy-done.19, ...), custom_call_target="tpu_custom_call" | custom-call | bytes 14680 | tf_op jit(solution)/shard_map/place/pallas_call | solution.py:1191
  461.5 7.9 %place.7 = (f32[512,4096]{1,0:T(8,128)}, f32[2048,1024]{1,0:T(8,128)}) custom-call(s32[4]{0:T(128)} %pad_add_fusion.1.idx, bf16[2,256,512]{2,1,0:T(8,128)(2,1)} %bitcast.107, bf16[2,256,512]{2,1,0:T(8,128)(2,1)} %copy-done.8, bf16[2,256,512]{2,1,0:T(8,128)(2,1)} %copy-done.10, ...), custom_call_target="tpu_custom_call", output_to_operand_aliasing={{0}: (10, {}), {1}: (11, {})} | custom-call | bytes 14680 | tf_op jit(solution)/shard_map/place/pallas_call | solution.py:1191
  470.3 6.2 %place.4.refs_9_ = f32[512,3072]{1,0:T(8,128)} custom-call(s32[4]{0:T(128)} %pad_add_fusion.1.idx, bf16[1,256,512]{2,1,0:T(8,128)(2,1)} %bitcast.133, bf16[1,256,512]{2,1,0:T(8,128)(2,1)} %collective-permute-done.73.refs_1_, bf16[1,256,512]{2,1,0:T(8,128)(2,1)} %copy-done.32, bf16[1,256,512]{2,1,0:T(8,128)(2,1)} %copy-done.34, ...), custom_call_target="tpu_custom_call" | custom-call | bytes 14680 | tf_op jit(solution)/shard_map/place/pallas_call | solution.py:1191
  476.6 4.9 %place.5 = (f32[512,3072]{1,0:T(8,128)}, f32[512,1024]{1,0:T(8,128)}) custom-call(s32[4]{0:T(128)} %pad_add_fusion.1.idx, bf16[1,256,512]{2,1,0:T(8,128)(2,1)} %bitcast.67.refs_0_, bf16[1,256,512]{2,1,0:T(8,128)(2,1)} %copy-done.44, bf16[1,256,512]{2,1,0:T(8,128)(2,1)} %collective-permute-done.82.refs_2_, ...), custom_call_target="tpu_custom_call", output_to_operand_aliasing={{0}: (10, {})} | custom-call | bytes 14680 | tf_op jit(solution)/shard_map/place/pallas_call | solution.py:1191
  (463 shorter events, 199.4 us)
Async XLA Ops:
  10.6 24.4 %collective-permute-start.6 = (bf16[512,2048]{1,0:T(8,128)(2,1)}, bf16[512,2048]{1,0:T(8,128)(2,1)}, u32[]{:S(2)}, u32[]{:S(2)}) collective-permute-start(bf16[512,2048]{1,0:T(8,128)(2,1)} %constant_dynamic-slice_fusion.3), channel_id=1, source_target_pairs={{0,1},{1,0},{2,3},{3,2},{4,5},{5,4},{6,7},{7,6},{8,9},{9,8},{10,11... | collective-permute-start | bytes 6291464 | tf_op jit(solution)/shard_map/ppermute | solution.py:61
  23.8 30.3 %collective-permute-start.3 = (bf16[1,2,16,1024]{3,2,1,0:T(8,128)(2,1)S(1)}, bf16[1,2,16,1024]{3,2,1,0:T(8,128)(2,1)S(1)}, u32[]{:S(2)}, u32[]{:S(2)}) collective-permute-start(bf16[1,2,16,1024]{3,2,1,0:T(8,128)(2,1)S(1)} %pad_maximum_fusion.5), channel_id=1, source_target_pairs={{0,2},{2,0},{4,6},{6,4},{1,3},{3,1},{5,7},{7,5},{8,10},{10,8},{12,... | collective-permute-start | bytes 196616 | tf_op jit(solution)/shard_map/ppermute | solution.py:65
  26.9 27.8 %collective-permute-start.4 = (bf16[1,2,16,1024]{3,2,1,0:T(8,128)(2,1)S(1)}, bf16[1,2,16,1024]{3,2,1,0:T(8,128)(2,1)S(1)}, u32[]{:S(2)}, u32[]{:S(2)}) collective-permute-start(bf16[1,2,16,1024]{3,2,1,0:T(8,128)(2,1)S(1)} %pad_maximum_fusion.5), channel_id=1, source_target_pairs={{0,4},{2,6},{4,0},{6,2},{1,5},{3,7},{5,1},{7,3},{8,12},{10,14},{12... | collective-permute-start | bytes 196616 | tf_op jit(solution)/shard_map/ppermute | solution.py:65
  29.5 25.2 %collective-permute-start.5 = (bf16[1,2,16,1024]{3,2,1,0:T(8,128)(2,1)S(1)}, bf16[1,2,16,1024]{3,2,1,0:T(8,128)(2,1)S(1)}, u32[]{:S(2)}, u32[]{:S(2)}) collective-permute-start(bf16[1,2,16,1024]{3,2,1,0:T(8,128)(2,1)S(1)} %pad_maximum_fusion.5), channel_id=1, source_target_pairs={{0,6},{2,4},{4,2},{6,0},{1,7},{3,5},{5,3},{7,1},{8,14},{10,12},{12... | collective-permute-start | bytes 196616 | tf_op jit(solution)/shard_map/ppermute | solution.py:65
  29.5 29.4 %collective-permute-start.9 = (bf16[512,1024]{1,0:T(8,128)(2,1)}, bf16[512,1024]{1,0:T(8,128)(2,1)}, u32[]{:S(2)}, u32[]{:S(2)}) collective-permute-start(bf16[512,1024]{1,0:T(8,128)(2,1)} %bitcast.x_ref), channel_id=1, source_target_pairs={{0,2},{2,4},{4,6},{1,3},{3,5},{5,7},{8,10},{10,12},{12,14},{9,11},... | collective-permute-start | bytes 3145736 | tf_op jit(solution)/shard_map/ppermute | solution.py:70
  54.1 35.3 %collective-permute-start.12 = (bf16[512,1536]{1,0:T(8,128)(2,1)}, bf16[512,1536]{1,0:T(8,128)(2,1)S(1)}, u32[]{:S(2)}, u32[]{:S(2)}) collective-permute-start(bf16[512,1536]{1,0:T(8,128)(2,1)} %pad_maximum_fusion), channel_id=1, source_target_pairs={{0,1},{1,0},{2,3},{3,2},{4,5},{5,4},{6,7},{7,6},{8,9},{9,8},{10,11... | collective-permute-start | bytes 4718600 | tf_op jit(solution)/shard_map/ppermute | solution.py:61
  54.7 25.4 %collective-permute-start.7 = (bf16[2,2,256,512]{3,2,1,0:T(8,128)(2,1)}, bf16[2,2,256,512]{3,2,1,0:T(8,128)(2,1)S(1)}, u32[]{:S(2)}, u32[]{:S(2)}) collective-permute-start(bf16[2,2,256,512]{3,2,1,0:T(8,128)(2,1)} %get-tuple-element.279), channel_id=1, source_target_pairs={{0,8},{8,0},{16,24},{24,16},{1,9},{9,1},{17,25},{25,17},{2,10},{10... | collective-permute-start | bytes 3145736 | tf_op jit(solution)/shard_map/ppermute | solution.py:65
  56.2 25.4 %collective-permute-start.8 = (bf16[2,2,256,512]{3,2,1,0:T(8,128)(2,1)}, bf16[2,2,256,512]{3,2,1,0:T(8,128)(2,1)}, u32[]{:S(2)}, u32[]{:S(2)}) collective-permute-start(bf16[2,2,256,512]{3,2,1,0:T(8,128)(2,1)} %get-tuple-element.280), channel_id=1, source_target_pairs={{0,16},{8,24},{16,0},{24,8},{1,17},{9,25},{17,1},{25,9},{2,18},{10... | collective-permute-start | bytes 3145736 | tf_op jit(solution)/shard_map/ppermute | solution.py:65
  58.8 30.6 %collective-permute-start.10 = (bf16[512,1024]{1,0:T(8,128)(2,1)}, bf16[512,1024]{1,0:T(8,128)(2,1)}, u32[]{:S(2)}, u32[]{:S(2)}) collective-permute-start(bf16[512,1024]{1,0:T(8,128)(2,1)} %collective-permute-done.9.prev_ref.refs_1_), channel_id=1, source_target_pairs={{0,1},{1,0},{2,3},{3,2},{4,5},{5,4},{6,7},{7,6},{8,9},{9,8},{10,11... | collective-permute-start | bytes 3145736 | tf_op jit(solution)/shard_map/ppermute | solution.py:61
  78.5 58.3 %collective-permute-start.18 = (bf16[2,2,256,512]{3,2,1,0:T(8,128)(2,1)}, bf16[2,2,256,512]{3,2,1,0:T(8,128)(2,1)}, u32[]{:S(2)}, u32[]{:S(2)}) collective-permute-start(bf16[2,2,256,512]{3,2,1,0:T(8,128)(2,1)} %get-tuple-element.312), channel_id=1, source_target_pairs={{0,8},{8,0},{16,24},{24,16},{1,9},{9,1},{17,25},{25,17},{2,10},{10... | collective-permute-start | bytes 3145736 | tf_op jit(solution)/shard_map/ppermute | solution.py:65
  80.1 56.7 %collective-permute-start.19 = (bf16[2,2,256,512]{3,2,1,0:T(8,128)(2,1)}, bf16[2,2,256,512]{3,2,1,0:T(8,128)(2,1)}, u32[]{:S(2)}, u32[]{:S(2)}) collective-permute-start(bf16[2,2,256,512]{3,2,1,0:T(8,128)(2,1)} %get-tuple-element.313), channel_id=1, source_target_pairs={{0,16},{8,24},{16,0},{24,8},{1,17},{9,25},{17,1},{25,9},{2,18},{10... | collective-permute-start | bytes 3145736 | tf_op jit(solution)/shard_map/ppermute | solution.py:65
  84.0 37.8 %collective-permute-start.15 = (bf16[2,256,512]{2,1,0:T(8,128)(2,1)}, bf16[2,256,512]{2,1,0:T(8,128)(2,1)}, u32[]{:S(2)}, u32[]{:S(2)}) collective-permute-start(bf16[2,256,512]{2,1,0:T(8,128)(2,1)} %get-tuple-element.286), channel_id=1, source_target_pairs={{0,16},{8,24},{16,0},{24,8},{1,17},{9,25},{17,1},{25,9},{2,18},{10... | collective-permute-start | bytes 1572872 | tf_op jit(solution)/shard_map/ppermute | solution.py:65
  139.2 44.4 %collective-permute-start.20 = (bf16[2,256,512]{2,1,0:T(8,128)(2,1)}, bf16[2,256,512]{2,1,0:T(8,128)(2,1)S(1)}, u32[]{:S(2)}, u32[]{:S(2)}) collective-permute-start(bf16[2,256,512]{2,1,0:T(8,128)(2,1)} %get-tuple-element.318), channel_id=1, source_target_pairs={{0,16},{8,24},{16,0},{24,8},{1,17},{9,25},{17,1},{25,9},{2,18},{10... | collective-permute-start | bytes 1572872 | tf_op jit(solution)/shard_map/ppermute | solution.py:65
  140.0 46.1 %collective-permute-start.21 = (bf16[2,256,512]{2,1,0:T(8,128)(2,1)}, bf16[2,256,512]{2,1,0:T(8,128)(2,1)S(1)}, u32[]{:S(2)}, u32[]{:S(2)}) collective-permute-start(bf16[2,256,512]{2,1,0:T(8,128)(2,1)} %get-tuple-element.319), channel_id=1, source_target_pairs={{0,8},{8,0},{16,24},{24,16},{1,9},{9,1},{17,25},{25,17},{2,10},{10... | collective-permute-start | bytes 1572872 | tf_op jit(solution)/shard_map/ppermute | solution.py:65
  141.5 39.6 %collective-permute-start.23 = (bf16[2,128,512]{2,1,0:T(8,128)(2,1)S(1)}, bf16[2,128,512]{2,1,0:T(8,128)(2,1)S(1)}, u32[]{:S(2)}, u32[]{:S(2)}) collective-permute-start(bf16[2,128,512]{2,1,0:T(8,128)(2,1)S(1)} %copy-done.80), channel_id=1, source_target_pairs={{0,4},{2,6},{4,0},{6,2},{1,5},{3,7},{5,1},{7,3},{8,12},{10,14},{12... | collective-permute-start | bytes 786440 | tf_op jit(solution)/shard_map/ppermute | solution.py:65
  144.0 37.1 %collective-permute-start.24 = (bf16[2,128,512]{2,1,0:T(8,128)(2,1)S(1)}, bf16[2,128,512]{2,1,0:T(8,128)(2,1)S(1)}, u32[]{:S(2)}, u32[]{:S(2)}) collective-permute-start(bf16[2,128,512]{2,1,0:T(8,128)(2,1)S(1)} %copy-done.79), channel_id=1, source_target_pairs={{0,6},{2,4},{4,2},{6,0},{1,7},{3,5},{5,3},{7,1},{8,14},{10,12},{12... | collective-permute-start | bytes 786440 | tf_op jit(solution)/shard_map/ppermute | solution.py:65
  144.4 47.2 %collective-permute-start.17 = (f32[8,72,128]{2,1,0:T(8,128)S(1)}, f32[8,72,128]{2,1,0:T(8,128)S(1)}, u32[]{:S(2)}, u32[]{:S(2)}) collective-permute-start(f32[8,72,128]{2,1,0:T(8,128)S(1)} %pad_maximum_fusion.1), channel_id=1, source_target_pairs={{0,4},{2,6},{4,0},{6,2},{1,5},{3,7},{5,1},{7,3},{8,12},{10,14},{12... | collective-permute-start | bytes 884744 | tf_op jit(solution)/shard_map/ppermute | solution.py:65
  181.3 34.7 %collective-permute-start.30 = (bf16[2,128,512]{2,1,0:T(8,128)(2,1)S(1)}, bf16[2,128,512]{2,1,0:T(8,128)(2,1)S(1)}, u32[]{:S(2)}, u32[]{:S(2)}) collective-permute-start(bf16[2,128,512]{2,1,0:T(8,128)(2,1)S(1)} %add_convert_fusion.3.refs_0_), channel_id=1, source_target_pairs={{0,2},{2,0},{4,6},{6,4},{1,3},{3,1},{5,7},{7,5},{8,10},{10,8},{12,... | collective-permute-start | bytes 786440 | tf_op jit(solution)/shard_map/ppermute | solution.py:65
  183.6 33.3 %collective-permute-start.31 = (bf16[2,128,512]{2,1,0:T(8,128)(2,1)S(1)}, bf16[2,128,512]{2,1,0:T(8,128)(2,1)S(1)}, u32[]{:S(2)}, u32[]{:S(2)}) collective-permute-start(bf16[2,128,512]{2,1,0:T(8,128)(2,1)S(1)} %add_convert_fusion.3.refs_0_), channel_id=1, source_target_pairs={{0,4},{2,6},{4,0},{6,2},{1,5},{3,7},{5,1},{7,3},{8,12},{10,14},{12... | collective-permute-start | bytes 786440 | tf_op jit(solution)/shard_map/ppermute | solution.py:65
  183.7 34.3 %collective-permute-start.32 = (bf16[2,128,512]{2,1,0:T(8,128)(2,1)S(1)}, bf16[2,128,512]{2,1,0:T(8,128)(2,1)S(1)}, u32[]{:S(2)}, u32[]{:S(2)}) collective-permute-start(bf16[2,128,512]{2,1,0:T(8,128)(2,1)S(1)} %add_convert_fusion.3.refs_0_), channel_id=1, source_target_pairs={{0,6},{2,4},{4,2},{6,0},{1,7},{3,5},{5,3},{7,1},{8,14},{10,12},{12... | collective-permute-start | bytes 786440 | tf_op jit(solution)/shard_map/ppermute | solution.py:65
  235.3 31.4 %collective-permute-start.39 = (bf16[2,1,256,512]{3,2,1,0:T(8,128)(2,1)}, bf16[2,1,256,512]{3,2,1,0:T(8,128)(2,1)S(1)}, u32[]{:S(2)}, u32[]{:S(2)}) collective-permute-start(bf16[2,1,256,512]{3,2,1,0:T(8,128)(2,1)} %get-tuple-element.365), channel_id=1, source_target_pairs={{0,8},{8,0},{16,24},{24,16},{1,9},{9,1},{17,25},{25,17},{2,10},{10... | collective-permute-start | bytes 1572872 | tf_op jit(solution)/shard_map/ppermute | solution.py:65
  235.9 31.4 %collective-permute-start.40 = (bf16[2,1,256,512]{3,2,1,0:T(8,128)(2,1)}, bf16[2,1,256,512]{3,2,1,0:T(8,128)(2,1)S(1)}, u32[]{:S(2)}, u32[]{:S(2)}) collective-permute-start(bf16[2,1,256,512]{3,2,1,0:T(8,128)(2,1)} %get-tuple-element.387), channel_id=1, source_target_pairs={{0,16},{8,24},{16,0},{24,8},{1,17},{9,25},{17,1},{25,9},{2,18},{10... | collective-permute-start | bytes 1572872 | tf_op jit(solution)/shard_map/ppermute | solution.py:65
  237.3 31.1 %collective-permute-start.37 = (bf16[2,256,512]{2,1,0:T(8,128)(2,1)}, bf16[2,256,512]{2,1,0:T(8,128)(2,1)S(1)}, u32[]{:S(2)}, u32[]{:S(2)}) collective-permute-start(bf16[2,256,512]{2,1,0:T(8,128)(2,1)} %bitcast.115), channel_id=1, source_target_pairs={{0,16},{8,24},{16,0},{24,8},{1,17},{9,25},{17,1},{25,9},{2,18},{10... | collective-permute-start | bytes 1572872 | tf_op jit(solution)/shard_map/ppermute | solution.py:65
  265.0 36.7 %collective-permute-start.33 = (bf16[512,1024]{1,0:T(8,128)(2,1)}, bf16[512,1024]{1,0:T(8,128)(2,1)}, u32[]{:S(2)}, u32[]{:S(2)}) collective-permute-start(bf16[512,1024]{1,0:T(8,128)(2,1)} %get-tuple-element.383), channel_id=1, source_target_pairs={{0,1},{1,0},{2,3},{3,2},{4,5},{5,4},{6,7},{7,6},{8,9},{9,8},{10,11... | collective-permute-start | bytes 3145736 | tf_op jit(solution)/shard_map/ppermute | solution.py:61
  327.4 40.5 %collective-permute-start.55 = (bf16[512,1024]{1,0:T(8,128)(2,1)}, bf16[512,1024]{1,0:T(8,128)(2,1)}, u32[]{:S(2)}, u32[]{:S(2)}) collective-permute-start(bf16[512,1024]{1,0:T(8,128)(2,1)} %get-tuple-element.443), channel_id=1, source_target_pairs={{0,1},{1,0},{2,3},{3,2},{4,5},{5,4},{6,7},{7,6},{8,9},{9,8},{10,11... | collective-permute-start | bytes 3145736 | tf_op jit(solution)/shard_map/ppermute | solution.py:61
  327.9 40.1 %collective-permute-start.56 = (bf16[512,1024]{1,0:T(8,128)(2,1)}, bf16[512,1024]{1,0:T(8,128)(2,1)}, u32[]{:S(2)}, u32[]{:S(2)}) collective-permute-start(bf16[512,1024]{1,0:T(8,128)(2,1)} %add_convert_fusion.1), channel_id=1, source_target_pairs={{2,0},{4,2},{6,4},{3,1},{5,3},{7,5},{10,8},{12,10},{14,12},{11,9},... | collective-permute-start | bytes 3145736 | tf_op jit(solution)/shard_map/ppermute | solution.py:70
  360.6 25.7 %collective-permute-start.60 = (bf16[2,256,512]{2,1,0:T(8,128)(2,1)S(1)}, bf16[2,256,512]{2,1,0:T(8,128)(2,1)S(1)}, u32[]{:S(2)}, u32[]{:S(2)}) collective-permute-start(bf16[2,256,512]{2,1,0:T(8,128)(2,1)S(1)} %bitcast.109), channel_id=1, source_target_pairs={{0,8},{8,0},{16,24},{24,16},{1,9},{9,1},{17,25},{25,17},{2,10},{10... | collective-permute-start | bytes 1572872 | tf_op jit(solution)/shard_map/ppermute | solution.py:65
  386.3 24.8 %collective-permute-start.63 = (bf16[2,256,512]{2,1,0:T(8,128)(2,1)S(1)}, bf16[2,256,512]{2,1,0:T(8,128)(2,1)S(1)}, u32[]{:S(2)}, u32[]{:S(2)}) collective-permute-start(bf16[2,256,512]{2,1,0:T(8,128)(2,1)S(1)} %collective-permute-done.45.refs_5_), channel_id=1, source_target_pairs={{0,16},{8,24},{16,0},{24,8},{1,17},{9,25},{17,1},{25,9},{2,18},{10... | collective-permute-start | bytes 1572872 | tf_op jit(solution)/shard_map/ppermute | solution.py:65
  411.1 39.7 %collective-permute-start.93 = (bf16[8,128,512]{2,1,0:T(8,128)(2,1)}, bf16[8,128,512]{2,1,0:T(8,128)(2,1)}, u32[]{:S(2)}, u32[]{:S(2)}) collective-permute-start(bf16[8,128,512]{2,1,0:T(8,128)(2,1)} %swap.4), channel_id=1, source_target_pairs={{0,1},{1,0},{2,3},{3,2},{4,5},{5,4},{6,7},{7,6},{8,9},{9,8},{10,11... | collective-permute-start | bytes 3145736 | tf_op jit(solution)/shard_map/ppermute | solution.py:61
  428.6 31.9 %collective-permute-start.92 = (bf16[8,128,512]{2,1,0:T(8,128)(2,1)S(1)}, bf16[8,128,512]{2,1,0:T(8,128)(2,1)S(1)}, u32[]{:S(2)}, u32[]{:S(2)}) collective-permute-start(bf16[8,128,512]{2,1,0:T(8,128)(2,1)S(1)} %copy-done.26), channel_id=1, source_target_pairs={{0,1},{1,0},{2,3},{3,2},{4,5},{5,4},{6,7},{7,6},{8,9},{9,8},{10,11... | collective-permute-start | bytes 3145736 | tf_op jit(solution)/shard_map/ppermute | solution.py:61
  428.6 40.7 %collective-permute-start.91 = (bf16[8,128,512]{2,1,0:T(8,128)(2,1)}, bf16[8,128,512]{2,1,0:T(8,128)(2,1)S(1)}, u32[]{:S(2)}, u32[]{:S(2)}) collective-permute-start(bf16[8,128,512]{2,1,0:T(8,128)(2,1)} %swap.7), channel_id=1, source_target_pairs={{0,1},{1,0},{2,3},{3,2},{4,5},{5,4},{6,7},{7,6},{8,9},{9,8},{10,11... | collective-permute-start | bytes 3145736 | tf_op jit(solution)/shard_map/ppermute | solution.py:61
  442.0 34.6 %collective-permute-start.86 = (bf16[4,128,512]{2,1,0:T(8,128)(2,1)}, bf16[4,128,512]{2,1,0:T(8,128)(2,1)}, u32[]{:S(2)}, u32[]{:S(2)}) collective-permute-start(bf16[4,128,512]{2,1,0:T(8,128)(2,1)} %swap.6), channel_id=1, source_target_pairs={{0,1},{1,0},{2,3},{3,2},{4,5},{5,4},{6,7},{7,6},{8,9},{9,8},{10,11... | collective-permute-start | bytes 1572872 | tf_op jit(solution)/shard_map/ppermute | solution.py:61
  (146 other events, 1830.9 us)
